TPU v7x, 32 devices: a whole 2x2x4 slice. The times are simulated.
32 devices in a mesh: dp: 16 (over z, y, x), head: 2 (over core).
Axes of the slice: x: 2, y: 2, z: 4, core: 2. Of those that a mesh axis runs over, the one named last changes fastest.
Arguments:
- tokens: bfloat16 [98304, 384], P(('dp', 'head')), may hold values from -6 to 6
- grad_out: bfloat16 [98304, 384], P(('dp', 'head')), may hold values from -6 to 6
- segments: int32 [96, 1024], P('dp'), may hold values from 0 to 7, as said below
- counts: int32 [96], P('dp'), may hold values from 1 to 6
- attn_w: float32 [4, 384, 384], P(None, 'dp', 'head')
- attn_m: float32 [4, 384, 384], P(None, 'dp', 'head')
- attn_v: float32 [4, 384, 384], P(None, 'dp', 'head')
- mlp_w: float32 [2, 384, 1536], P(None, 'dp', 'head')
- mlp_m: float32 [2, 384, 1536], P(None, 'dp', 'head')
- mlp_v: float32 [2, 384, 1536], P(None, 'dp', 'head')
- conv_w: float32 [9, 1536], P(None, 'head')
- conv_m: float32 [9, 1536], P(None, 'head')
- conv_v: float32 [9, 1536], P(None, 'head')
- norm_w: float32 [4, 384], replicated
- norm_m: float32 [4, 384], replicated
- norm_v: float32 [4, 384], replicated
Outputs:
- output: bfloat16 [98304, 384], P(('dp', 'head'))
- grad_tokens: float32 [98304, 384], P(('dp', 'head'))
- new_attn_w: float32 [4, 384, 384], P(None, 'dp', 'head')
- new_attn_m: float32 [4, 384, 384], P(None, 'dp', 'head')
- new_attn_v: float32 [4, 384, 384], P(None, 'dp', 'head')
- new_mlp_w: float32 [2, 384, 1536], P(None, 'dp', 'head')
- new_mlp_m: float32 [2, 384, 1536], P(None, 'dp', 'head')
- new_mlp_v: float32 [2, 384, 1536], P(None, 'dp', 'head')
- new_conv_w: float32 [9, 1536], P(None, 'head')
- new_conv_m: float32 [9, 1536], P(None, 'head')
- new_conv_v: float32 [9, 1536], P(None, 'head')
- new_norm_w: float32 [4, 384], replicated
- new_norm_m: float32 [4, 384], replicated
- new_norm_v: float32 [4, 384], replicated
Inputs may be any that keep to these rules, and one draw needn't show every extreme that they name: `segments`: within each packed row of 1024 tokens the ids start at 0 and grow by one at the first token of each image; an image is a run of whole grid rows of 16 tokens, and every row holds exactly 8 images.
All inputs are finite; a program needn't handle non-finite values.
Results may differ from a plain program's by a relative error of at most 0.012.
Values may be sent and summed in bfloat16 or wider, within the bound.
No kernel may reach another device: no remote copies, remote signals or barrier semaphores. Data moves between devices by JAX's collectives and lax.ppermute only.
A program may use at most 640 MiB of HBM per device.

v0:
```python
import jax
import jax.numpy as jnp
from jax import lax
from jax.sharding import PartitionSpec as P

HEAD_DIM = 64
GRID_W = 16
STEP = 10


NORM_EPS = 1e-06
NEG_LARGE = -1e30
BETA_ONE = 0.9
BETA_TWO = 0.999
ADAM_EPS = 1e-06
DECAY = 0.01
RATE = 0.5


def norm_forward(values, gain_row, bias_row):
    average = jnp.mean(values, axis=-1, keepdims=True)
    centered = values - average
    inverse = lax.rsqrt(jnp.mean(centered * centered, axis=-1, keepdims=True) + NORM_EPS)
    unit_rows = centered * inverse
    return (unit_rows * gain_row + bias_row, unit_rows, inverse)


def norm_backward(upstream, gain_row, unit_rows, inverse):
    grad_unit = upstream * gain_row
    first_term = jnp.mean(grad_unit, axis=-1, keepdims=True)
    second_term = jnp.mean(grad_unit * unit_rows, axis=-1, keepdims=True)
    grad_in = inverse * (grad_unit - first_term - unit_rows * second_term)
    return (grad_in, jnp.sum(upstream * unit_rows, axis=0), jnp.sum(upstream, axis=0))


def shifted(values, offset):
    if offset == 0:
        return values
    padding = jnp.zeros_like(values[:, : abs(offset)])
    if offset > 0:
        return jnp.concatenate([values[:, offset:], padding], axis=1)
    return jnp.concatenate([padding, values[:, :offset]], axis=1)


def build_masks(segments):
    length = segments.shape[1]
    column = jnp.arange(length, dtype=jnp.int32) % GRID_W
    tagged = segments + 1
    tap_mask = []
    for row_step in (-1, 0, 1):
        for col_step in (-1, 0, 1):
            offset = row_step * GRID_W + col_step
            inside = (column + col_step >= 0) & (column + col_step < GRID_W)
            same_image = shifted(tagged, offset) == tagged
            tap_mask.append((same_image & inside[None, :]).astype(jnp.float32))
    return jnp.stack(tap_mask)


def depthwise(hidden, tap_weights, tap_mask):
    summed = hidden
    tap_index = 0
    for row_step in (-1, 0, 1):
        for col_step in (-1, 0, 1):
            offset = row_step * GRID_W + col_step
            summed = summed + tap_weights[tap_index] * tap_mask[tap_index][:, :, None] * shifted(
                hidden, offset
            )
            tap_index += 1
    return summed


def row_scores(queries, key_rows, segment_row):
    scores = jnp.einsum(
        "qhe,khe->hqk", queries, key_rows, preferred_element_type=jnp.float32
    ) * HEAD_DIM ** (-0.5)
    same_image = segment_row[:, None] == segment_row[None, :]
    return jnp.where(same_image[None], scores, NEG_LARGE)


def attend_forward(row_item):
    queries, key_rows, value_rows, segment_row, active_row = row_item
    scores = row_scores(queries, key_rows, segment_row)
    row_max = jnp.max(scores, axis=-1, keepdims=True)
    exponent = jnp.exp(scores - row_max)
    row_total = jnp.sum(exponent, axis=-1, keepdims=True)
    probability = (exponent / row_total).astype(jnp.bfloat16)
    context = jnp.einsum(
        "hqk,khe->qhe", probability, value_rows, preferred_element_type=jnp.float32
    )
    context = (context * active_row[None, :, None]).astype(jnp.bfloat16)
    return (context, row_max + jnp.log(row_total))


def attend_backward(row_item):
    queries, key_rows, value_rows, segment_row, lse_row, grad_context = row_item
    scores = row_scores(queries, key_rows, segment_row)
    probability = jnp.exp(scores - lse_row)
    grad_probs = jnp.einsum(
        "qhe,khe->hqk", grad_context, value_rows, preferred_element_type=jnp.float32
    )
    grad_values = jnp.einsum(
        "hqk,qhe->khe",
        probability.astype(jnp.bfloat16),
        grad_context,
        preferred_element_type=jnp.float32,
    )
    inner_sum = jnp.sum(probability * grad_probs, axis=-1, keepdims=True)
    grad_scores = (probability * (grad_probs - inner_sum)).astype(jnp.bfloat16)
    score_scale = HEAD_DIM ** (-0.5)
    grad_queries = (
        jnp.einsum("hqk,khe->qhe", grad_scores, key_rows, preferred_element_type=jnp.float32)
        * score_scale
    )
    grad_keys = (
        jnp.einsum("hqk,qhe->khe", grad_scores, queries, preferred_element_type=jnp.float32)
        * score_scale
    )
    return jnp.stack([grad_queries, grad_keys, grad_values], axis=1).astype(jnp.bfloat16)


def adam_terms(grad_sum, first_old, second):
    first_new = BETA_ONE * first_old + (1.0 - BETA_ONE) * grad_sum
    second_new = BETA_TWO * second + (1.0 - BETA_TWO) * grad_sum * grad_sum
    direction = (
        first_new
        / (1.0 - BETA_ONE**STEP)
        / (jnp.sqrt(second_new / (1.0 - BETA_TWO**STEP)) + ADAM_EPS)
    )
    return (first_new, second_new, direction)


def body(
    tokens,
    grad_out,
    segments,
    counts,
    attn_w,
    attn_m,
    attn_v,
    mlp_w,
    mlp_m,
    mlp_v,
    conv_w,
    conv_m,
    conv_v,
    norm_w,
    norm_m,
    norm_v,
):
    head_rank = lax.axis_index("head")
    attn_full, mlp_full = (
        lax.all_gather(attn_w.astype(jnp.bfloat16), "dp", axis=1, tiled=True),
        lax.all_gather(mlp_w.astype(jnp.bfloat16), "dp", axis=1, tiled=True),
    )
    conv_low = conv_w.astype(jnp.bfloat16)
    row_total = segments.shape[0]
    head_first = head_rank * (attn_w.shape[2] // HEAD_DIM)
    conv_taps = conv_low.astype(jnp.float32)
    heads_work = attn_full.shape[2] // HEAD_DIM
    length = segments.shape[1]
    tap_mask = build_masks(segments)
    active = (
        (head_first + jnp.arange(heads_work, dtype=jnp.int32))[None, :] < counts[:, None]
    ).astype(jnp.float32)
    residual = tokens.astype(jnp.float32)
    normed_one, unit_one, inverse_one = norm_forward(residual, norm_w[0], norm_w[1])
    normed_low = normed_one.astype(jnp.bfloat16)
    inputs_one = lax.all_gather(normed_low, "head", axis=0, tiled=True)
    projected = jnp.einsum(
        "td,kde->tke", inputs_one, attn_full[:3], preferred_element_type=jnp.float32
    ).astype(jnp.bfloat16)
    shaped = projected.reshape(row_total, length, 3, heads_work, HEAD_DIM)
    queries = shaped[:, :, 0]
    key_rows = shaped[:, :, 1]
    value_rows = shaped[:, :, 2]
    context, lse_rows = lax.map(attend_forward, (queries, key_rows, value_rows, segments, active))
    context = context.reshape(row_total * length, heads_work * HEAD_DIM)
    piece = context
    attn_out = lax.psum_scatter(
        jnp.einsum("tj,dj->td", piece, attn_full[3], preferred_element_type=jnp.float32),
        "head",
        scatter_dimension=0,
        tiled=True,
    )
    middle = residual + attn_out
    normed_two, unit_two, inverse_two = norm_forward(middle, norm_w[2], norm_w[3])
    normed_two_low = normed_two.astype(jnp.bfloat16)
    inputs_two = lax.all_gather(normed_two_low, "head", axis=0, tiled=True)
    hidden = jnp.dot(inputs_two, mlp_full[0], preferred_element_type=jnp.float32).reshape(
        row_total, length, -1
    )
    mixed_rows = depthwise(hidden, conv_taps, tap_mask)
    activated = jax.nn.gelu(mixed_rows).reshape(row_total * length, -1).astype(jnp.bfloat16)
    piece = activated
    mlp_out = lax.psum_scatter(
        jnp.einsum("tf,df->td", piece, mlp_full[1], preferred_element_type=jnp.float32),
        "head",
        scatter_dimension=0,
        tiled=True,
    )
    output = (middle + mlp_out).astype(jnp.bfloat16)
    grad_top = grad_out.astype(jnp.float32)
    grad_rows_all = lax.all_gather(grad_out, "head", axis=0, tiled=True)
    grad_act = jnp.einsum(
        "td,df->tf", grad_rows_all, mlp_full[1], preferred_element_type=jnp.float32
    )
    grad_fc2 = jnp.einsum("td,tf->df", grad_rows_all, activated, preferred_element_type=jnp.float32)
    gelu_value, gelu_back = jax.vjp(jax.nn.gelu, mixed_rows)
    grad_mixed = gelu_back(grad_act.reshape(mixed_rows.shape))[0]
    conv_value, conv_back = jax.vjp(
        lambda hidden_in, tap_weights: depthwise(hidden_in, tap_weights, tap_mask),
        hidden,
        conv_taps,
    )
    grad_hidden, grad_conv = conv_back(grad_mixed)
    grad_hidden_low = grad_hidden.reshape(row_total * length, -1).astype(jnp.bfloat16)
    grad_fc1 = jnp.einsum(
        "td,tf->df", inputs_two, grad_hidden_low, preferred_element_type=jnp.float32
    )
    piece = grad_hidden_low
    grad_norm_two = lax.psum_scatter(
        jnp.einsum("tf,df->td", piece, mlp_full[0], preferred_element_type=jnp.float32),
        "head",
        scatter_dimension=0,
        tiled=True,
    )
    grad_mid_in, gain_two_grad, bias_two_grad = norm_backward(
        grad_norm_two, norm_w[2], unit_two, inverse_two
    )
    grad_middle = grad_top + grad_mid_in
    grad_middle_low = grad_middle.astype(jnp.bfloat16)
    grad_mid_rows = lax.all_gather(grad_middle_low, "head", axis=0, tiled=True)
    grad_context = jnp.einsum(
        "td,dj->tj", grad_mid_rows, attn_full[3], preferred_element_type=jnp.float32
    ).astype(jnp.bfloat16)
    grad_context = grad_context.reshape(row_total, length, heads_work, HEAD_DIM)
    grad_context = (grad_context.astype(jnp.float32) * active[:, None, :, None]).astype(
        jnp.bfloat16
    )
    grad_out_proj = jnp.einsum(
        "td,tj->dj", grad_mid_rows, context, preferred_element_type=jnp.float32
    )
    grad_projected = lax.map(
        attend_backward, (queries, key_rows, value_rows, segments, lse_rows, grad_context)
    )
    grad_projected = grad_projected.reshape(row_total * length, 3, heads_work * HEAD_DIM)
    grad_qkv = jnp.einsum(
        "td,tke->kde", inputs_one, grad_projected, preferred_element_type=jnp.float32
    )
    piece = grad_projected
    grad_norm_one = lax.psum_scatter(
        jnp.einsum("tke,kde->td", piece, attn_full[:3], preferred_element_type=jnp.float32),
        "head",
        scatter_dimension=0,
        tiled=True,
    )
    grad_in_one, gain_one_grad, bias_one_grad = norm_backward(
        grad_norm_one, norm_w[0], unit_one, inverse_one
    )
    grad_tokens = grad_middle + grad_in_one
    grad_attn = jnp.concatenate([grad_qkv, grad_out_proj[None]], axis=0)
    grad_mlp = jnp.stack([grad_fc1, grad_fc2])
    grad_attn, grad_mlp = (
        lax.psum_scatter(grad_attn, "dp", scatter_dimension=1, tiled=True),
        lax.psum_scatter(grad_mlp, "dp", scatter_dimension=1, tiled=True),
    )
    grad_conv = lax.psum(grad_conv, "dp")
    norm_part = jnp.stack([gain_one_grad, bias_one_grad, gain_two_grad, bias_two_grad])
    new_attn_m, new_attn_v, attn_direction = adam_terms(grad_attn, attn_m, attn_v)
    new_mlp_m, new_mlp_v, mlp_direction = adam_terms(grad_mlp, mlp_m, mlp_v)
    new_conv_m, new_conv_v, conv_direction = adam_terms(grad_conv, conv_m, conv_v)
    attn_update = attn_direction + DECAY * attn_w
    mlp_update = mlp_direction + DECAY * mlp_w
    conv_update = conv_direction + DECAY * conv_w
    first_line = (lax.axis_index("dp") == 0).astype(jnp.float32)
    weight_squares = jnp.concatenate(
        [
            jnp.sum(attn_w * attn_w, axis=(1, 2)),
            jnp.sum(mlp_w * mlp_w, axis=(1, 2)),
            (first_line * jnp.sum(conv_w * conv_w))[None],
        ]
    )
    update_squares = jnp.concatenate(
        [
            jnp.sum(attn_update * attn_update, axis=(1, 2)),
            jnp.sum(mlp_update * mlp_update, axis=(1, 2)),
            (first_line * jnp.sum(conv_update * conv_update))[None],
        ]
    )
    squares, norm_grads = lax.psum(
        (jnp.stack([weight_squares, update_squares]), norm_part), ("dp", "head")
    )
    ratio = jnp.sqrt(squares[0]) / jnp.sqrt(squares[1])
    new_attn_w = attn_w - RATE * ratio[:4, None, None] * attn_update
    new_mlp_w = mlp_w - RATE * ratio[4:6, None, None] * mlp_update
    new_conv_w = conv_w - RATE * ratio[6] * conv_update
    new_norm_m, new_norm_v, norm_direction = adam_terms(norm_grads, norm_m, norm_v)
    new_norm_w = norm_w - RATE * norm_direction
    return (
        output,
        grad_tokens,
        new_attn_w,
        new_attn_m,
        new_attn_v,
        new_mlp_w,
        new_mlp_m,
        new_mlp_v,
        new_conv_w,
        new_conv_m,
        new_conv_v,
        new_norm_w,
        new_norm_m,
        new_norm_v,
    )


def solution(mesh):
    in_specs = (
        P(("dp", "head"), None),
        P(("dp", "head"), None),
        P("dp", None),
        P("dp"),
        P(None, "dp", "head"),
        P(None, "dp", "head"),
        P(None, "dp", "head"),
        P(None, "dp", "head"),
        P(None, "dp", "head"),
        P(None, "dp", "head"),
        P(None, "head"),
        P(None, "head"),
        P(None, "head"),
        P(),
        P(),
        P(),
    )
    out_specs = (
        P(("dp", "head"), None),
        P(("dp", "head"), None),
        P(None, "dp", "head"),
        P(None, "dp", "head"),
        P(None, "dp", "head"),
        P(None, "dp", "head"),
        P(None, "dp", "head"),
        P(None, "dp", "head"),
        P(None, "head"),
        P(None, "head"),
        P(None, "head"),
        P(),
        P(),
        P(),
    )
    return jax.shard_map(body, mesh=mesh, in_specs=in_specs, out_specs=out_specs, check_vma=False)
```

profile of v0, /device:TPU:0, one launch (start us, length us, event | category | flops | bytes accessed | tf_op | source)
XLA Modules:
  0.0 1188.9 jit_solution(358238312445196892)
XLA Ops:
  20.2 47.2 %all_gather.19 = bf16[4,384,192]{2,0,1:T(4,128)(2,1)S(1)} all-gather(bf16[4,24,192]{2,0,1:T(4,128)(2,1)S(1)} %copy.154), channel_id=1, replica_groups=mesh['dp'=16,'head'=2] {'dp'}, dimensions={1}, use_global_device_ids=true | all-gather | bytes 626688 | tf_op jit(solution)/shard_map/all_gather | solution.py:152
  70.0 9.5 fusion.158
  79.4 8.9 convert_element_type.123
  88.3 15.4 %reshape.352 = bf16[6,1024,3,3,64]{1,0,4,3,2:T(8,128)(2,1)} reshape(bf16[6144,3,192]{0,2,1:T(8,128)(2,1)} %convert_element_type.123) | data formatting | bytes 14155776 | tf_op jit(solution)/shard_map/reshape | solution.py:172
  116.1 94.6 %while.22 = (s32[]{:T(128)}, bf16[6,1024,3,64]{1,3,2,0:T(8,128)(2,1)}, f32[6,3,1024,1]{2,1,3,0:T(4,128)}, bf16[6,1024,3,64]{1,3,2,0:T(8,128)(2,1)}, s32[6,1024]{...) while((s32[]{:T(128)}, ...), condition=%wide.region_5.6_spmd, body=%wide.region_2.5_spmd.sunk | while | flops 844493824 | bytes 47827120 | solution.py:176
  223.1 13.1 %reduce-scatter.6.cloned.1.call-done = f32[3072,384]{1,0:T(8,128)} async-done(((f32[6144,384]{1,0:T(8,128)}), f32[3072,384]{1,0:T(8,128)}) %reduce-scatter.6.cloned.1.call-update) | async-done | bytes 4718608 | tf_op jit(solution)/shard_map/reduce_scatter | solution.py:179
  245.6 12.7 %broadcast_multiply_fusion.2 = (f32[6,1024,768]{2,1,0:T(8,128)}, f32[6,1024,768]{2,1,0:T(8,128)}) fusion(f32[6,1024]{1,0:T(8,128)S(1)} %get-tuple-element.333, f32[768]{0:T(1024)S(1)} %get-tuple-element.247, f32[6,1024]{1,0:T(8,128)S(1)} %get-tuple-element.342, f32[768]{0:T(1024)S(1)} %get-tuple-element.248), kind=kLoop, calls=%fused_computation.109 | loop fusion | flops 9437184 | bytes 37804032 | tf_op jit(solution)/shard_map/mul | solution.py:65
  258.3 12.6 %broadcast_multiply_fusion.4 = (f32[6,1024,768]{2,1,0:T(8,128)}, f32[6,1024,768]{2,1,0:T(8,128)}) fusion(f32[6,1024]{1,0:T(8,128)S(1)} %get-tuple-element.332, f32[768]{0:T(1024)S(1)} %get-tuple-element.250, f32[6,1024]{1,0:T(8,128)S(1)} %get-tuple-element.343, f32[768]{0:T(1024)S(1)} %get-tuple-element.251), kind=kLoop, calls=%fused_computation.111 | loop fusion | flops 9437184 | bytes 37804032 | tf_op jit(solution)/shard_map/mul | solution.py:65
  270.9 12.7 %broadcast_multiply_fusion.6 = (f32[6,1024,768]{2,1,0:T(8,128)}, f32[6,1024,768]{2,1,0:T(8,128)}) fusion(f32[6,1024]{1,0:T(8,128)S(1)} %get-tuple-element.340, f32[768]{0:T(1024)S(1)} %get-tuple-element.252, f32[6,1024]{1,0:T(8,128)S(1)} %get-tuple-element.331, f32[768]{0:T(1024)S(1)} %get-tuple-element.253), kind=kLoop, calls=%fused_computation.113 | loop fusion | flops 9437184 | bytes 37804032 | tf_op jit(solution)/shard_map/mul | solution.py:65
  283.6 14.4 %broadcast_multiply_fusion = (f32[6,1024,768]{2,1,0:T(8,128)}, f32[6,1024,768]{2,1,0:T(8,128)}) fusion(f32[6,1024]{1,0:T(8,128)S(1)} %get-tuple-element.341, f32[768]{0:T(1024)S(1)} %get-tuple-element.245, f32[6,1024]{1,0:T(8,128)S(1)} %get-tuple-element.339, f32[768]{0:T(1024)S(1)} %get-tuple-element.246), kind=kLoop, calls=%fused_computation.107 | loop fusion | flops 9437184 | bytes 37804032 | tf_op jit(solution)/shard_map/mul | solution.py:65
  298.0 7.1 fusion.97
  305.1 13.0 %fusion.151 = (f32[6,1008,768]{2,1,0:T(8,128)}, f32[6,1008,768]{2,1,0:T(8,128)}) fusion(f32[6,1024,768]{2,1,0:T(8,128)S(1)} %fusion.97), kind=kLoop, calls=%fused_computation.275 | loop fusion | bytes 74317824 | tf_op jit(solution)/shard_map/slice | solution.py:42
  318.1 14.9 %fusion.150 = (f32[6,1007,768]{2,1,0:T(8,128)}, f32[6,1007,768]{2,1,0:T(8,128)}) fusion(f32[6,1024,768]{2,1,0:T(8,128)S(1)} %fusion.97), kind=kLoop, calls=%fused_computation.274 | loop fusion | bytes 74244096 | tf_op jit(solution)/shard_map/slice | solution.py:42
  333.0 12.9 %fusion.152 = (f32[6,1009,768]{2,1,0:T(8,128)}, f32[6,1009,768]{2,1,0:T(8,128)}) fusion(f32[6,1024,768]{2,1,0:T(8,128)S(1)} %fusion.97), kind=kLoop, calls=%fused_computation.276 | loop fusion | bytes 74391552 | tf_op jit(solution)/shard_map/slice | solution.py:42
  345.9 12.7 %fusion.153 = (f32[6,1023,768]{2,1,0:T(8,128)}, f32[6,1023,768]{2,1,0:T(8,128)}) fusion(f32[6,1024,768]{2,1,0:T(8,128)S(1)} %fusion.97), kind=kLoop, calls=%fused_computation.277 | loop fusion | bytes 75423744 | tf_op jit(solution)/shard_map/slice | solution.py:42
  358.6 59.7 %multiply_convert_fusion.1 = (bf16[6,1024,768]{2,1,0:T(8,128)(2,1)}, f32[6,1024,768]{2,1,0:T(8,128)}) fusion(f32[6,1007,768]{2,1,0:T(8,128)} %get-tuple-element.320, f32[6,1024]{1,0:T(8,128)S(1)} %get-tuple-element.341, f32[768]{0:T(1024)S(1)} %get-tuple-element.245, f32[6,1008,768]{2,1,0:T(8,128)} %get-tuple-element.322, ...), kind=kLoop, calls=%fused_computation.100 | loop fusion | flops 169869312 | bytes 196602880 | tf_op jit(solution)/shard_map/convert_element_type | solution.py:193
  418.3 70.0 %multiply_reduce_fusion.9 = (f32[768]{0:T(1024)}, f32[768]{0:T(1024)}, f32[768]{0:T(1024)}, f32[768]{0:T(1024)}, f32[768]{0:T(1024)}, /*index=5*/f32[768]{0:T(10...) fusion(f32[6,1007,768]{2,1,0:T(8,128)} %get-tuple-element.320, ...), kind=kOutput, calls=%fused_computation.99 | convolution fusion | flops 3840926976 | bytes 211414016 | tf_op jit(solution)/shard_map/td,df->tf/dot_general | solution.py:204
  488.3 38.5 %slice_multiply_fusion.1 = (f32[6,1023,768]{2,1,0:T(8,128)}, f32[6,1023,768]{2,1,0:T(8,128)}) fusion(f32[6,1024,768]{2,1,0:T(8,128)} %get-tuple-element.352, f32[6,1024,768]{2,1,0:T(8,128)} %get-tuple-element.356, f32[6,1024,768]{2,1,0:T(8,128)} %get-tuple-element.357), kind=kLoop, calls=%fused_computation.90 | loop fusion | flops 9427968 | bytes 113135616 | tf_op jit(solution)/shard_map/transpose(jvp())/mul | solution.py:65
  529.9 26.8 %slice_multiply_fusion.3 = (f32[6,1009,768]{2,1,0:T(8,128)}, f32[6,1009,768]{2,1,0:T(8,128)}) fusion(f32[6,1024,768]{2,1,0:T(8,128)S(1)} %bitcast.200, f32[6,1024,768]{2,1,0:T(8,128)} %get-tuple-element.355, f32[6,1024,768]{2,1,0:T(8,128)} %get-tuple-element.358), kind=kLoop, calls=%fused_computation.102 | loop fusion | flops 9298944 | bytes 111587328 | tf_op jit(solution)/shard_map/transpose(jvp())/mul | solution.py:65
  556.7 25.0 %slice_multiply_fusion.7 = (f32[6,1007,768]{2,1,0:T(8,128)}, f32[6,1007,768]{2,1,0:T(8,128)}) fusion(f32[6,1024,768]{2,1,0:T(8,128)S(1)} %bitcast.200, f32[6,1024,768]{2,1,0:T(8,128)} %get-tuple-element.353, f32[6,1024,768]{2,1,0:T(8,128)} %get-tuple-element.360), kind=kLoop, calls=%fused_computation.106 | loop fusion | flops 9280512 | bytes 111366144 | tf_op jit(solution)/shard_map/transpose(jvp())/mul | solution.py:65
  581.6 25.9 %slice_multiply_fusion.6 = (f32[6,1008,768]{2,1,0:T(8,128)}, f32[6,1008,768]{2,1,0:T(8,128)}) fusion(f32[6,1024,768]{2,1,0:T(8,128)S(1)} %bitcast.200, f32[6,1024,768]{2,1,0:T(8,128)} %get-tuple-element.354, f32[6,1024,768]{2,1,0:T(8,128)} %get-tuple-element.359), kind=kLoop, calls=%fused_computation.105 | loop fusion | flops 9289728 | bytes 111476736 | tf_op jit(solution)/shard_map/transpose(jvp())/mul | solution.py:65
  607.5 56.8 %fusion.67 = bf16[6,1024,768]{2,1,0:T(8,128)(2,1)} fusion(f32[6,1024,768]{2,1,0:T(8,128)} %get-tuple-element.352, f32[6,1007,768]{2,1,0:T(8,128)} %get-tuple-element.312, f32[6,1008,768]{2,1,0:T(8,128)} %get-tuple-element.314, f32[6,1009,768]{2,1,0:T(8,128)} %get-tuple-element.316, f32[6,1023,768]{2,1,0:T(8,128)} %get-tuple-element.318, ...), kind=kLoop, calls=%fused_computation.82 | loop fusion | flops 56623104 | bytes 177507328 | tf_op jit(solution)/shard_map/convert_element_type | solution.py:216
  664.4 10.9 fusion.99
  675.4 11.4 fusion.95
  686.9 7.5 reduce-scatter.10.cloned.1.call-done
  700.2 15.6 %reduce-scatter.8.cloned.1.call-done = f32[3072,384]{1,0:T(8,128)} async-done(((f32[6144,384]{1,0:T(8,128)}), f32[3072,384]{1,0:T(8,128)}) %reduce-scatter.8.cloned.1.call-update) | async-done | bytes 4718608 | tf_op jit(solution)/shard_map/reduce_scatter | solution.py:195
  715.8 10.2 fusion.147
  726.1 9.7 convolution_bitcast_fusion.1
  750.7 7.4 reshape.355
  763.1 183.0 %while.23 = (s32[]{:T(128)}, bf16[6,1024,3,3,64]{1,4,3,2,0:T(8,128)(2,1)}, bf16[6,1024,3,64]{1,3,2,0:T(8,128)(2,1)}, s32[6,1024]{1,0:T(8,128)}, bf16[6,1024,3,64...) while((s32[]{:T(128)}, ...), condition=%wide.region_15.16_spmd, body=%wide.region_13.15_spmd.sunk | while | flops 2066019328 | bytes 104966256 | solution.py:243
  772.2 8.2 multiply_reduce_fusion.22
  780.4 7.0 multiply_convert_fusion.4
  802.7 8.2 multiply_reduce_fusion.22
  833.1 8.2 multiply_reduce_fusion.22
  841.3 7.0 multiply_convert_fusion.4
  863.6 8.2 multiply_reduce_fusion.22
  871.7 7.0 multiply_convert_fusion.4
  894.0 8.2 multiply_reduce_fusion.22
  924.4 8.2 multiply_reduce_fusion.22
  946.1 11.8 copy.137
  957.9 15.8 %reshape.354 = bf16[6144,3,192]{0,2,1:T(8,128)(2,1)} reshape(bf16[6,1024,3,3,64]{1,0,4,3,2:T(8,128)(2,1)} %copy.137) | data formatting | bytes 14155776 | tf_op jit(solution)/shard_map/reshape | solution.py:246
  977.5 7.5 fusion.91
  987.0 10.4 convolution_bitcast_fusion
  999.1 78.1 %psum.21 = f32[9,768]{1,0:T(8,128)S(1)} all-reduce(f32[9,768]{1,0:T(8,128)S(1)} %pad_add_fusion), channel_id=1, replica_groups=mesh['dp'=16,'head'=2] {'dp'}, use_global_device_ids=true, to_apply=%region_35.36 | all-reduce | flops 6912 | bytes 55296 | tf_op jit(solution)/shard_map/psum | solution.py:267
  1081.0 24.2 %all-reduce.37.cloned.1.call-done = f32[4,384,192]{2,0,1:T(4,128)} async-done(((f32[4,384,192]{2,0,1:T(4,128)}), f32[4,384,192]{2,0,1:T(4,128)}) %all-reduce.37.cloned.1.call-update) | async-done | bytes 1179664
  1108.0 16.5 %reduce-scatter.12.cloned.1.call-done = f32[3072,384]{1,0:T(8,128)} async-done(((f32[6144,384]{1,0:T(8,128)}), f32[3072,384]{1,0:T(8,128)}) %reduce-scatter.12.cloned.1.call-update) | async-done | bytes 4718608 | tf_op jit(solution)/shard_map/reduce_scatter | solution.py:251
  1129.1 40.9 %all-reduce.34 = (f32[2,7]{1,0:T(2,128)S(1)}, f32[4,384]{1,0:T(4,128)S(1)}) all-reduce(f32[2,7]{1,0:T(2,128)S(1)} %pad_maximum_fusion.3, f32[4,384]{1,0:T(4,128)S(1)} %pad_maximum_fusion.2), channel_id=1, replica_groups=mesh['dp'=16,'head'=2] {'dp','head'}, use_global_device_ids=true, to_apply=%region_37.38 | all-reduce | flops 1550 | bytes 12400 | tf_op jit(solution)/shard_map/psum | solution.py:290
  1174.1 7.4 fusion.86
  (361 shorter events, 303.7 us)
Async XLA Ops:
  8.0 61.9 %copy-start.61 = (s32[6]{0:T(128)S(1)}, s32[6]{0:T(128)}, u32[]{:S(2)}) copy-start(s32[6]{0:T(128)} %param.23) | copy-start | bytes 76
  8.0 61.9 %all-gather.6.cloned.1.call-start = ((), (), s32[]{:S(2)}) async-start(), calls=%async_computation.5 | async-start | bytes 7077888 | tf_op jit(solution)/shard_map/all_gather | solution.py:168
  19.2 217.0 %reduce-scatter.6.cloned.1.call-start = ((), (), s32[]{:S(2)}) async-start(), calls=%async_computation.6 | async-start | bytes 14155776 | tf_op jit(solution)/shard_map/reduce_scatter | solution.py:179
  116.1 100.7 %copy-start.12 = (bf16[1,384,192]{1,2,0:T(8,128)(2,1)S(1)}, bf16[1,384,192]{1,2,0:T(8,128)(2,1)}, u32[]{:S(2)}) copy-start(bf16[1,384,192]{1,2,0:T(8,128)(2,1)} %copy.149) | copy-start | bytes 442372
  222.3 75.7 %all-gather.10.cloned.1.call-start = ((), (), s32[]{:S(2)}) async-start(), calls=%async_computation.8 | async-start | bytes 1253376 | tf_op jit(solution)/shard_map/all_gather | solution.py:153
  223.0 75.0 %all-gather.8.cloned.1.call-start = ((), (), s32[]{:S(2)}) async-start(), calls=%async_computation.7 | async-start | bytes 7077888 | tf_op jit(solution)/shard_map/all_gather | solution.py:188
  244.3 174.0 %all-gather.12.cloned.1.call-start = ((), (), s32[]{:S(2)}) async-start(), calls=%async_computation.10 | async-start | bytes 7077888 | tf_op jit(solution)/shard_map/all_gather | solution.py:203
  244.9 449.5 %reduce-scatter.10.cloned.1.call-start = ((), (), s32[]{:S(2)}) async-start(), calls=%async_computation.11 | async-start | bytes 14155776 | tf_op jit(solution)/shard_map/reduce_scatter | solution.py:221
  245.4 113.2 %copy-start.38 = (f32[768]{0:T(1024)}, f32[768]{0:T(1024)S(1)}, u32[]{:S(2)}) copy-start(f32[768]{0:T(1024)S(1)} %get-tuple-element.249) | copy-start | bytes 9220
  305.1 53.5 %copy-start = (f32[6,1024,768]{2,1,0:T(8,128)}, f32[6,1024,768]{2,1,0:T(8,128)S(1)}, u32[]{:S(2)}) copy-start(f32[6,1024,768]{2,1,0:T(8,128)S(1)} %fusion.97) | copy-start | bytes 56623108
  358.6 59.7 %copy-start.26 = (bf16[2,384,768]{2,1,0:T(8,128)(2,1)S(1)}, bf16[2,384,768]{2,1,0:T(8,128)(2,1)}, u32[]{:S(2)}) copy-start(bf16[2,384,768]{2,1,0:T(8,128)(2,1)} %all-gather.10.cloned.1.call-done) | copy-start | bytes 3538948
  488.3 38.5 %slice-start = ((s8[18874368]{0:T(1024)(128)(4,1)}), s8[4194304]{0:T(1024)(128)(4,1)S(1)}, s32[]{:S(2)}) async-start(s8[18874368]{0:T(1024)(128)(4,1)} %bitcast.199), calls=%async_computation.16 | async-start | bytes 8388608
  488.3 38.5 %slice-start.1 = ((s8[18874368]{0:T(1024)(128)(4,1)}), s8[4194304]{0:T(1024)(128)(4,1)S(1)}, s32[]{:S(2)}) async-start(s8[18874368]{0:T(1024)(128)(4,1)} %bitcast.199), calls=%async_computation.17 | async-start | bytes 8388608
  488.3 39.8 %slice-start.2 = ((s8[18874368]{0:T(1024)(128)(4,1)}), s8[4194304]{0:T(1024)(128)(4,1)S(1)}, s32[]{:S(2)}) async-start(s8[18874368]{0:T(1024)(128)(4,1)} %bitcast.199), calls=%async_computation.18 | async-start | bytes 8388608
  488.3 41.0 %slice-start.3 = ((s8[18874368]{0:T(1024)(128)(4,1)}), s8[4194304]{0:T(1024)(128)(4,1)S(1)}, s32[]{:S(2)}) async-start(s8[18874368]{0:T(1024)(128)(4,1)} %bitcast.199), calls=%async_computation.19 | async-start | bytes 8388608
  488.3 41.6 %slice-start.4 = ((s8[18874368]{0:T(1024)(128)(4,1)}), s8[2097152]{0:T(1024)(128)(4,1)S(1)}, s32[]{:S(2)}) async-start(s8[18874368]{0:T(1024)(128)(4,1)} %bitcast.199), calls=%async_computation.20 | async-start | bytes 4194304
  581.6 25.9 %copy-start.39 = (f32[768]{0:T(1024)S(1)}, f32[768]{0:T(1024)}, u32[]{:S(2)}) copy-start(f32[768]{0:T(1024)} %copy-done.38) | copy-start | bytes 9220
  607.5 56.9 %copy-start.27 = (bf16[2,384,768]{2,1,0:T(8,128)(2,1)S(1)}, bf16[2,384,768]{2,1,0:T(8,128)(2,1)}, u32[]{:S(2)}) copy-start(bf16[2,384,768]{2,1,0:T(8,128)(2,1)} %all-gather.10.cloned.1.call-done) | copy-start | bytes 3538948
  675.4 40.4 %reduce-scatter.8.cloned.1.call-start = ((), (), s32[]{:S(2)}) async-start(), calls=%async_computation.9 | async-start | bytes 14155776 | tf_op jit(solution)/shard_map/reduce_scatter | solution.py:195
  686.8 28.9 %copy-start.7 = (bf16[3072,384]{1,0:T(8,128)(2,1)S(1)}, bf16[3072,384]{1,0:T(8,128)(2,1)}, u32[]{:S(2)}) copy-start(bf16[3072,384]{1,0:T(8,128)(2,1)} %param.21) | copy-start | bytes 7077892
  686.9 57.4 %all-gather.14.cloned.1.call-start = ((), (), s32[]{:S(2)}) async-start(), calls=%async_computation.12 | async-start | bytes 7077888 | tf_op jit(solution)/shard_map/all_gather | solution.py:232
  700.2 25.9 %copy-start.46 = (f32[6,3]{1,0:T(8,128)S(1)}, f32[6,3]{1,0:T(8,128)}, u32[]{:S(2)}) copy-start(f32[6,3]{1,0:T(8,128)} %copy-done.45) | copy-start | bytes 220
  726.0 353.2 %reduce-scatter.14.cloned.1.call-start = ((), (), s32[]{:S(2)}) async-start(), calls=%async_computation.14 | async-start | bytes 2506752 | tf_op jit(solution)/shard_map/reduce_scatter | solution.py:265
  744.2 361.0 %all-reduce.37.cloned.1.call-start = ((), (), s32[]{:S(2)}) async-start(), calls=%async_computation.15 | async-start | bytes 3145728
  946.1 27.6 %copy-start.6 = (bf16[24,8,6,1024]{3,1,2,0:T(8,128)(2,1)S(1)}, bf16[24,8,6,1024]{3,1,2,0:T(8,128)(2,1)}, u32[]{:S(2)}) copy-start(bf16[24,8,6,1024]{3,1,2,0:T(8,128)(2,1)} %copy-done.5) | copy-start | bytes 7077892
  986.8 90.4 %copy-start.18 = (f32[9,768]{1,0:T(8,128)S(1)}, f32[9,768]{1,0:T(8,128)}, u32[]{:S(2)}) copy-start(f32[9,768]{1,0:T(8,128)} %param.30) | copy-start | bytes 82948
  986.8 90.3 %copy-start.36 = (f32[9,768]{1,0:T(8,128)S(1)}, f32[9,768]{1,0:T(8,128)}, u32[]{:S(2)}) copy-start(f32[9,768]{1,0:T(8,128)} %param.31) | copy-start | bytes 82948
  986.9 90.3 %copy-start.37 = (f32[9,768]{1,0:T(8,128)S(1)}, f32[9,768]{1,0:T(8,128)}, u32[]{:S(2)}) copy-start(f32[9,768]{1,0:T(8,128)} %param.32) | copy-start | bytes 82948
  986.9 92.3 %copy-start.11 = (f32[2,24,768]{2,1,0:T(8,128)S(1)}, f32[2,24,768]{2,1,0:T(8,128)}, u32[]{:S(2)}) copy-start(f32[2,24,768]{2,1,0:T(8,128)} %param.27) | copy-start | bytes 442372
  986.9 92.3 %copy-start.34 = (f32[2,24,768]{2,1,0:T(8,128)S(1)}, f32[2,24,768]{2,1,0:T(8,128)}, u32[]{:S(2)}) copy-start(f32[2,24,768]{2,1,0:T(8,128)} %param.28) | copy-start | bytes 442372
  986.9 94.1 %copy-start.48 = (f32[384]{0:T(512)S(1)}, f32[384]{0:T(512)}, u32[]{:S(2)}) copy-start(f32[384]{0:T(512)} %get-tuple-element.231) | copy-start | bytes 4612
  986.9 94.1 %copy-start.47 = (f32[384]{0:T(512)S(1)}, f32[384]{0:T(512)}, u32[]{:S(2)}) copy-start(f32[384]{0:T(512)} %get-tuple-element.238) | copy-start | bytes 4612
  986.9 119.2 %copy-start.14 = (f32[4,24,192]{2,1,0:T(8,128)S(1)}, f32[4,24,192]{2,1,0:T(8,128)}, u32[]{:S(2)}) copy-start(f32[4,24,192]{2,1,0:T(8,128)} %param.24) | copy-start | bytes 221188
  986.9 119.2 %copy-start.35 = (f32[4,24,192]{2,1,0:T(8,128)S(1)}, f32[4,24,192]{2,1,0:T(8,128)}, u32[]{:S(2)}) copy-start(f32[4,24,192]{2,1,0:T(8,128)} %param.25) | copy-start | bytes 221188
  986.9 137.6 %copy-start.23 = (f32[3072]{0:T(1024)S(1)}, f32[3072]{0:T(1024)}, u32[]{:S(2)}) copy-start(f32[3072]{0:T(1024)} %copy-done.22) | copy-start | bytes 36868
  986.9 137.5 %copy-start.31 = (f32[3072]{0:T(1024)S(1)}, f32[3072]{0:T(1024)}, u32[]{:S(2)}) copy-start(f32[3072]{0:T(1024)} %copy-done.30) | copy-start | bytes 36868
  987.0 137.5 %copy-start.41 = (f32[384]{0:T(512)S(1)}, f32[384]{0:T(512)}, u32[]{:S(2)}) copy-start(f32[384]{0:T(512)} %copy-done.40) | copy-start | bytes 4612
  987.0 137.5 %reduce-scatter.12.cloned.1.call-start = ((), (), s32[]{:S(2)}) async-start(), calls=%async_computation.13 | async-start | bytes 14155776 | tf_op jit(solution)/shard_map/reduce_scatter | solution.py:251
  997.4 127.1 %copy-start.4 = (bf16[3072,384]{1,0:T(8,128)(2,1)S(1)}, bf16[3072,384]{1,0:T(8,128)(2,1)}, u32[]{:S(2)}) copy-start(bf16[3072,384]{1,0:T(8,128)(2,1)} %param.20) | copy-start | bytes 7077892
  997.4 173.9 %copy-start.44 = (f32[4,384]{1,0:T(4,128)S(1)}, f32[4,384]{1,0:T(4,128)}, u32[]{:S(2)}) copy-start(f32[4,384]{1,0:T(4,128)} %param.33) | copy-start | bytes 18436
  997.4 173.9 %copy-start.50 = (f32[4,384]{1,0:T(4,128)S(1)}, f32[4,384]{1,0:T(4,128)}, u32[]{:S(2)}) copy-start(f32[4,384]{1,0:T(4,128)} %param.34) | copy-start | bytes 18436
  997.4 173.9 %copy-start.51 = (f32[4,384]{1,0:T(4,128)S(1)}, f32[4,384]{1,0:T(4,128)}, u32[]{:S(2)}) copy-start(f32[4,384]{1,0:T(4,128)} %param.35) | copy-start | bytes 18436
  1077.9 103.6 %copy-start.28 = (f32[9,768]{1,0:T(8,128)}, f32[9,768]{1,0:T(8,128)S(1)}, u32[]{:S(2)}) copy-start(f32[9,768]{1,0:T(8,128)S(1)} %get-tuple-element.299) | copy-start | bytes 82948
  1077.9 103.6 %copy-start.29 = (f32[9,768]{1,0:T(8,128)}, f32[9,768]{1,0:T(8,128)S(1)}, u32[]{:S(2)}) copy-start(f32[9,768]{1,0:T(8,128)S(1)} %get-tuple-element.300) | copy-start | bytes 82948
  1080.9 100.6 %copy-start.15 = (f32[2,24,768]{2,1,0:T(8,128)}, f32[2,24,768]{2,1,0:T(8,128)S(1)}, u32[]{:S(2)}) copy-start(f32[2,24,768]{2,1,0:T(8,128)S(1)} %get-tuple-element.297) | copy-start | bytes 442372
  1080.9 100.6 %copy-start.16 = (f32[2,24,768]{2,1,0:T(8,128)}, f32[2,24,768]{2,1,0:T(8,128)S(1)}, u32[]{:S(2)}) copy-start(f32[2,24,768]{2,1,0:T(8,128)S(1)} %get-tuple-element.298) | copy-start | bytes 442372
  1107.2 74.3 %copy-start.19 = (f32[4,24,192]{2,1,0:T(8,128)}, f32[4,24,192]{2,1,0:T(8,128)S(1)}, u32[]{:S(2)}) copy-start(f32[4,24,192]{2,1,0:T(8,128)S(1)} %get-tuple-element.295) | copy-start | bytes 221188
  1107.2 74.3 %copy-start.20 = (f32[4,24,192]{2,1,0:T(8,128)}, f32[4,24,192]{2,1,0:T(8,128)S(1)}, u32[]{:S(2)}) copy-start(f32[4,24,192]{2,1,0:T(8,128)S(1)} %get-tuple-element.296) | copy-start | bytes 221188
  (39 other events, 397.1 us)
Sparse Core Ops, SparseCore 0:
  19.3 17.1 all-gather.5
  222.4 13.7 reduce-scatter.5
  726.1 15.8 all-gather.13
Sparse Core Ops, SparseCore 1:
  226.0 52.0 all-gather.9
  280.1 13.1 all-gather.7
  294.6 15.5 all-gather.11
  675.4 18.9 reduce-scatter.9
  696.7 19.0 reduce-scatter.7
  744.3 129.9 reduce-scatter.13
  986.8 118.3 all-reduce.36
  1107.4 17.1 reduce-scatter.11
where the time goes:
time: 1200 us; the launch traced here: 1190 us
  other arithmetic  435 us (36%)
  matrix products  337 us (28%)
  blocking collectives  166 us (14%)
  local copies, waits for them, and re-layouts  152 us (13%)
  waiting for transfers between devices  77.6 us (6%)
  between operations  19.4 us (2%)
    mul x8, other arithmetic, depthwise(): tap_weights[tap_index] * tap_mask[tap_index][:, :, None]  169 us
    psum x1, blocking collectives, body(): grad_conv = lax.psum(grad_conv, 'dp')  78.1 us
    dot_general x1, matrix products, body(): jnp.einsum('td,df->tf', grad_rows_all, mlp_full[1], preferred_element_typ...  70 us
    convert_element_type x1, other arithmetic, body(): jax.nn.gelu(mixed_rows).reshape(row_total * length, -1).astype(jnp.bfloat16)  59.7 us
    convert_element_type x1, other arithmetic, body(): grad_hidden.reshape(row_total * length, -1).astype(jnp.bfloat16)  56.8 us
    slice x8, local copies, waits for them, and re-layouts, shifted(): return jnp.concatenate([padding, values[:, :offset]], axis=1)  53.8 us
    dot_general x6, matrix products, attend_backward(): jnp.einsum('qhe,khe->hqk', grad_context, value_rows, preferred_element_ty...  49.1 us
    all_gather x1, blocking collectives, body(): lax.all_gather(attn_w.astype(jnp.bfloat16), 'dp', axis=1, tiled=True)  47.2 us
  transfers between devices with their start and end apart: 11, of which 5 were waited for; matrix products, arithmetic and copies ran while one was open for 40% of the time, Pallas kernels for 0%

commit v1 on v0

v1 whole, which is shorter than its diff:
```python
import functools
import jax
import jax.numpy as jnp
from jax import lax
from jax.experimental import pallas as pl
from jax.experimental.pallas import tpu as pltpu
from jax.sharding import PartitionSpec as P

HEAD_DIM = 64
GRID_W = 16
STEP = 10
IMAGES = 8

NORM_EPS = 1e-06
BETA_ONE = 0.9
BETA_TWO = 0.999
ADAM_EPS = 1e-06
DECAY = 0.01
RATE = 0.5
LOG2E = 1.4426950408889634
LN2 = 0.6931471805599453
BIG = 2.0**100
GELU_ONE = 0.7978845608028654
GELU_TWO = 0.044715
TILE = 128
LANES = 128
VMEM_BYTES = 60 * 1024 * 1024

f32 = jnp.float32
bf16 = jnp.bfloat16
NN = (((1,), (0,)), ((), ()))
NT = (((1,), (1,)), ((), ()))
TN = (((0,), (0,)), ((), ()))


def dot(left, right, dims=NN):
    return lax.dot_general(left, right, dims, preferred_element_type=f32)


def widths_for(length):
    return [w for w in (256, 384, 512, 768) if w < length] + [length]


def lane_iota(rows):
    return lax.broadcasted_iota(jnp.int32, (rows, LANES), 1)


def norm_parts(values):
    average = jnp.mean(values, axis=-1, keepdims=True)
    centered = values - average
    inverse = lax.rsqrt(jnp.mean(centered * centered, axis=-1, keepdims=True) + NORM_EPS)
    return centered * inverse, inverse


def norm_back(upstream, gain_row, unit_rows, inverse):
    grad_unit = upstream * gain_row
    first_term = jnp.mean(grad_unit, axis=-1, keepdims=True)
    second_term = jnp.mean(grad_unit * unit_rows, axis=-1, keepdims=True)
    return inverse * (grad_unit - first_term - unit_rows * second_term)


def fold_rows(values):
    rows, columns = values.shape
    return jnp.sum(values.reshape(rows // 8, 8, columns), axis=0)


def half_masks():
    lane = lax.broadcasted_iota(jnp.int32, (1, LANES), 1)
    first = (lane < HEAD_DIM).astype(f32).astype(bf16)
    second = (lane >= HEAD_DIM).astype(f32).astype(bf16)
    return first, second


def split_lanes(column, lane, at):
    high = column.astype(bf16).astype(f32)
    rest = column - high
    middle = rest.astype(bf16).astype(f32)
    low = rest - middle
    return jnp.where(lane == at, high, jnp.where(lane == at + 1, middle, jnp.where(lane == at + 2, low, 0.0)))


def attn_forward_kernel(
    start_ref, class_ref, count_ref, tokens_ref, w_ref, norm_ref, image_ref,
    middle_ref, qkv_ref, context_ref, ext_ref, tag_ref,
):
    row = pl.program_id(0)
    length, width = tokens_ref.shape
    pairs = width // LANES
    big = 256
    gain, bias = norm_ref[0:1, :], norm_ref[1:2, :]
    first_row, last_row = image_ref[0, 0:1, :], image_ref[0, 1:2, :]

    def project(step, carry):
        rows = pl.ds(pl.multiple_of(step * big, big), big)
        unit, _ = norm_parts(tokens_ref[rows, :].astype(f32))
        normed = (unit * gain + bias).astype(bf16)
        for k in range(3):
            product = dot(normed, w_ref[k])
            if k == 0:
                product = product * (HEAD_DIM**-0.5 * LOG2E)
            qkv_ref[rows, k * width : (k + 1) * width] = product.astype(bf16)
        place = step * big + lax.broadcasted_iota(jnp.int32, (big, LANES), 0)
        inside = (place >= first_row) & (place < last_row)
        tag_ref[rows, :] = jnp.where(inside, 1.0, 0.0).astype(bf16)
        return carry

    lax.fori_loop(0, length // big, project, 0)
    first_half, second_half = half_masks()

    def tile(step, carry):
        q0 = pl.multiple_of(step * TILE, TILE)
        here = pl.ds(q0, TILE)

        def attend(window):
            there = pl.ds(pl.multiple_of(start_ref[row, step], GRID_W), window)
            lane = lane_iota(TILE)
            tags = tag_ref[there, :]
            base = jnp.where(lane < IMAGES, (tag_ref[here, :].astype(f32) - 1.0) * BIG, 0.0)
            base_low = base.astype(bf16)
            for p in range(pairs):
                at = slice(p * LANES, (p + 1) * LANES)
                queries = qkv_ref[here, at]
                keys = qkv_ref[there, width + p * LANES : width + (p + 1) * LANES]
                values = qkv_ref[there, 2 * width + p * LANES : 2 * width + (p + 1) * LANES]
                left = jnp.concatenate(
                    [
                        jnp.concatenate([queries * first_half, base_low], axis=1),
                        jnp.concatenate([queries * second_half, base_low], axis=1),
                    ],
                    axis=0,
                )
                scores = dot(left, jnp.concatenate([keys, tags], axis=1), NT)
                row_max = jnp.max(scores, axis=1, keepdims=True)
                exponent = jnp.exp2(scores - row_max).astype(bf16)
                mixed = dot(exponent, jnp.concatenate([values, tags], axis=1))
                total = mixed[:, LANES + IMAGES : LANES + IMAGES + 1]
                minus_lse = -(row_max + jnp.log(total) * LOG2E)
                scale = 1.0 / total
                active_one = jnp.where(2 * p < count_ref[row], 1.0, 0.0)
                active_two = jnp.where(2 * p + 1 < count_ref[row], 1.0, 0.0)
                context = jnp.where(
                    lane < HEAD_DIM,
                    mixed[:TILE, :LANES] * (scale[:TILE] * active_one),
                    mixed[TILE:, :LANES] * (scale[TILE:] * active_two),
                )
                context_ref[here, at] = context.astype(bf16)
                base = base + split_lanes(minus_lse[:TILE], lane, IMAGES + 6 * p)
                base = base + split_lanes(minus_lse[TILE:], lane, IMAGES + 6 * p + 3)
            ext_ref[here, :] = base.astype(bf16)

        for index, window in enumerate(widths_for(length)):
            pl.when(class_ref[row, step] == index)(functools.partial(attend, window))
        return carry

    lax.fori_loop(0, length // TILE, tile, 0)

    def finish(step, carry):
        rows = pl.ds(pl.multiple_of(step * big, big), big)
        middle_ref[rows, :] = tokens_ref[rows, :].astype(f32) + dot(context_ref[rows, :], w_ref[3], NT)
        return carry

    lax.fori_loop(0, length // big, finish, 0)


def attn_forward(starts, classes, counts, tokens, attn_use, norm_w, images):
    rows_all, width = tokens.shape
    row_count = counts.shape[0]
    length = rows_all // row_count
    by_row = lambda columns: pl.BlockSpec((length, columns), lambda r, *_: (r, 0))
    return pl.pallas_call(
        attn_forward_kernel,
        grid_spec=pltpu.PrefetchScalarGridSpec(
            num_scalar_prefetch=3,
            grid=(row_count,),
            in_specs=[
                by_row(width),
                pl.BlockSpec(attn_use.shape, lambda r, *_: (0, 0, 0)),
                pl.BlockSpec(norm_w.shape, lambda r, *_: (0, 0)),
                pl.BlockSpec((1, 8, LANES), lambda r, *_: (r, 0, 0)),
            ],
            out_specs=[by_row(width), by_row(3 * width), by_row(width), by_row(LANES)],
            scratch_shapes=[pltpu.VMEM((length, LANES), bf16)],
        ),
        out_shape=[
            jax.ShapeDtypeStruct((rows_all, width), f32),
            jax.ShapeDtypeStruct((rows_all, 3 * width), bf16),
            jax.ShapeDtypeStruct((rows_all, width), bf16),
            jax.ShapeDtypeStruct((rows_all, LANES), bf16),
        ],
        compiler_params=pltpu.CompilerParams(vmem_limit_bytes=VMEM_BYTES),
    )(starts, classes, counts, tokens, attn_use, norm_w, images)


def attn_backward_kernel(
    start_ref, class_ref, count_ref, tokens_ref, middle_grad_ref, qkv_ref, context_ref, ext_ref, w_ref, norm_ref, image_ref,
    tokens_grad_ref, w_grad_ref, norm_grad_ref,
    tag_ref, up_ref, delta_ref, normed_ref, dq_ref, dk_ref, dv_ref, low_ref, proj_ref,
):
    row = pl.program_id(0)
    length, width = tokens_ref.shape
    pairs = width // LANES
    heads = 2 * pairs
    big = 256
    gain, bias = norm_ref[0:1, :], norm_ref[1:2, :]
    first_row, last_row = image_ref[0, 0:1, :], image_ref[0, 1:2, :]

    @pl.when(row == 0)
    def _():
        w_grad_ref[...] = jnp.zeros_like(w_grad_ref)
        norm_grad_ref[...] = jnp.zeros_like(norm_grad_ref)

    source = lax.broadcasted_iota(jnp.int32, (width, LANES), 0)
    target = lax.broadcasted_iota(jnp.int32, (width, LANES), 1) - IMAGES
    low_edge = source // HEAD_DIM * 3
    collect = jnp.where((target >= low_edge) & (target < low_edge + 3), 1.0, 0.0).astype(bf16)
    active = jnp.where(
        lax.broadcasted_iota(jnp.int32, (1, width), 1) // HEAD_DIM < count_ref[row], 1.0, 0.0
    )

    def prepare(step, carry):
        rows = pl.ds(pl.multiple_of(step * big, big), big)
        unit, _ = norm_parts(tokens_ref[rows, :].astype(f32))
        normed_ref[rows, :] = (unit * gain + bias).astype(bf16)
        place = step * big + lax.broadcasted_iota(jnp.int32, (big, LANES), 0)
        inside = (place >= first_row) & (place < last_row)
        tag_ref[rows, :] = jnp.where(inside, 1.0, 0.0).astype(bf16)
        low = middle_grad_ref[rows, :].astype(bf16)
        low_ref[rows, :] = low
        up = (dot(low, w_ref[3]) * active).astype(bf16)
        up_ref[rows, :] = up
        product = up.astype(f32) * context_ref[rows, :].astype(f32)
        high = product.astype(bf16)
        rest = (product - high.astype(f32)).astype(bf16)
        delta = -(dot(high, collect) + dot(rest, collect))
        lane = lane_iota(big)
        part = lax.rem(lane + 3 * LANES - IMAGES, 3)
        d_high = delta.astype(bf16).astype(f32)
        d_rest = delta - d_high
        d_mid = d_rest.astype(bf16).astype(f32)
        delta_ref[rows, :] = jnp.where(
            part == 0, d_high, jnp.where(part == 1, d_mid, d_rest - d_mid)
        ).astype(bf16)
        dk_ref[rows, :] = jnp.zeros((big, width), f32)
        dv_ref[rows, :] = jnp.zeros((big, width), f32)
        return carry

    lax.fori_loop(0, length // big, prepare, 0)
    first_half, second_half = half_masks()

    def tile(step, carry):
        q0 = pl.multiple_of(step * TILE, TILE)
        here = pl.ds(q0, TILE)

        def attend(window):
            there = pl.ds(pl.multiple_of(start_ref[row, step], GRID_W), window)
            lane = lax.broadcasted_iota(jnp.int32, (1, LANES), 1)
            tags = tag_ref[there, :]
            ext = ext_ref[here, :]
            delta = delta_ref[here, :]
            for p in range(pairs):
                at = slice(p * LANES, (p + 1) * LANES)
                queries = qkv_ref[here, at]
                keys = qkv_ref[there, width + p * LANES : width + (p + 1) * LANES]
                values = qkv_ref[there, 2 * width + p * LANES : 2 * width + (p + 1) * LANES]
                ups = up_ref[here, at]
                edge = IMAGES + 6 * p
                keep_one = jnp.where((lane < IMAGES) | ((lane >= edge) & (lane < edge + 3)), 1.0, 0.0).astype(bf16)
                keep_two = jnp.where((lane < IMAGES) | ((lane >= edge + 3) & (lane < edge + 6)), 1.0, 0.0).astype(bf16)
                only_one = jnp.where((lane >= edge) & (lane < edge + 3), 1.0, 0.0).astype(bf16)
                only_two = jnp.where((lane >= edge + 3) & (lane < edge + 6), 1.0, 0.0).astype(bf16)
                q_pair = jnp.concatenate([queries * first_half, queries * second_half], axis=0)
                up_pair = jnp.concatenate([ups * first_half, ups * second_half], axis=0)
                q_side = jnp.concatenate(
                    [q_pair, jnp.concatenate([ext * keep_one, ext * keep_two], axis=0)], axis=1
                )
                up_side = jnp.concatenate(
                    [up_pair, jnp.concatenate([delta * only_one, delta * only_two], axis=0)], axis=1
                )
                probs = jnp.exp2(dot(jnp.concatenate([keys, tags], axis=1), q_side, NT))
                grad_probs = dot(jnp.concatenate([values, tags], axis=1), up_side, NT)
                grad_scores = (probs * grad_probs).astype(bf16)
                dv_ref[there, at] += dot(probs.astype(bf16), up_pair)
                dk_ref[there, at] += dot(grad_scores, q_pair)
                dq = dot(keys, grad_scores, TN)
                half = lax.broadcasted_iota(jnp.int32, (LANES, TILE), 0)
                dq = jnp.where(half < HEAD_DIM, dq[:, :TILE], dq[:, TILE:])
                dq_ref[here, at] = jnp.transpose(dq * HEAD_DIM**-0.5).astype(bf16)

        for index, window in enumerate(widths_for(length)):
            pl.when(class_ref[row, step] == index)(functools.partial(attend, window))
        return carry

    lax.fori_loop(0, length // TILE, tile, 0)

    def finish(step, carry):
        rows = pl.ds(pl.multiple_of(step * big, big), big)
        queries_grad = dq_ref[rows, :]
        keys_grad = (dk_ref[rows, :] * LN2).astype(bf16)
        values_grad = dv_ref[rows, :].astype(bf16)
        proj_ref[rows, :] = jnp.concatenate([queries_grad, keys_grad, values_grad], axis=1)
        upstream = dot(queries_grad, w_ref[0], NT) + dot(keys_grad, w_ref[1], NT) + dot(values_grad, w_ref[2], NT)
        unit, inverse = norm_parts(tokens_ref[rows, :].astype(f32))
        tokens_grad_ref[rows, :] = middle_grad_ref[rows, :] + norm_back(upstream, gain, unit, inverse)
        norm_grad_ref[0:8, :] += fold_rows(upstream * unit)
        norm_grad_ref[8:16, :] += fold_rows(upstream)
        return carry

    lax.fori_loop(0, length // big, finish, 0)
    normed_t = jnp.transpose(normed_ref[...])
    for k in range(3):
        w_grad_ref[k] += dot(normed_t, proj_ref[:, k * width : (k + 1) * width])
    w_grad_ref[3] += dot(jnp.transpose(low_ref[...]), context_ref[...])


def attn_backward(starts, classes, counts, tokens, middle_grad, qkv, context, ext, attn_use, norm_w, images):
    rows_all, width = tokens.shape
    row_count = counts.shape[0]
    length = rows_all // row_count
    by_row = lambda columns: pl.BlockSpec((length, columns), lambda r, *_: (r, 0))
    return pl.pallas_call(
        attn_backward_kernel,
        grid_spec=pltpu.PrefetchScalarGridSpec(
            num_scalar_prefetch=3,
            grid=(row_count,),
            in_specs=[
                by_row(width),
                by_row(width),
                by_row(3 * width),
                by_row(width),
                by_row(LANES),
                pl.BlockSpec(attn_use.shape, lambda r, *_: (0, 0, 0)),
                pl.BlockSpec(norm_w.shape, lambda r, *_: (0, 0)),
                pl.BlockSpec((1, 8, LANES), lambda r, *_: (r, 0, 0)),
            ],
            out_specs=[
                by_row(width),
                pl.BlockSpec(attn_use.shape, lambda r, *_: (0, 0, 0)),
                pl.BlockSpec((16, width), lambda r, *_: (0, 0)),
            ],
            scratch_shapes=[
                pltpu.VMEM((length, LANES), bf16),
                pltpu.VMEM((length, width), bf16),
                pltpu.VMEM((length, LANES), bf16),
                pltpu.VMEM((length, width), bf16),
                pltpu.VMEM((length, width), bf16),
                pltpu.VMEM((length, width), f32),
                pltpu.VMEM((length, width), f32),
                pltpu.VMEM((length, width), bf16),
                pltpu.VMEM((length, 3 * width), bf16),
            ],
        ),
        out_shape=[
            jax.ShapeDtypeStruct((rows_all, width), f32),
            jax.ShapeDtypeStruct(attn_use.shape, f32),
            jax.ShapeDtypeStruct((16, width), f32),
        ],
        compiler_params=pltpu.CompilerParams(vmem_limit_bytes=VMEM_BYTES),
    )(starts, classes, counts, tokens, middle_grad, qkv, context, ext, attn_use, norm_w, images)


def mlp_kernel(
    middle_ref, out_grad_ref, w_ref, taps_ref, norm_ref, near_ref,
    output_ref, middle_grad_ref, w_grad_ref, taps_grad_ref, norm_grad_ref,
    normed_ref, hm_ref, h0_ref, hp_ref, act_ref, g_ref, gh_ref, tap_sum_ref,
):
    row = pl.program_id(0)
    length, width = middle_ref.shape
    hidden = w_ref.shape[2]
    chunk = 256
    block = 128
    sub = 32
    halo = GRID_W
    gain, bias = norm_ref[2:3, :], norm_ref[3:4, :]

    @pl.when(row == 0)
    def _():
        w_grad_ref[...] = jnp.zeros_like(w_grad_ref)
        norm_grad_ref[...] = jnp.zeros_like(norm_grad_ref)
        tap_sum_ref[...] = jnp.zeros_like(tap_sum_ref)
        for ref in (hm_ref, h0_ref, hp_ref, g_ref):
            ref[0:halo, :] = jnp.zeros((halo, hidden), bf16)
            ref[halo + length :, :] = jnp.zeros((halo, hidden), bf16)

    def normalize(step, carry):
        rows = pl.ds(pl.multiple_of(step * chunk, chunk), chunk)
        unit, _ = norm_parts(middle_ref[rows, :])
        normed_ref[rows, :] = (unit * gain + bias).astype(bf16)
        return carry

    lax.fori_loop(0, length // chunk, normalize, 0)
    column = lax.rem(lax.broadcasted_iota(jnp.int32, (block, LANES), 0), GRID_W)
    not_first = column != 0
    not_last = column != GRID_W - 1

    def expand(step, carry):
        c = step // (length // block)
        t = step - c * (length // block)
        rows = pl.ds(pl.multiple_of(t * block, block), block)
        place = pl.ds(pl.multiple_of(t * block + halo, GRID_W), block)
        values = dot(normed_ref[rows, :], w_ref[0, :, pl.ds(pl.multiple_of(c * chunk, chunk), chunk)])
        for part in range(chunk // LANES):
            lanes = pl.ds(pl.multiple_of(c * chunk + part * LANES, LANES), LANES)
            one = values[:, part * LANES : (part + 1) * LANES]
            h0_ref[place, lanes] = one.astype(bf16)
            hm_ref[place, lanes] = jnp.where(not_first, pltpu.roll(one, 1, 0), 0.0).astype(bf16)
            hp_ref[place, lanes] = jnp.where(not_last, pltpu.roll(one, block - 1, 0), 0.0).astype(bf16)
        return carry

    lax.fori_loop(0, (hidden // chunk) * (length // block), expand, 0)

    def tile_rows(values, rows):
        return jnp.concatenate([values] * (rows // GRID_W), axis=0)

    def activate(step, carry):
        c = step // (length // block)
        t = step - c * (length // block)
        rows = pl.ds(pl.multiple_of(t * block, block), block)
        act_grad = dot(out_grad_ref[rows, :], w_ref[1, :, pl.ds(pl.multiple_of(c * chunk, chunk), chunk)])
        for part in range(chunk // LANES):
            lanes = pl.ds(pl.multiple_of(c * chunk + part * LANES, LANES), LANES)
            taps = [tile_rows(taps_ref[k * GRID_W : (k + 1) * GRID_W, lanes], sub) for k in range(9)]
            for s in range(block // sub):
                base = t * block + s * sub
                near = pl.ds(pl.multiple_of(base, GRID_W), sub)
                mixed = None
                for a in (-1, 0, 1):
                    at = pl.ds(pl.multiple_of(base + halo + a * GRID_W, GRID_W), sub)
                    total = None
                    for b, ref in ((-1, hm_ref), (0, h0_ref), (1, hp_ref)):
                        term = ref[at, lanes] * taps[3 * (a + 1) + b + 1]
                        total = term if total is None else total + term
                    if a == 0:
                        total = total + h0_ref[at, lanes]
                    elif a == -1:
                        total = total * near_ref[0, near, :]
                    else:
                        total = total * near_ref[1, near, :]
                    mixed = total if mixed is None else mixed + total
                x = mixed.astype(f32)
                square = x * x
                t_value = jnp.tanh(x * (GELU_ONE + (GELU_ONE * GELU_TWO) * square))
                half = 0.5 * x
                act_ref[near, lanes] = (half + half * t_value).astype(bf16)
                slope = (0.5 + 0.5 * t_value) + half * (1.0 - t_value * t_value) * (
                    GELU_ONE + (3.0 * GELU_ONE * GELU_TWO) * square
                )
                grad = act_grad[s * sub : (s + 1) * sub, part * LANES : (part + 1) * LANES] * slope
                g_ref[pl.ds(pl.multiple_of(base + halo, GRID_W), sub), lanes] = grad.astype(bf16)
        return carry

    lax.fori_loop(0, (hidden // chunk) * (length // block), activate, 0)

    def conv_back(step, carry):
        c = step // (length // block)
        t = step - c * (length // block)
        lanes = pl.ds(pl.multiple_of(c * LANES, LANES), LANES)
        taps = [tile_rows(taps_ref[k * GRID_W : (k + 1) * GRID_W, lanes], sub) for k in range(9)]
        sums = [None] * 9
        col = lax.rem(lax.broadcasted_iota(jnp.int32, (sub, LANES), 0), GRID_W)
        for s in range(block // sub):
            base = t * block + s * sub
            near = pl.ds(pl.multiple_of(base, GRID_W), sub)
            at = pl.ds(pl.multiple_of(base + halo, GRID_W), sub)
            before = pl.ds(pl.multiple_of(base, GRID_W), sub)
            after = pl.ds(pl.multiple_of(base + 2 * halo, GRID_W), sub)
            here = g_ref[at, lanes]
            sources = (
                g_ref[after, lanes] * near_ref[1, near, :],
                here,
                g_ref[before, lanes] * near_ref[0, near, :],
            )
            side = {}
            for b, ref in ((-1, hm_ref), (0, h0_ref), (1, hp_ref)):
                moved = ref[at, lanes]
                total = None
                for a in (-1, 0, 1):
                    k = 3 * (a + 1) + b + 1
                    term = sources[a + 1] * taps[k]
                    total = term if total is None else total + term
                    product = moved * sources[a + 1]
                    folded = product[:GRID_W]
                    for piece in range(1, sub // GRID_W):
                        folded = folded + product[piece * GRID_W : (piece + 1) * GRID_W]
                    sums[k] = folded if sums[k] is None else sums[k] + folded
                side[b] = total
            result = (side[0] + here).astype(f32)
            result = result + jnp.where(col != 0, pltpu.roll(side[1].astype(f32), 1, 0), 0.0)
            result = result + jnp.where(col != GRID_W - 1, pltpu.roll(side[-1].astype(f32), sub - 1, 0), 0.0)
            gh_ref[near, lanes] = result.astype(bf16)
        for k in range(9):
            tap_sum_ref[k * GRID_W : (k + 1) * GRID_W, lanes] += sums[k].astype(f32)
        return carry

    lax.fori_loop(0, (hidden // LANES) * (length // block), conv_back, 0)

    def finish(step, carry):
        rows = pl.ds(pl.multiple_of(step * chunk, chunk), chunk)
        middle = middle_ref[rows, :]
        output_ref[rows, :] = (middle + dot(act_ref[rows, :], w_ref[1], NT)).astype(bf16)
        upstream = dot(gh_ref[rows, :], w_ref[0], NT)
        unit, inverse = norm_parts(middle)
        middle_grad_ref[rows, :] = out_grad_ref[rows, :].astype(f32) + norm_back(upstream, gain, unit, inverse)
        norm_grad_ref[0:8, :] += fold_rows(upstream * unit)
        norm_grad_ref[8:16, :] += fold_rows(upstream)
        return carry

    lax.fori_loop(0, length // chunk, finish, 0)
    normed_t = jnp.transpose(normed_ref[...])
    out_grad_t = jnp.transpose(out_grad_ref[...])

    def weights(c, carry):
        lanes = pl.ds(pl.multiple_of(c * chunk, chunk), chunk)
        w_grad_ref[0, :, lanes] += dot(normed_t, gh_ref[:, lanes])
        w_grad_ref[1, :, lanes] += dot(out_grad_t, act_ref[:, lanes])
        return carry

    lax.fori_loop(0, hidden // chunk, weights, 0)

    @pl.when(row == pl.num_programs(0) - 1)
    def _():
        taps_grad_ref[...] = jnp.zeros_like(taps_grad_ref)
        for k in range(9):
            taps_grad_ref[k : k + 1, :] = jnp.sum(tap_sum_ref[k * GRID_W : (k + 1) * GRID_W, :], axis=0, keepdims=True)


def mlp_layer(middle, out_grad, mlp_use, taps, norm_w, near, row_count):
    rows_all, width = middle.shape
    length = rows_all // row_count
    hidden = mlp_use.shape[2]
    by_row = lambda columns: pl.BlockSpec((length, columns), lambda r: (r, 0))
    return pl.pallas_call(
        mlp_kernel,
        grid=(row_count,),
        in_specs=[
            by_row(width),
            by_row(width),
            pl.BlockSpec(mlp_use.shape, lambda r: (0, 0, 0)),
            pl.BlockSpec(taps.shape, lambda r: (0, 0)),
            pl.BlockSpec(norm_w.shape, lambda r: (0, 0)),
            pl.BlockSpec((2, length, LANES), lambda r: (0, r, 0)),
        ],
        out_specs=[
            by_row(width),
            by_row(width),
            pl.BlockSpec(mlp_use.shape, lambda r: (0, 0, 0)),
            pl.BlockSpec((16, hidden), lambda r: (0, 0)),
            pl.BlockSpec((16, width), lambda r: (0, 0)),
        ],
        out_shape=[
            jax.ShapeDtypeStruct((rows_all, width), bf16),
            jax.ShapeDtypeStruct((rows_all, width), f32),
            jax.ShapeDtypeStruct(mlp_use.shape, f32),
            jax.ShapeDtypeStruct((16, hidden), f32),
            jax.ShapeDtypeStruct((16, width), f32),
        ],
        scratch_shapes=[
            pltpu.VMEM((length, width), bf16),
            pltpu.VMEM((length + 2 * GRID_W, hidden), bf16),
            pltpu.VMEM((length + 2 * GRID_W, hidden), bf16),
            pltpu.VMEM((length + 2 * GRID_W, hidden), bf16),
            pltpu.VMEM((length, hidden), bf16),
            pltpu.VMEM((length + 2 * GRID_W, hidden), bf16),
            pltpu.VMEM((length, hidden), bf16),
            pltpu.VMEM((9 * GRID_W, hidden), f32),
        ],
        compiler_params=pltpu.CompilerParams(vmem_limit_bytes=VMEM_BYTES),
    )(middle, out_grad, mlp_use, taps, norm_w, near)


def attention_plan(segments):
    row_count, length = segments.shape
    tiles = segments.reshape(row_count, length // TILE, TILE)
    first, last = tiles[:, :, 0], tiles[:, :, -1]
    low_end = jnp.sum((segments[:, None, :] < first[:, :, None]).astype(jnp.int32), axis=-1)
    high_end = jnp.sum((segments[:, None, :] <= last[:, :, None]).astype(jnp.int32), axis=-1)
    widths = widths_for(length)
    classes = sum(((high_end - low_end) > w).astype(jnp.int32) for w in widths[:-1])
    chosen = jnp.full_like(classes, widths[-1])
    for index, w in enumerate(widths):
        chosen = jnp.where(classes == index, w, chosen)
    starts = jnp.minimum(low_end, length - chosen)
    lane = jnp.arange(LANES, dtype=jnp.int32)
    begins = jnp.sum((segments[:, :, None] < lane).astype(jnp.int32), axis=1)
    ends = jnp.sum((segments[:, :, None] <= lane).astype(jnp.int32), axis=1)
    used = lane < IMAGES
    open_lane = (lane >= IMAGES) & (lane < IMAGES + 3 * 6)
    begins = jnp.where(used, begins, 0)
    ends = jnp.where(used, ends, jnp.where(open_lane, length, 0))
    images = jnp.zeros((row_count, 8, LANES), jnp.int32).at[:, 0].set(begins).at[:, 1].set(ends)
    return starts, classes, images


def neighbour_masks(segments):
    same = (segments[:, GRID_W:] == segments[:, :-GRID_W]).astype(bf16)
    zeros = jnp.zeros((segments.shape[0], GRID_W), bf16)
    above = jnp.concatenate([zeros, same], axis=1).reshape(-1)
    below = jnp.concatenate([same, zeros], axis=1).reshape(-1)
    return jnp.broadcast_to(jnp.stack([above, below])[:, :, None], (2, above.shape[0], LANES))


def bits_of(size):
    bits = []
    b = 1
    while b < size:
        bits.append(b)
        b *= 2
    return bits


def swap(values, axis, size, bit):
    return lax.ppermute(values, axis, [(i, i ^ bit) for i in range(size)])


def gather_lines(shard, size):
    place = lax.axis_index("dp")
    held = shard[None]
    for bit in reversed(bits_of(size)):
        other = swap(held, "dp", size, bit)
        mine_first = (place & bit) == 0
        pair = jnp.stack([jnp.where(mine_first, held, other), jnp.where(mine_first, other, held)], axis=1)
        held = pair.reshape((-1,) + shard.shape)
    return held


def join_columns(mine, other, rank):
    first = jnp.where(rank == 0, mine, other)
    second = jnp.where(rank == 0, other, mine)
    return jnp.concatenate([first, second], axis=-1)


def gather_weights(shard, size, rank):
    count, part, columns = shard.shape
    held = gather_lines(shard, size)
    full = join_columns(held, swap(held, "head", 2, 1), rank)
    return jnp.moveaxis(full, 0, 1).reshape(count, size * part, 2 * columns)


def own_columns(values, rank):
    half = values.shape[-1] // 2
    mine = lax.dynamic_slice_in_dim(values, rank * half, half, axis=values.ndim - 1)
    other = lax.dynamic_slice_in_dim(values, (1 - rank) * half, half, axis=values.ndim - 1)
    return mine + swap(other.astype(bf16), "head", 2, 1).astype(f32)


def scatter_lines(values, size):
    count, rows, columns = values.shape
    place = lax.axis_index("dp")
    held = jnp.moveaxis(values.reshape(count, size, rows // size, columns), 1, 0)
    for bit in bits_of(size):
        held = held.reshape((-1, 2) + held.shape[1:])
        side = (place & bit) // bit
        mine = lax.dynamic_index_in_dim(held, side, 1, keepdims=False)
        other = lax.dynamic_index_in_dim(held, 1 - side, 1, keepdims=False)
        held = mine + swap(other.astype(bf16), "dp", size, bit).astype(f32)
    return held[0]


def sum_everywhere(values, size):
    values = values + swap(values, "head", 2, 1)
    for bit in bits_of(size):
        values = values + swap(values, "dp", size, bit)
    return values


def adam_terms(grad_sum, first_old, second):
    first_new = BETA_ONE * first_old + (1.0 - BETA_ONE) * grad_sum
    second_new = BETA_TWO * second + (1.0 - BETA_TWO) * grad_sum * grad_sum
    direction = (
        first_new
        / (1.0 - BETA_ONE**STEP)
        / (jnp.sqrt(second_new / (1.0 - BETA_TWO**STEP)) + ADAM_EPS)
    )
    return (first_new, second_new, direction)


def body(
    size,
    tokens, grad_out, segments, counts,
    attn_w, attn_m, attn_v, mlp_w, mlp_m, mlp_v, conv_w, conv_m, conv_v, norm_w, norm_m, norm_v,
):
    rank = lax.axis_index("head")
    own_rows = segments.shape[0] // 2
    segments = lax.dynamic_slice_in_dim(segments, rank * own_rows, own_rows, axis=0)
    counts = lax.dynamic_slice_in_dim(counts, rank * own_rows, own_rows, axis=0)
    attn_use = gather_weights(attn_w.astype(bf16), size, rank)
    mlp_lines = lax.all_gather(mlp_w.astype(bf16), "dp", axis=1, tiled=True)
    mlp_use = join_columns(mlp_lines, swap(mlp_lines, "head", 2, 1), rank)
    conv_low = conv_w.astype(bf16)
    conv_use = join_columns(conv_low, swap(conv_low, "head", 2, 1), rank)
    starts, classes, images = attention_plan(segments)
    middle, qkv, context, ext = attn_forward(starts, classes, counts, tokens, attn_use, norm_w, images)
    output, grad_middle, grad_mlp, grad_conv, grad_norm_two = mlp_layer(
        middle, grad_out, mlp_use, jnp.repeat(conv_use, GRID_W, axis=0), norm_w, neighbour_masks(segments), own_rows
    )
    grad_tokens, grad_attn, grad_norm_one = attn_backward(
        starts, classes, counts, tokens, grad_middle, qkv, context, ext, attn_use, norm_w, images
    )
    grad_mlp = scatter_lines(own_columns(grad_mlp, rank), size)
    grad_conv = own_columns(grad_conv[:9], rank)
    for bit in bits_of(size):
        grad_conv = grad_conv + swap(grad_conv, "dp", size, bit)
    grad_attn = scatter_lines(own_columns(grad_attn, rank), size)
    new_attn_m, new_attn_v, attn_direction = adam_terms(grad_attn, attn_m, attn_v)
    new_mlp_m, new_mlp_v, mlp_direction = adam_terms(grad_mlp, mlp_m, mlp_v)
    new_conv_m, new_conv_v, conv_direction = adam_terms(grad_conv, conv_m, conv_v)
    attn_update = attn_direction + DECAY * attn_w
    mlp_update = mlp_direction + DECAY * mlp_w
    conv_update = conv_direction + DECAY * conv_w
    first_line = (lax.axis_index("dp") == 0).astype(f32)
    weight_squares = jnp.concatenate(
        [
            jnp.sum(attn_w * attn_w, axis=(1, 2)),
            jnp.sum(mlp_w * mlp_w, axis=(1, 2)),
            (first_line * jnp.sum(conv_w * conv_w))[None],
        ]
    )
    update_squares = jnp.concatenate(
        [
            jnp.sum(attn_update * attn_update, axis=(1, 2)),
            jnp.sum(mlp_update * mlp_update, axis=(1, 2)),
            (first_line * jnp.sum(conv_update * conv_update))[None],
        ]
    )
    width = norm_w.shape[1]
    norm_part = jnp.concatenate(
        [
            jnp.sum(grad_norm_one.reshape(2, 8, width), axis=1),
            jnp.sum(grad_norm_two.reshape(2, 8, width), axis=1),
        ]
    )
    squares = jnp.pad(jnp.stack([weight_squares, update_squares]), ((0, 0), (0, width - 7)))
    summed = sum_everywhere(jnp.concatenate([squares, norm_part, jnp.zeros((2, width), f32)]), size)
    squares, norm_grads = summed[:2, :7], summed[2:6]
    ratio = jnp.sqrt(squares[0]) / jnp.sqrt(squares[1])
    new_attn_w = attn_w - RATE * ratio[:4, None, None] * attn_update
    new_mlp_w = mlp_w - RATE * ratio[4:6, None, None] * mlp_update
    new_conv_w = conv_w - RATE * ratio[6] * conv_update
    new_norm_m, new_norm_v, norm_direction = adam_terms(norm_grads, norm_m, norm_v)
    new_norm_w = norm_w - RATE * norm_direction
    return (
        output, grad_tokens, new_attn_w, new_attn_m, new_attn_v, new_mlp_w, new_mlp_m, new_mlp_v,
        new_conv_w, new_conv_m, new_conv_v, new_norm_w, new_norm_m, new_norm_v,
    )


def solution(mesh):
    rows, lines = P(("dp", "head"), None), P("dp", None)
    shards, columns = P(None, "dp", "head"), P(None, "head")
    in_specs = (rows, rows, lines, P("dp")) + (shards,) * 6 + (columns,) * 3 + (P(),) * 3
    out_specs = (rows, rows) + (shards,) * 6 + (columns,) * 3 + (P(),) * 3
    return jax.shard_map(
        functools.partial(body, mesh.shape["dp"]), mesh=mesh, in_specs=in_specs, out_specs=out_specs, check_vma=False
    )
```

time: 1200 us -> 425 us (0.35)
  other arithmetic: 435 us -> 19.8 us
  matrix products: 337 us -> 0 us
  Pallas kernels: 0 us -> 249 us
  blocking collectives: 166 us -> 0 us
  local copies, waits for them, and re-layouts: 152 us -> 15.9 us
  starting transfers between devices: 0.47 us -> 24.9 us
  waiting for transfers between devices: 77.6 us -> 97.5 us
    dot_general x53 -> x0, matrix products: 328 us -> none  [the longest x1 70 us: body(): jnp.einsum('td,df->tf', grad_rows_all, mlp_full[1], preferred_element_typ...]
    pallas_call x0 -> x3, Pallas kernels: none -> 249 us  [the longest x1 141 us: mlp_layer(): pl.pallas_call(mlp_kernel, grid=(row_count,), in_specs=[by_row(width), by...]
    convert_element_type x18 -> x3, other arithmetic: 189 us -> 3.28 us  [the longest x1 1.55 us: body(): mlp_lines = lax.all_gather(mlp_w.astype(bf16), 'dp', axis=1, tiled=True)]
    mul x8 -> x0, other arithmetic: 169 us -> none  [depthwise(): tap_weights[tap_index] * tap_mask[tap_index][:, :, None]]
    psum x2 -> x0, blocking collectives: 119 us -> none  [the longest x1 78.1 us: body(): grad_conv = lax.psum(grad_conv, 'dp')]
    ppermute x0 -> x27, waiting for transfers between devices: none -> 69.8 us  [swap(): return lax.ppermute(values, axis, [(i, i ^ bit) for i in range(size)])]
    slice x11 -> x1, local copies, waits for them, and re-layouts: 55.7 us -> 0.25 us  [attention_plan(): first, last = (tiles[:, :, 0], tiles[:, :, -1])]
    reduce_scatter x5 -> x0, waiting for transfers between devices: 52.6 us -> none  [the longest x1 16.5 us: body(): lax.psum_scatter(jnp.einsum('tke,kde->td', piece, attn_full[:3], preferre...]
  transfers between devices with their start and end apart: 11 -> 28, of which waited for: 5 -> 19; matrix products, arithmetic and copies ran while one was open for 40% -> 6% of each run, Pallas kernels for 0% -> 25%
where the time goes in v1:
time: 425 us; the launch traced here: 424 us
  Pallas kernels  249 us (59%)
  waiting for transfers between devices  97.5 us (23%)
  starting transfers between devices  24.9 us (6%)
  other arithmetic  19.8 us (5%)
  between operations  16.6 us (4%)
  local copies, waits for them, and re-layouts  15.9 us (4%)
    pallas_call x1, Pallas kernels, mlp_layer(): pl.pallas_call(mlp_kernel, grid=(row_count,), in_specs=[by_row(width), by...  141 us
    ppermute x27, waiting for transfers between devices, swap(): return lax.ppermute(values, axis, [(i, i ^ bit) for i in range(size)])  69.8 us
    pallas_call x1, Pallas kernels, attn_backward(): pl.pallas_call(attn_backward_kernel, grid_spec=pltpu.PrefetchScalarGridSp...  59.4 us
    pallas_call x1, Pallas kernels, attn_forward(): pl.pallas_call(attn_forward_kernel, grid_spec=pltpu.PrefetchScalarGridSpe...  48.3 us
    all_gather x1, waiting for transfers between devices, body(): mlp_lines = lax.all_gather(mlp_w.astype(bf16), 'dp', axis=1, tiled=True)  27.7 us
    ppermute x27, starting transfers between devices, swap(): return lax.ppermute(values, axis, [(i, i ^ bit) for i in range(size)])  24.9 us
  transfers between devices with their start and end apart: 28, of which 19 were waited for; matrix products, arithmetic and copies ran while one was open for 6% of the time, Pallas kernels for 25%

profile of v1, /device:TPU:0, one launch (start us, length us, event | category | flops | bytes accessed | tf_op | source)
XLA Modules:
  0.0 423.8 jit_solution(8337125958328893462)
XLA Ops:
  7.2 0.9 convert_bitcast_fusion
  8.1 4.0 collective-permute-start
  12.2 1.6 convert_element_type.136
  16.3 0.9 fusion.11
  18.2 0.9 select_bitcast_fusion.7
  19.2 1.6 collective-permute-start.1
  20.8 3.6 collective-permute-done.1
  24.5 1.6 collective-permute-start.2
  26.7 4.4 %collective-permute-done.2 = bf16[4,4,24,192]{3,2,1,0:T(8,128)(2,1)S(1)} collective-permute-done((bf16[4,4,24,192]{3,2,1,0:T(8,128)(2,1)S(1)}, bf16[4,4,24,192]{3,2,1,0:T(8,128)(2,1)S(1)}, u32[]{:S(2)}, u32[]{:S(2)}) %collective-permute-start.2) | collective-permute-done | bytes 147488 | tf_op jit(solution)/shard_map/ppermute | solution.py:611
  31.3 1.6 collective-permute-start.3
  32.9 9.6 %collective-permute-done.3 = bf16[8,4,24,192]{3,2,1,0:T(8,128)(2,1)S(1)} collective-permute-done((bf16[8,4,24,192]{3,2,1,0:T(8,128)(2,1)S(1)}, bf16[8,4,24,192]{3,2,1,0:T(8,128)(2,1)S(1)}, u32[]{:S(2)}, u32[]{:S(2)}) %collective-permute-start.3) | collective-permute-done | bytes 294944 | tf_op jit(solution)/shard_map/ppermute | solution.py:611
  42.5 27.7 %all-gather.2.cloned.1.call-done = bf16[2,384,768]{2,1,0:T(8,128)(2,1)} async-done(((bf16[2,24,768]{2,1,0:T(8,128)(2,1)}), bf16[2,384,768]{2,1,0:T(8,128)(2,1)}) %all-gather.2.cloned.1.call-update) | async-done | bytes 1179664 | tf_op jit(solution)/shard_map/all_gather | solution.py:686
  71.7 2.5 collective-permute-done.4
  74.8 1.1 copy.61
  75.9 48.3 %shard_map.263 = (f32[3072,384]{1,0:T(8,128)}, bf16[3072,1152]{1,0:T(8,128)(2,1)}, bf16[3072,384]{1,0:T(8,128)(2,1)}, bf16[3072,128]{1,0:T(8,128)(2,1)}) custom-call(s32[3,8]{1,0:T(4,128)} %get-tuple-element.100.start_ref, s32[3,8]{1,0:T(4,128)} %get-tuple-element.99.class_ref, s32[3]{0:T(128)} %dynamic_slice.73.count_ref, bf16[3072,384]{1,0:T(8,128)(2,1)} %tokens_ref.3, ...), custom_call_target="tpu_custom_call" | custom-call | tf_op jit(solution)/shard_map/pallas_call | solution.py:170
  124.4 1.6 pad_maximum_fusion.w_ref
  126.0 1.9 broadcast_in_dim.68.near_ref
  128.7 141.4 %shard_map.264 = (bf16[3072,384]{1,0:T(8,128)(2,1)}, f32[3072,384]{1,0:T(8,128)}, f32[2,384,1536]{2,1,0:T(8,128)}, f32[16,1536]{1,0:T(8,128)}, f32[16,384]{1,0:T(8,128)}) custom-call(f32[3072,384]{1,0:T(8,128)} %get-tuple-element.50.middle_ref, bf16[3072,384]{1,0:T(8,128)(2,1)} %out_grad_ref.1, bf16[2,384,1536]{2,1,0:T(8,128)(2,1)} %pad_maximum_fusion.w_ref, ...), custom_call_target="tpu_custom_call" | custom-call | tf_op jit(solution)/shard_map/pallas_call | solution.py:531
  270.1 2.9 dynamic-slice_convert_fusion
  273.0 59.4 %shard_map.265 = (f32[3072,384]{1,0:T(8,128)}, f32[4,384,384]{2,1,0:T(8,128)}, f32[16,384]{1,0:T(8,128)}) custom-call(s32[3,8]{1,0:T(4,128)} %get-tuple-element.100.start_ref, s32[3,8]{1,0:T(4,128)} %get-tuple-element.99.class_ref, s32[3]{0:T(128)} %dynamic_slice.73.count_ref, bf16[3072,384]{1,0:T(8,128)(2,1)} %tokens_ref.3, ...), custom_call_target="tpu_custom_call" | custom-call | tf_op jit(solution)/shard_map/pallas_call | solution.py:320
  332.4 1.8 dynamic-slice_convert_fusion.1
  334.2 1.1 copy.62
  335.9 1.5 collective-permute-done.17
  337.6 3.9 collective-permute-done.18
  341.5 2.1 collective-permute-start.19
  343.7 2.0 collective-permute-done.19
  345.8 4.0 collective-permute-done.20
  350.6 1.3 copy.63
  353.6 1.9 collective-permute-start.8
  355.5 2.3 convert_add_fusion
  358.6 1.5 multiply_reduce_fusion.5
  361.4 4.4 %collective-permute-done.8 = bf16[8,4,24,192]{3,2,1,0:T(8,128)(2,1)S(1)} collective-permute-done((bf16[8,4,24,192]{3,2,1,0:T(8,128)(2,1)}, bf16[8,4,24,192]{3,2,1,0:T(8,128)(2,1)S(1)}, u32[]{:S(2)}, u32[]{:S(2)}) %collective-permute-start.8) | collective-permute-done | bytes 294944 | tf_op jit(solution)/shard_map/ppermute | solution.py:611
  365.8 1.2 bitcast_add_fusion.1
  367.1 1.4 collective-permute-start.9
  368.5 6.6 %collective-permute-done.13 = bf16[8,2,24,768]{3,2,1,0:T(8,128)(2,1)} collective-permute-done((bf16[8,2,24,768]{3,2,1,0:T(8,128)(2,1)S(1)}, bf16[8,2,24,768]{3,2,1,0:T(8,128)(2,1)}, u32[]{:S(2)}, u32[]{:S(2)}) %collective-permute-start.13) | collective-permute-done | bytes 589856 | tf_op jit(solution)/shard_map/ppermute | solution.py:611
  375.1 1.2 bitcast_add_fusion
  377.0 1.6 collective-permute-start.10
  378.6 4.5 %collective-permute-done.14 = bf16[4,2,24,768]{3,2,1,0:T(8,128)(2,1)S(1)} collective-permute-done((bf16[4,2,24,768]{3,2,1,0:T(8,128)(2,1)S(1)}, bf16[4,2,24,768]{3,2,1,0:T(8,128)(2,1)S(1)}, u32[]{:S(2)}, u32[]{:S(2)}) %collective-permute-start.14) | collective-permute-done | bytes 294944 | tf_op jit(solution)/shard_map/ppermute | solution.py:611
  383.3 1.8 collective-permute-start.15
  385.5 3.7 collective-permute-done.15
  389.3 1.5 collective-permute-start.16
  391.0 4.4 %collective-permute-done.16 = bf16[1,2,24,768]{3,2,1,0:T(8,128)(2,1)S(1)} collective-permute-done((bf16[1,2,24,768]{3,2,1,0:T(8,128)(2,1)S(1)}, bf16[1,2,24,768]{3,2,1,0:T(8,128)(2,1)S(1)}, u32[]{:S(2)}, u32[]{:S(2)}) %collective-permute-start.16) | collective-permute-done | bytes 73760 | tf_op jit(solution)/shard_map/ppermute | solution.py:611
  395.8 1.2 collective-permute-done.22
  397.1 1.2 collective-permute-start.23
  398.2 2.5 collective-permute-done.23
  400.8 3.7 collective-permute-done.24
  404.8 3.4 collective-permute-done.25
  409.0 3.8 collective-permute-done.26
  (154 shorter events, 18.1 us)
Async XLA Ops:
  7.2 63.0 %all-gather.2.cloned.1.call-start = ((), (), s32[]{:S(2)}) async-start(), calls=%async_computation | async-start | bytes 1253376 | tf_op jit(solution)/shard_map/all_gather | solution.py:686
  8.1 10.1 %collective-permute-start = (bf16[1,4,24,192]{3,2,1,0:T(8,128)(2,1)S(1)}, bf16[1,4,24,192]{3,2,1,0:T(8,128)(2,1)S(1)}, u32[]{:S(2)}, u32[]{:S(2)}) collective-permute-start(bf16[1,4,24,192]{3,2,1,0:T(8,128)(2,1)S(1)} %convert_bitcast_fusion), channel_id=1, source_target_pairs={{0,16},{2,18},{4,20},{6,22},{8,24},{10,26},{12,28},{14,30},{16,0},... | collective-permute-start | bytes 110600 | tf_op jit(solution)/shard_map/ppermute | solution.py:611
  14.5 57.1 %collective-permute-start.6 = (bf16[9,768]{1,0:T(8,128)(2,1)S(1)}, bf16[9,768]{1,0:T(8,128)(2,1)S(1)}, u32[]{:S(2)}, u32[]{:S(2)}) collective-permute-start(bf16[9,768]{1,0:T(8,128)(2,1)S(1)} %convert_element_type.137), channel_id=1, source_target_pairs={{0,1},{1,0},{2,3},{3,2},{4,5},{5,4},{6,7},{7,6},{8,9},{9,8},{10,11... | collective-permute-start | bytes 41480 | tf_op jit(solution)/shard_map/ppermute | solution.py:611
  19.2 5.3 %collective-permute-start.1 = (bf16[2,4,24,192]{3,2,1,0:T(8,128)(2,1)S(1)}, bf16[2,4,24,192]{3,2,1,0:T(8,128)(2,1)S(1)}, u32[]{:S(2)}, u32[]{:S(2)}) collective-permute-start(bf16[2,4,24,192]{3,2,1,0:T(8,128)(2,1)S(1)} %maximum_bitcast_fusion.1), channel_id=1, source_target_pairs={{0,8},{2,10},{4,12},{6,14},{8,0},{10,2},{12,4},{14,6},{16,24},{18,... | collective-permute-start | bytes 221192 | tf_op jit(solution)/shard_map/ppermute | solution.py:611
  24.5 6.6 %collective-permute-start.2 = (bf16[4,4,24,192]{3,2,1,0:T(8,128)(2,1)S(1)}, bf16[4,4,24,192]{3,2,1,0:T(8,128)(2,1)S(1)}, u32[]{:S(2)}, u32[]{:S(2)}) collective-permute-start(bf16[4,4,24,192]{3,2,1,0:T(8,128)(2,1)S(1)} %bitcast.139), channel_id=1, source_target_pairs={{0,4},{2,6},{4,0},{6,2},{8,12},{10,14},{12,8},{14,10},{16,20},{18,... | collective-permute-start | bytes 442376 | tf_op jit(solution)/shard_map/ppermute | solution.py:611
  31.3 11.1 %collective-permute-start.3 = (bf16[8,4,24,192]{3,2,1,0:T(8,128)(2,1)S(1)}, bf16[8,4,24,192]{3,2,1,0:T(8,128)(2,1)S(1)}, u32[]{:S(2)}, u32[]{:S(2)}) collective-permute-start(bf16[8,4,24,192]{3,2,1,0:T(8,128)(2,1)S(1)} %bitcast.136), channel_id=1, source_target_pairs={{0,2},{2,0},{4,6},{6,4},{8,10},{10,8},{12,14},{14,12},{16,18},{18,... | collective-permute-start | bytes 884744 | tf_op jit(solution)/shard_map/ppermute | solution.py:611
  70.2 54.1 %collective-permute-start.5 = (bf16[2,384,768]{2,1,0:T(8,128)(2,1)}, bf16[2,384,768]{2,1,0:T(8,128)(2,1)S(1)}, u32[]{:S(2)}, u32[]{:S(2)}) collective-permute-start(bf16[2,384,768]{2,1,0:T(8,128)(2,1)} %all-gather.2.cloned.1.call-done), channel_id=1, source_target_pairs={{0,1},{1,0},{2,3},{3,2},{4,5},{5,4},{6,7},{7,6},{8,9},{9,8},{10,11... | collective-permute-start | bytes 3538952 | tf_op jit(solution)/shard_map/ppermute | solution.py:611
  70.4 3.7 collective-permute-start.4
  75.9 48.3 %copy-start.4 = (bf16[2,384,768]{2,1,0:T(8,128)(2,1)S(1)}, bf16[2,384,768]{2,1,0:T(8,128)(2,1)}, u32[]{:S(2)}) copy-start(bf16[2,384,768]{2,1,0:T(8,128)(2,1)} %all-gather.2.cloned.1.call-done) | copy-start | bytes 3538948
  273.0 82.4 %collective-permute-start.12 = (bf16[2,384,768]{2,1,0:T(8,128)(2,1)}, bf16[2,384,768]{2,1,0:T(8,128)(2,1)}, u32[]{:S(2)}, u32[]{:S(2)}) collective-permute-start(bf16[2,384,768]{2,1,0:T(8,128)(2,1)} %dynamic-slice_convert_fusion), channel_id=1, source_target_pairs={{0,1},{1,0},{2,3},{3,2},{4,5},{5,4},{6,7},{7,6},{8,9},{9,8},{10,11... | collective-permute-start | bytes 3538952 | tf_op jit(solution)/shard_map/ppermute | solution.py:611
  332.4 3.0 copy-start.18
  332.4 11.2 %copy-start.22 = (f32[16,384]{1,0:T(8,128)S(1)}, f32[16,384]{1,0:T(8,128)}, u32[]{:S(2)}) copy-start(f32[16,384]{1,0:T(8,128)} %get-tuple-element.60) | copy-start | bytes 73732
  332.4 13.4 %copy-start.21 = (f32[16,384]{1,0:T(8,128)S(1)}, f32[16,384]{1,0:T(8,128)}, u32[]{:S(2)}) copy-start(f32[16,384]{1,0:T(8,128)} %get-tuple-element.61) | copy-start | bytes 73732
  334.2 17.8 %copy-start.1 = (f32[4,384,384]{2,1,0:T(8,128)S(1)}, f32[4,384,384]{2,1,0:T(8,128)}, u32[]{:S(2)}) copy-start(f32[4,384,384]{2,1,0:T(8,128)} %get-tuple-element.57) | copy-start | bytes 7077892
  335.4 15.3 %collective-permute-start.7 = (bf16[4,384,192]{1,2,0:T(8,128)(2,1)}, bf16[4,384,192]{1,2,0:T(8,128)(2,1)}, u32[]{:S(2)}, u32[]{:S(2)}) collective-permute-start(bf16[4,384,192]{1,2,0:T(8,128)(2,1)} %copy.62), channel_id=1, source_target_pairs={{0,1},{1,0},{2,3},{3,2},{4,5},{5,4},{6,7},{7,6},{8,9},{9,8},{10,11... | collective-permute-start | bytes 1769480 | tf_op jit(solution)/shard_map/ppermute | solution.py:611
  335.4 2.0 collective-permute-start.17
  337.4 4.2 collective-permute-start.18
  341.5 4.2 collective-permute-start.19
  345.7 4.2 collective-permute-start.20
  349.9 8.7 %collective-permute-start.21 = (f32[9,768]{1,0:T(8,128)S(1)}, f32[9,768]{1,0:T(8,128)}, u32[]{:S(2)}, u32[]{:S(2)}) collective-permute-start(f32[9,768]{1,0:T(8,128)S(1)} %add.243), channel_id=1, source_target_pairs={{0,16},{2,18},{4,20},{6,22},{8,24},{10,26},{12,28},{14,30},{16,0},... | collective-permute-start | bytes 82952 | tf_op jit(solution)/shard_map/ppermute | solution.py:611
  353.6 12.3 %collective-permute-start.8 = (bf16[8,4,24,192]{3,2,1,0:T(8,128)(2,1)}, bf16[8,4,24,192]{3,2,1,0:T(8,128)(2,1)S(1)}, u32[]{:S(2)}, u32[]{:S(2)}) collective-permute-start(bf16[8,4,24,192]{3,2,1,0:T(8,128)(2,1)} %fusion.1), channel_id=1, source_target_pairs={{0,2},{2,0},{4,6},{6,4},{8,10},{10,8},{12,14},{14,12},{16,18},{18,... | collective-permute-start | bytes 884744 | tf_op jit(solution)/shard_map/ppermute | solution.py:611
  358.1 16.9 %collective-permute-start.13 = (bf16[8,2,24,768]{3,2,1,0:T(8,128)(2,1)S(1)}, bf16[8,2,24,768]{3,2,1,0:T(8,128)(2,1)}, u32[]{:S(2)}, u32[]{:S(2)}) collective-permute-start(bf16[8,2,24,768]{3,2,1,0:T(8,128)(2,1)S(1)} %fusion), channel_id=1, source_target_pairs={{0,2},{2,0},{4,6},{6,4},{8,10},{10,8},{12,14},{14,12},{16,18},{18,... | collective-permute-start | bytes 1769480 | tf_op jit(solution)/shard_map/ppermute | solution.py:611
  360.1 54.7 %copy-start.10 = (f32[9,768]{1,0:T(8,128)}, f32[9,768]{1,0:T(8,128)S(1)}, u32[]{:S(2)}) copy-start(f32[9,768]{1,0:T(8,128)S(1)} %get-tuple-element.81) | copy-start | bytes 82948
  360.1 54.7 %copy-start.11 = (f32[9,768]{1,0:T(8,128)}, f32[9,768]{1,0:T(8,128)S(1)}, u32[]{:S(2)}) copy-start(f32[9,768]{1,0:T(8,128)S(1)} %get-tuple-element.82) | copy-start | bytes 82948
  367.1 9.8 %collective-permute-start.9 = (bf16[4,4,24,192]{3,2,1,0:T(8,128)(2,1)S(1)}, bf16[4,4,24,192]{3,2,1,0:T(8,128)(2,1)S(1)}, u32[]{:S(2)}, u32[]{:S(2)}) collective-permute-start(bf16[4,4,24,192]{3,2,1,0:T(8,128)(2,1)S(1)} %fusion.3), channel_id=1, source_target_pairs={{0,4},{2,6},{4,0},{6,2},{8,12},{10,14},{12,8},{14,10},{16,20},{18,... | collective-permute-start | bytes 442376 | tf_op jit(solution)/shard_map/ppermute | solution.py:611
  376.3 6.8 %collective-permute-start.14 = (bf16[4,2,24,768]{3,2,1,0:T(8,128)(2,1)S(1)}, bf16[4,2,24,768]{3,2,1,0:T(8,128)(2,1)S(1)}, u32[]{:S(2)}, u32[]{:S(2)}) collective-permute-start(bf16[4,2,24,768]{3,2,1,0:T(8,128)(2,1)S(1)} %fusion.2), channel_id=1, source_target_pairs={{0,4},{2,6},{4,0},{6,2},{8,12},{10,14},{12,8},{14,10},{16,20},{18,... | collective-permute-start | bytes 884744 | tf_op jit(solution)/shard_map/ppermute | solution.py:611
  376.9 13.8 %copy-start.2 = (f32[4,24,192]{2,1,0:T(8,128)S(1)}, f32[4,24,192]{2,1,0:T(8,128)}, u32[]{:S(2)}) copy-start(f32[4,24,192]{2,1,0:T(8,128)} %param.24) | copy-start | bytes 221188
  376.9 13.8 %copy-start.16 = (f32[4,24,192]{2,1,0:T(8,128)S(1)}, f32[4,24,192]{2,1,0:T(8,128)}, u32[]{:S(2)}) copy-start(f32[4,24,192]{2,1,0:T(8,128)} %param.25) | copy-start | bytes 221188
  377.0 13.8 %copy-start.17 = (f32[4,24,192]{2,1,0:T(8,128)S(1)}, f32[4,24,192]{2,1,0:T(8,128)}, u32[]{:S(2)}) copy-start(f32[4,24,192]{2,1,0:T(8,128)} %param.26) | copy-start | bytes 221188
  377.0 8.1 %collective-permute-start.10 = (bf16[2,4,24,192]{3,2,1,0:T(8,128)(2,1)S(1)}, bf16[2,4,24,192]{3,2,1,0:T(8,128)(2,1)S(1)}, u32[]{:S(2)}, u32[]{:S(2)}) collective-permute-start(bf16[2,4,24,192]{3,2,1,0:T(8,128)(2,1)S(1)} %fusion.8), channel_id=1, source_target_pairs={{0,8},{2,10},{4,12},{6,14},{8,0},{10,2},{12,4},{14,6},{16,24},{18,... | collective-permute-start | bytes 221192 | tf_op jit(solution)/shard_map/ppermute | solution.py:611
  383.2 12.2 %copy-start.3 = (f32[2,24,768]{2,1,0:T(8,128)S(1)}, f32[2,24,768]{2,1,0:T(8,128)}, u32[]{:S(2)}) copy-start(f32[2,24,768]{2,1,0:T(8,128)} %param.27) | copy-start | bytes 442372
  383.2 12.2 %copy-start.12 = (f32[2,24,768]{2,1,0:T(8,128)S(1)}, f32[2,24,768]{2,1,0:T(8,128)}, u32[]{:S(2)}) copy-start(f32[2,24,768]{2,1,0:T(8,128)} %param.28) | copy-start | bytes 442372
  383.2 12.2 %copy-start.13 = (f32[2,24,768]{2,1,0:T(8,128)S(1)}, f32[2,24,768]{2,1,0:T(8,128)}, u32[]{:S(2)}) copy-start(f32[2,24,768]{2,1,0:T(8,128)} %param.29) | copy-start | bytes 442372
  383.2 30.9 %copy-start.15 = (f32[4,384]{1,0:T(4,128)S(1)}, f32[4,384]{1,0:T(4,128)}, u32[]{:S(2)}) copy-start(f32[4,384]{1,0:T(4,128)} %norm_ref.5) | copy-start | bytes 18436
  383.3 30.9 %copy-start.23 = (f32[4,384]{1,0:T(4,128)S(1)}, f32[4,384]{1,0:T(4,128)}, u32[]{:S(2)}) copy-start(f32[4,384]{1,0:T(4,128)} %param.34) | copy-start | bytes 18436
  383.3 30.9 %copy-start.24 = (f32[4,384]{1,0:T(4,128)S(1)}, f32[4,384]{1,0:T(4,128)}, u32[]{:S(2)}) copy-start(f32[4,384]{1,0:T(4,128)} %param.35) | copy-start | bytes 18436
  383.3 5.9 %collective-permute-start.15 = (bf16[2,2,24,768]{3,2,1,0:T(8,128)(2,1)S(1)}, bf16[2,2,24,768]{3,2,1,0:T(8,128)(2,1)S(1)}, u32[]{:S(2)}, u32[]{:S(2)}) collective-permute-start(bf16[2,2,24,768]{3,2,1,0:T(8,128)(2,1)S(1)} %fusion.5), channel_id=1, source_target_pairs={{0,8},{2,10},{4,12},{6,14},{8,0},{10,2},{12,4},{14,6},{16,24},{18,... | collective-permute-start | bytes 442376 | tf_op jit(solution)/shard_map/ppermute | solution.py:611
  385.1 5.6 %collective-permute-start.11 = (bf16[1,4,24,192]{3,2,1,0:T(8,128)(2,1)S(1)}, bf16[1,4,24,192]{3,2,1,0:T(8,128)(2,1)S(1)}, u32[]{:S(2)}, u32[]{:S(2)}) collective-permute-start(bf16[1,4,24,192]{3,2,1,0:T(8,128)(2,1)S(1)} %dynamic-slice_convert_fusion.9), channel_id=1, source_target_pairs={{0,16},{2,18},{4,20},{6,22},{8,24},{10,26},{12,28},{14,30},{16,0},... | collective-permute-start | bytes 110600 | tf_op jit(solution)/shard_map/ppermute | solution.py:611
  389.3 6.1 %collective-permute-start.16 = (bf16[1,2,24,768]{3,2,1,0:T(8,128)(2,1)S(1)}, bf16[1,2,24,768]{3,2,1,0:T(8,128)(2,1)S(1)}, u32[]{:S(2)}, u32[]{:S(2)}) collective-permute-start(bf16[1,2,24,768]{3,2,1,0:T(8,128)(2,1)S(1)} %dynamic-slice_convert_fusion.8), channel_id=1, source_target_pairs={{0,16},{2,18},{4,20},{6,22},{8,24},{10,26},{12,28},{14,30},{16,0},... | collective-permute-start | bytes 221192 | tf_op jit(solution)/shard_map/ppermute | solution.py:611
  391.0 25.9 %copy-start.8 = (f32[4,24,192]{2,1,0:T(8,128)}, f32[4,24,192]{2,1,0:T(8,128)S(1)}, u32[]{:S(2)}) copy-start(f32[4,24,192]{2,1,0:T(8,128)S(1)} %get-tuple-element.77) | copy-start | bytes 221188
  391.0 25.9 %copy-start.9 = (f32[4,24,192]{2,1,0:T(8,128)}, f32[4,24,192]{2,1,0:T(8,128)S(1)}, u32[]{:S(2)}) copy-start(f32[4,24,192]{2,1,0:T(8,128)S(1)} %get-tuple-element.78) | copy-start | bytes 221188
  395.6 21.3 %copy-start.6 = (f32[2,24,768]{2,1,0:T(8,128)}, f32[2,24,768]{2,1,0:T(8,128)S(1)}, u32[]{:S(2)}) copy-start(f32[2,24,768]{2,1,0:T(8,128)S(1)} %get-tuple-element.79) | copy-start | bytes 442372
  395.6 21.3 %copy-start.7 = (f32[2,24,768]{2,1,0:T(8,128)}, f32[2,24,768]{2,1,0:T(8,128)S(1)}, u32[]{:S(2)}) copy-start(f32[2,24,768]{2,1,0:T(8,128)S(1)} %get-tuple-element.80) | copy-start | bytes 442372
  395.8 1.2 collective-permute-start.22
  397.1 3.7 collective-permute-start.23
  400.8 3.7 collective-permute-start.24
  404.5 3.7 collective-permute-start.25
  408.2 4.6 %collective-permute-start.26 = (f32[8,384]{1,0:T(8,128)S(1)}, f32[8,384]{1,0:T(8,128)S(1)}, u32[]{:S(2)}, u32[]{:S(2)}) collective-permute-start(f32[8,384]{1,0:T(8,128)S(1)} %add.253), channel_id=1, source_target_pairs={{0,16},{2,18},{4,20},{6,22},{8,24},{10,26},{12,28},{14,30},{16,0},... | collective-permute-start | bytes 36872 | tf_op jit(solution)/shard_map/ppermute | solution.py:611
  (6 other events, 9.5 us)
Sparse Core Ops, SparseCore 0:
  13.9 56.2 all-gather.1

commit v2 on v1

--- a/solution.py
+++ b/solution.py
@@ -22,8 +22,14 @@
 BIG = 2.0**100
 GELU_ONE = 0.7978845608028654
 GELU_TWO = 0.044715
+GELU_S = (GELU_ONE * GELU_TWO) ** (1.0 / 3.0)
+GELU_A = GELU_ONE / GELU_S
+ACT_SCALE = 0.5 / GELU_S
+MXU_ROWS = 64
+MXU_LAG = 6
 TILE = 128
 LANES = 128
+STRIDE = GRID_W + 8
 VMEM_BYTES = 60 * 1024 * 1024
 
 f32 = jnp.float32
@@ -192,11 +198,28 @@
 
 
 def attn_backward_kernel(
-    start_ref, class_ref, count_ref, tokens_ref, middle_grad_ref, qkv_ref, context_ref, ext_ref, w_ref, norm_ref, image_ref,
+    first, start_ref, class_ref, count_ref, tokens_ref, middle_grad_ref, qkv_ref, context_ref, ext_ref, w_ref, norm_ref, image_ref,
+    *refs,
+):
+    if first:
+        attn_backward_row(
+            first, refs[1:3], start_ref, class_ref, count_ref, tokens_ref, middle_grad_ref, qkv_ref, context_ref, ext_ref, w_ref,
+            norm_ref, image_ref, *refs[3:],
+        )
+    else:
+        attn_backward_row(
+            first, None, start_ref, class_ref, count_ref, tokens_ref, middle_grad_ref, qkv_ref, context_ref, ext_ref, w_ref,
+            norm_ref, image_ref, *refs,
+        )
+
+
+def attn_backward_row(
+    first, sums, start_ref, class_ref, count_ref, tokens_ref, middle_grad_ref, qkv_ref, context_ref, ext_ref, w_ref, norm_ref, image_ref,
     tokens_grad_ref, w_grad_ref, norm_grad_ref,
     tag_ref, up_ref, delta_ref, normed_ref, dq_ref, dk_ref, dv_ref, low_ref, proj_ref,
 ):
-    row = pl.program_id(0)
+    step_at = pl.program_id(0)
+    row = first + step_at
     length, width = tokens_ref.shape
     pairs = width // LANES
     heads = 2 * pairs
@@ -204,10 +227,10 @@
     gain, bias = norm_ref[0:1, :], norm_ref[1:2, :]
     first_row, last_row = image_ref[0, 0:1, :], image_ref[0, 1:2, :]
 
-    @pl.when(row == 0)
+    @pl.when(step_at == 0)
     def _():
-        w_grad_ref[...] = jnp.zeros_like(w_grad_ref)
-        norm_grad_ref[...] = jnp.zeros_like(norm_grad_ref)
+        for n, ref in enumerate((w_grad_ref, norm_grad_ref)):
+            ref[...] = sums[n][...] if sums else jnp.zeros_like(ref)
 
     source = lax.broadcasted_iota(jnp.int32, (width, LANES), 0)
     target = lax.broadcasted_iota(jnp.int32, (width, LANES), 1) - IMAGES
@@ -312,31 +335,29 @@
     w_grad_ref[3] += dot(jnp.transpose(low_ref[...]), context_ref[...])
 
 
-def attn_backward(starts, classes, counts, tokens, middle_grad, qkv, context, ext, attn_use, norm_w, images):
+def attn_backward(first, count, so_far, starts, classes, counts, tokens, middle_grad, qkv, context, ext, attn_use, norm_w, images):
     rows_all, width = tokens.shape
-    row_count = counts.shape[0]
-    length = rows_all // row_count
-    by_row = lambda columns: pl.BlockSpec((length, columns), lambda r, *_: (r, 0))
+    length = rows_all // counts.shape[0]
+    by_row = lambda columns: pl.BlockSpec((length, columns), lambda r, *_: (first + r, 0))
+    whole = pl.BlockSpec(attn_use.shape, lambda r, *_: (0, 0, 0))
+    sums = pl.BlockSpec((16, width), lambda r, *_: (0, 0))
     return pl.pallas_call(
-        attn_backward_kernel,
+        functools.partial(attn_backward_kernel, first),
         grid_spec=pltpu.PrefetchScalarGridSpec(
             num_scalar_prefetch=3,
-            grid=(row_count,),
+            grid=(count,),
             in_specs=[
                 by_row(width),
                 by_row(width),
                 by_row(3 * width),
                 by_row(width),
                 by_row(LANES),
-                pl.BlockSpec(attn_use.shape, lambda r, *_: (0, 0, 0)),
+                whole,
                 pl.BlockSpec(norm_w.shape, lambda r, *_: (0, 0)),
-                pl.BlockSpec((1, 8, LANES), lambda r, *_: (r, 0, 0)),
-            ],
-            out_specs=[
-                by_row(width),
-                pl.BlockSpec(attn_use.shape, lambda r, *_: (0, 0, 0)),
-                pl.BlockSpec((16, width), lambda r, *_: (0, 0)),
-            ],
+                pl.BlockSpec((1, 8, LANES), lambda r, *_: (first + r, 0, 0)),
+            ]
+            + ([pl.BlockSpec(memory_space=pl.ANY), whole, sums] if first else []),
+            out_specs=[by_row(width), whole, sums],
             scratch_shapes=[
                 pltpu.VMEM((length, LANES), bf16),
                 pltpu.VMEM((length, width), bf16),
@@ -354,22 +375,26 @@
             jax.ShapeDtypeStruct(attn_use.shape, f32),
             jax.ShapeDtypeStruct((16, width), f32),
         ],
+        input_output_aliases={11: 0} if first else {},
         compiler_params=pltpu.CompilerParams(vmem_limit_bytes=VMEM_BYTES),
-    )(starts, classes, counts, tokens, middle_grad, qkv, context, ext, attn_use, norm_w, images)
+    )(starts, classes, counts, tokens, middle_grad, qkv, context, ext, attn_use, norm_w, images, *(so_far or ()))
 
 
 def mlp_kernel(
-    middle_ref, out_grad_ref, w_ref, taps_ref, norm_ref, near_ref,
+    same_ref, middle_ref, out_grad_ref, w_ref, taps_ref, norm_ref,
     output_ref, middle_grad_ref, w_grad_ref, taps_grad_ref, norm_grad_ref,
-    normed_ref, hm_ref, h0_ref, hp_ref, act_ref, g_ref, gh_ref, tap_sum_ref,
+    normed_ref, normed_t_ref, out_grad_t_ref, out_sum_ref, up_sum_ref, tap_sum_ref,
+    act_grads_ref, acts_ref, hidden_grads_ref, *buffers,
 ):
     row = pl.program_id(0)
     length, width = middle_ref.shape
     hidden = w_ref.shape[2]
-    chunk = 256
-    block = 128
-    sub = 32
-    halo = GRID_W
+    chunk = 2 * LANES
+    big = 256
+    grid_rows = length // GRID_W
+    chunks = hidden // chunk
+    empty = grid_rows * STRIDE + 8
+    h_refs, g_refs = buffers[:2], buffers[2:]
     gain, bias = norm_ref[2:3, :], norm_ref[3:4, :]
 
     @pl.when(row == 0)
@@ -377,175 +402,183 @@
         w_grad_ref[...] = jnp.zeros_like(w_grad_ref)
         norm_grad_ref[...] = jnp.zeros_like(norm_grad_ref)
         tap_sum_ref[...] = jnp.zeros_like(tap_sum_ref)
-        for ref in (hm_ref, h0_ref, hp_ref, g_ref):
-            ref[0:halo, :] = jnp.zeros((halo, hidden), bf16)
-            ref[halo + length :, :] = jnp.zeros((halo, hidden), bf16)
+        for ref in buffers:
+            ref[...] = jnp.zeros_like(ref)
 
     def normalize(step, carry):
-        rows = pl.ds(pl.multiple_of(step * chunk, chunk), chunk)
-        unit, _ = norm_parts(middle_ref[rows, :])
+        rows = pl.ds(pl.multiple_of(step * big, big), big)
+        middle = middle_ref[rows, :]
+        unit, _ = norm_parts(middle)
         normed_ref[rows, :] = (unit * gain + bias).astype(bf16)
+        out_sum_ref[rows, :] = jnp.zeros((big, width), f32)
+        up_sum_ref[rows, :] = jnp.zeros((big, width), f32)
         return carry
 
-    lax.fori_loop(0, length // chunk, normalize, 0)
-    column = lax.rem(lax.broadcasted_iota(jnp.int32, (block, LANES), 0), GRID_W)
-    not_first = column != 0
-    not_last = column != GRID_W - 1
-
-    def expand(step, carry):
-        c = step // (length // block)
-        t = step - c * (length // block)
-        rows = pl.ds(pl.multiple_of(t * block, block), block)
-        place = pl.ds(pl.multiple_of(t * block + halo, GRID_W), block)
-        values = dot(normed_ref[rows, :], w_ref[0, :, pl.ds(pl.multiple_of(c * chunk, chunk), chunk)])
-        for part in range(chunk // LANES):
-            lanes = pl.ds(pl.multiple_of(c * chunk + part * LANES, LANES), LANES)
-            one = values[:, part * LANES : (part + 1) * LANES]
-            h0_ref[place, lanes] = one.astype(bf16)
-            hm_ref[place, lanes] = jnp.where(not_first, pltpu.roll(one, 1, 0), 0.0).astype(bf16)
-            hp_ref[place, lanes] = jnp.where(not_last, pltpu.roll(one, block - 1, 0), 0.0).astype(bf16)
+    lax.fori_loop(0, length // big, normalize, 0)
+    normed_t_ref[...] = jnp.transpose(normed_ref[...])
+    out_grad_t_ref[...] = jnp.transpose(out_grad_ref[...])
+
+    def lanes_of(c):
+        return pl.ds(pl.multiple_of(c * chunk, chunk), chunk)
+
+    def lanes_of(c):
+        return pl.ds(pl.multiple_of(c * chunk, chunk), chunk)
+
+    def places(r):
+        here = r * STRIDE + 8
+        above = jnp.where(same_ref[row, r] == 1, here - STRIDE, empty)
+        below = jnp.where(same_ref[row, r + 1] == 1, here + STRIDE, empty)
+        return [pl.multiple_of(at, 8) for at in (above, here, below)]
+
+    def neighbours(ref, at):
+        return [ref[pl.ds(at - 1, GRID_W), :], ref[pl.ds(at, GRID_W), :], ref[pl.ds(at + 1, GRID_W), :]]
+
+    def tall(values):
+        return jnp.concatenate([values, values], axis=0)
+
+    def total_of(terms):
+        while len(terms) > 1:
+            terms = [a + b for a, b in zip(terms[::2], terms[1::2])] + ([terms[-1]] if len(terms) % 2 else [])
+        return terms[0]
+
+    def taps_for(c, part, at):
+        lane = pl.ds(pl.multiple_of(c * chunk + part * LANES, LANES), LANES)
+        return [tall(taps_ref[at + k * 8 : at + (k + 1) * 8, lane]) for k in range(9)]
+
+    lines = 16
+
+    def do_chunk(c, carry):
+        lanes = lanes_of(c)
+        for t in range(length // big):
+            rows = slice(t * big, (t + 1) * big)
+            values = dot(normed_ref[rows, :], w_ref[0, :, lanes])
+            for part in range(2):
+                for s in range(big // GRID_W):
+                    at = (t * (big // GRID_W) + s) * STRIDE + 8
+                    h_refs[part][at : at + GRID_W, :] = values[
+                        s * GRID_W : (s + 1) * GRID_W, part * LANES : (part + 1) * LANES
+                    ]
+        act_grads_ref[...] = dot(out_grad_ref[...], w_ref[1, :, lanes])
+
+        def forward(t, carry):
+            for part in range(2):
+                taps = taps_for(c, part, 0)
+                cols = slice(part * LANES, (part + 1) * LANES)
+                for s in range(lines):
+                    r = t * lines + s
+                    near = pl.ds(pl.multiple_of(r * GRID_W, GRID_W), GRID_W)
+                    around = places(r)
+                    terms = []
+                    for a, at in enumerate(around):
+                        terms += [x * taps[3 * a + b] for b, x in enumerate(neighbours(h_refs[part], at))]
+                    x = total_of(terms)
+                    square = x * x
+                    value = jnp.tanh(x * (GELU_A + square))
+                    gate = 1.0 + value
+                    twice = x * gate
+                    acts_ref[near, cols] = twice.astype(bf16)
+                    slope = gate + (twice * (1.0 - value)) * (GELU_A + 3.0 * square)
+                    g_refs[part][pl.ds(around[1], GRID_W), :] = act_grads_ref[near, cols] * slope
+            return carry
+
+        lax.fori_loop(0, grid_rows // lines, forward, 0)
+
+        def backward(t, carry):
+            for part in range(2):
+                taps = taps_for(c, part, 72)
+                lane = pl.ds(pl.multiple_of(c * chunk + part * LANES, LANES), LANES)
+                cols = slice(part * LANES, (part + 1) * LANES)
+                totals = [None] * 9
+                for s in range(lines):
+                    r = t * lines + s
+                    near = pl.ds(pl.multiple_of(r * GRID_W, GRID_W), GRID_W)
+                    around = places(r)
+                    source = h_refs[part][pl.ds(around[1], GRID_W), :]
+                    terms = []
+                    for a in range(3):
+                        moved = neighbours(g_refs[part], around[2 - a])[::-1]
+                        for b in range(3):
+                            k = 3 * a + b
+                            terms.append(moved[b] * taps[k])
+                            product = source * moved[b]
+                            folded = product[:8] + product[8:]
+                            totals[k] = folded if totals[k] is None else totals[k] + folded
+                    hidden_grads_ref[near, cols] = total_of(terms).astype(bf16)
+                for k in range(9):
+                    tap_sum_ref[k * 8 : (k + 1) * 8, lane] += totals[k]
+            return carry
+
+        lax.fori_loop(0, grid_rows // lines, backward, 0)
+        w_grad_ref[0, :, lanes] += dot(normed_t_ref[...], hidden_grads_ref[...])
+        w_grad_ref[1, :, lanes] += dot(out_grad_t_ref[...], acts_ref[...])
+        out_sum_ref[...] += dot(acts_ref[...], w_ref[1, :, lanes], NT)
+        up_sum_ref[...] += dot(hidden_grads_ref[...], w_ref[0, :, lanes], NT)
         return carry
 
-    lax.fori_loop(0, (hidden // chunk) * (length // block), expand, 0)
-
-    def tile_rows(values, rows):
-        return jnp.concatenate([values] * (rows // GRID_W), axis=0)
-
-    def activate(step, carry):
-        c = step // (length // block)
-        t = step - c * (length // block)
-        rows = pl.ds(pl.multiple_of(t * block, block), block)
-        act_grad = dot(out_grad_ref[rows, :], w_ref[1, :, pl.ds(pl.multiple_of(c * chunk, chunk), chunk)])
-        for part in range(chunk // LANES):
-            lanes = pl.ds(pl.multiple_of(c * chunk + part * LANES, LANES), LANES)
-            taps = [tile_rows(taps_ref[k * GRID_W : (k + 1) * GRID_W, lanes], sub) for k in range(9)]
-            for s in range(block // sub):
-                base = t * block + s * sub
-                near = pl.ds(pl.multiple_of(base, GRID_W), sub)
-                mixed = None
-                for a in (-1, 0, 1):
-                    at = pl.ds(pl.multiple_of(base + halo + a * GRID_W, GRID_W), sub)
-                    total = None
-                    for b, ref in ((-1, hm_ref), (0, h0_ref), (1, hp_ref)):
-                        term = ref[at, lanes] * taps[3 * (a + 1) + b + 1]
-                        total = term if total is None else total + term
-                    if a == 0:
-                        total = total + h0_ref[at, lanes]
-                    elif a == -1:
-                        total = total * near_ref[0, near, :]
-                    else:
-                        total = total * near_ref[1, near, :]
-                    mixed = total if mixed is None else mixed + total
-                x = mixed.astype(f32)
-                square = x * x
-                t_value = jnp.tanh(x * (GELU_ONE + (GELU_ONE * GELU_TWO) * square))
-                half = 0.5 * x
-                act_ref[near, lanes] = (half + half * t_value).astype(bf16)
-                slope = (0.5 + 0.5 * t_value) + half * (1.0 - t_value * t_value) * (
-                    GELU_ONE + (3.0 * GELU_ONE * GELU_TWO) * square
-                )
-                grad = act_grad[s * sub : (s + 1) * sub, part * LANES : (part + 1) * LANES] * slope
-                g_ref[pl.ds(pl.multiple_of(base + halo, GRID_W), sub), lanes] = grad.astype(bf16)
-        return carry
-
-    lax.fori_loop(0, (hidden // chunk) * (length // block), activate, 0)
-
-    def conv_back(step, carry):
-        c = step // (length // block)
-        t = step - c * (length // block)
-        lanes = pl.ds(pl.multiple_of(c * LANES, LANES), LANES)
-        taps = [tile_rows(taps_ref[k * GRID_W : (k + 1) * GRID_W, lanes], sub) for k in range(9)]
-        sums = [None] * 9
-        col = lax.rem(lax.broadcasted_iota(jnp.int32, (sub, LANES), 0), GRID_W)
-        for s in range(block // sub):
-            base = t * block + s * sub
-            near = pl.ds(pl.multiple_of(base, GRID_W), sub)
-            at = pl.ds(pl.multiple_of(base + halo, GRID_W), sub)
-            before = pl.ds(pl.multiple_of(base, GRID_W), sub)
-            after = pl.ds(pl.multiple_of(base + 2 * halo, GRID_W), sub)
-            here = g_ref[at, lanes]
-            sources = (
-                g_ref[after, lanes] * near_ref[1, near, :],
-                here,
-                g_ref[before, lanes] * near_ref[0, near, :],
-            )
-            side = {}
-            for b, ref in ((-1, hm_ref), (0, h0_ref), (1, hp_ref)):
-                moved = ref[at, lanes]
-                total = None
-                for a in (-1, 0, 1):
-                    k = 3 * (a + 1) + b + 1
-                    term = sources[a + 1] * taps[k]
-                    total = term if total is None else total + term
-                    product = moved * sources[a + 1]
-                    folded = product[:GRID_W]
-                    for piece in range(1, sub // GRID_W):
-                        folded = folded + product[piece * GRID_W : (piece + 1) * GRID_W]
-                    sums[k] = folded if sums[k] is None else sums[k] + folded
-                side[b] = total
-            result = (side[0] + here).astype(f32)
-            result = result + jnp.where(col != 0, pltpu.roll(side[1].astype(f32), 1, 0), 0.0)
-            result = result + jnp.where(col != GRID_W - 1, pltpu.roll(side[-1].astype(f32), sub - 1, 0), 0.0)
-            gh_ref[near, lanes] = result.astype(bf16)
-        for k in range(9):
-            tap_sum_ref[k * GRID_W : (k + 1) * GRID_W, lanes] += sums[k].astype(f32)
-        return carry
-
-    lax.fori_loop(0, (hidden // LANES) * (length // block), conv_back, 0)
+    lax.fori_loop(0, chunks, do_chunk, 0)
 
     def finish(step, carry):
-        rows = pl.ds(pl.multiple_of(step * chunk, chunk), chunk)
+        rows = pl.ds(pl.multiple_of(step * big, big), big)
         middle = middle_ref[rows, :]
-        output_ref[rows, :] = (middle + dot(act_ref[rows, :], w_ref[1], NT)).astype(bf16)
-        upstream = dot(gh_ref[rows, :], w_ref[0], NT)
+        output_ref[rows, :] = (middle + ACT_SCALE * out_sum_ref[rows, :]).astype(bf16)
+        upstream = 0.5 * up_sum_ref[rows, :]
         unit, inverse = norm_parts(middle)
         middle_grad_ref[rows, :] = out_grad_ref[rows, :].astype(f32) + norm_back(upstream, gain, unit, inverse)
         norm_grad_ref[0:8, :] += fold_rows(upstream * unit)
         norm_grad_ref[8:16, :] += fold_rows(upstream)
         return carry
 
-    lax.fori_loop(0, length // chunk, finish, 0)
-    normed_t = jnp.transpose(normed_ref[...])
-    out_grad_t = jnp.transpose(out_grad_ref[...])
-
-    def weights(c, carry):
-        lanes = pl.ds(pl.multiple_of(c * chunk, chunk), chunk)
-        w_grad_ref[0, :, lanes] += dot(normed_t, gh_ref[:, lanes])
-        w_grad_ref[1, :, lanes] += dot(out_grad_t, act_ref[:, lanes])
-        return carry
-
-    lax.fori_loop(0, hidden // chunk, weights, 0)
+    lax.fori_loop(0, length // big, finish, 0)
 
     @pl.when(row == pl.num_programs(0) - 1)
     def _():
+        w_grad_ref[0] = w_grad_ref[0] * 0.5
+        w_grad_ref[1] = w_grad_ref[1] * ACT_SCALE
         taps_grad_ref[...] = jnp.zeros_like(taps_grad_ref)
         for k in range(9):
-            taps_grad_ref[k : k + 1, :] = jnp.sum(tap_sum_ref[k * GRID_W : (k + 1) * GRID_W, :], axis=0, keepdims=True)
-
-
-def mlp_layer(middle, out_grad, mlp_use, taps, norm_w, near, row_count):
+            total = jnp.sum(tap_sum_ref[k * 8 : (k + 1) * 8, :], axis=0, keepdims=True)
+            taps_grad_ref[k : k + 1, :] = 0.5 * total
+
+
+def mlp_layer(same, middle, out_grad, mlp_use, taps, norm_w):
     rows_all, width = middle.shape
+    row_count = same.shape[0]
     length = rows_all // row_count
     hidden = mlp_use.shape[2]
-    by_row = lambda columns: pl.BlockSpec((length, columns), lambda r: (r, 0))
+    by_row = lambda columns: pl.BlockSpec((length, columns), lambda r, *_: (r, 0))
+    slots = (length // GRID_W + 2) * STRIDE
     return pl.pallas_call(
         mlp_kernel,
-        grid=(row_count,),
-        in_specs=[
-            by_row(width),
-            by_row(width),
-            pl.BlockSpec(mlp_use.shape, lambda r: (0, 0, 0)),
-            pl.BlockSpec(taps.shape, lambda r: (0, 0)),
-            pl.BlockSpec(norm_w.shape, lambda r: (0, 0)),
-            pl.BlockSpec((2, length, LANES), lambda r: (0, r, 0)),
-        ],
-        out_specs=[
-            by_row(width),
-            by_row(width),
-            pl.BlockSpec(mlp_use.shape, lambda r: (0, 0, 0)),
-            pl.BlockSpec((16, hidden), lambda r: (0, 0)),
-            pl.BlockSpec((16, width), lambda r: (0, 0)),
-        ],
+        grid_spec=pltpu.PrefetchScalarGridSpec(
+            num_scalar_prefetch=1,
+            grid=(row_count,),
+            in_specs=[
+                by_row(width),
+                by_row(width),
+                pl.BlockSpec(mlp_use.shape, lambda r, *_: (0, 0, 0)),
+                pl.BlockSpec(taps.shape, lambda r, *_: (0, 0)),
+                pl.BlockSpec(norm_w.shape, lambda r, *_: (0, 0)),
+            ],
+            out_specs=[
+                by_row(width),
+                by_row(width),
+                pl.BlockSpec(mlp_use.shape, lambda r, *_: (0, 0, 0)),
+                pl.BlockSpec((16, hidden), lambda r, *_: (0, 0)),
+                pl.BlockSpec((16, width), lambda r, *_: (0, 0)),
+            ],
+            scratch_shapes=[
+                pltpu.VMEM((length, width), bf16),
+                pltpu.VMEM((width, length), bf16),
+                pltpu.VMEM((width, length), bf16),
+                pltpu.VMEM((length, width), f32),
+                pltpu.VMEM((length, width), f32),
+                pltpu.VMEM((9 * 8, hidden), f32),
+                pltpu.VMEM((length, 2 * LANES), f32),
+                pltpu.VMEM((length, 2 * LANES), bf16),
+                pltpu.VMEM((length, 2 * LANES), bf16),
+            ]
+            + [pltpu.VMEM((slots, LANES), f32)] * 4,
+        ),
         out_shape=[
             jax.ShapeDtypeStruct((rows_all, width), bf16),
             jax.ShapeDtypeStruct((rows_all, width), f32),
@@ -553,18 +586,8 @@
             jax.ShapeDtypeStruct((16, hidden), f32),
             jax.ShapeDtypeStruct((16, width), f32),
         ],
-        scratch_shapes=[
-            pltpu.VMEM((length, width), bf16),
-            pltpu.VMEM((length + 2 * GRID_W, hidden), bf16),
-            pltpu.VMEM((length + 2 * GRID_W, hidden), bf16),
-            pltpu.VMEM((length + 2 * GRID_W, hidden), bf16),
-            pltpu.VMEM((length, hidden), bf16),
-            pltpu.VMEM((length + 2 * GRID_W, hidden), bf16),
-            pltpu.VMEM((length, hidden), bf16),
-            pltpu.VMEM((9 * GRID_W, hidden), f32),
-        ],
         compiler_params=pltpu.CompilerParams(vmem_limit_bytes=VMEM_BYTES),
-    )(middle, out_grad, mlp_use, taps, norm_w, near)
+    )(same, middle, out_grad, mlp_use, taps, norm_w)
 
 
 def attention_plan(segments):
@@ -590,12 +613,17 @@
     return starts, classes, images
 
 
-def neighbour_masks(segments):
-    same = (segments[:, GRID_W:] == segments[:, :-GRID_W]).astype(bf16)
-    zeros = jnp.zeros((segments.shape[0], GRID_W), bf16)
-    above = jnp.concatenate([zeros, same], axis=1).reshape(-1)
-    below = jnp.concatenate([same, zeros], axis=1).reshape(-1)
-    return jnp.broadcast_to(jnp.stack([above, below])[:, :, None], (2, above.shape[0], LANES))
+def spread_taps(conv_use):
+    taps = conv_use.astype(f32)
+    own = (jnp.arange(9) == 4).astype(f32)[:, None]
+    taps = jnp.repeat(taps + own, 8, axis=0)
+    return jnp.concatenate([taps * GELU_S, taps], axis=0)
+
+
+def same_images(segments):
+    ids = segments[:, ::GRID_W]
+    edge = jnp.zeros((ids.shape[0], 1), jnp.int32)
+    return jnp.concatenate([edge, (ids[:, 1:] == ids[:, :-1]).astype(jnp.int32), edge], axis=1)
 
 
 def bits_of(size):
@@ -635,24 +663,44 @@
     return jnp.moveaxis(full, 0, 1).reshape(count, size * part, 2 * columns)
 
 
-def own_columns(values, rank):
+def half_columns(values, side):
     half = values.shape[-1] // 2
-    mine = lax.dynamic_slice_in_dim(values, rank * half, half, axis=values.ndim - 1)
-    other = lax.dynamic_slice_in_dim(values, (1 - rank) * half, half, axis=values.ndim - 1)
-    return mine + swap(other.astype(bf16), "head", 2, 1).astype(f32)
-
-
-def scatter_lines(values, size):
+    return lax.dynamic_slice_in_dim(values, side * half, half, axis=values.ndim - 1)
+
+
+def by_line(values, size):
     count, rows, columns = values.shape
-    place = lax.axis_index("dp")
-    held = jnp.moveaxis(values.reshape(count, size, rows // size, columns), 1, 0)
-    for bit in bits_of(size):
-        held = held.reshape((-1, 2) + held.shape[1:])
-        side = (place & bit) // bit
-        mine = lax.dynamic_index_in_dim(held, side, 1, keepdims=False)
-        other = lax.dynamic_index_in_dim(held, 1 - side, 1, keepdims=False)
-        held = mine + swap(other.astype(bf16), "dp", size, bit).astype(f32)
-    return held[0]
+    return jnp.moveaxis(values.reshape(count, size, rows // size, columns), 1, 0).reshape(size, -1, columns)
+
+
+def two_parts(values):
+    high = values.astype(bf16)
+    return jnp.concatenate([high, (values - high.astype(f32)).astype(bf16)], axis=0)
+
+
+def from_parts(parts):
+    count = parts.shape[0] // 2
+    return parts[:count].astype(f32) + parts[count:].astype(f32)
+
+
+def finish_exchange(keep, got, small_keep):
+    rows = keep.size // keep.shape[-1]
+    small = from_parts(two_parts(small_keep)) + from_parts(got[rows:])
+    return keep + got[:rows].reshape(keep.shape).astype(f32), small
+
+
+def start_exchange(send, small_send, axis, size, bit):
+    sent = send.astype(bf16).reshape(-1, send.shape[-1])
+    if small_send is not None:
+        sent = jnp.concatenate([sent, two_parts(small_send)], axis=0)
+    return swap(sent, axis, size, bit)
+
+
+def halves(held, bit):
+    held = held.reshape((-1, 2) + held.shape[1:])
+    side = (lax.axis_index("dp") & bit) // bit
+    mine = lax.dynamic_index_in_dim(held, side, 1, keepdims=False)
+    return mine, lax.dynamic_index_in_dim(held, 1 - side, 1, keepdims=False)
 
 
 def sum_everywhere(values, size):
@@ -673,6 +721,10 @@
     return (first_new, second_new, direction)
 
 
+def after(first, second):
+    return lax.optimization_barrier((first, second))
+
+
 def body(
     size,
     tokens, grad_out, segments, counts,
@@ -682,24 +734,65 @@
     own_rows = segments.shape[0] // 2
     segments = lax.dynamic_slice_in_dim(segments, rank * own_rows, own_rows, axis=0)
     counts = lax.dynamic_slice_in_dim(counts, rank * own_rows, own_rows, axis=0)
+    width = norm_w.shape[1]
     attn_use = gather_weights(attn_w.astype(bf16), size, rank)
     mlp_lines = lax.all_gather(mlp_w.astype(bf16), "dp", axis=1, tiled=True)
-    mlp_use = join_columns(mlp_lines, swap(mlp_lines, "head", 2, 1), rank)
     conv_low = conv_w.astype(bf16)
     conv_use = join_columns(conv_low, swap(conv_low, "head", 2, 1), rank)
     starts, classes, images = attention_plan(segments)
     middle, qkv, context, ext = attn_forward(starts, classes, counts, tokens, attn_use, norm_w, images)
+    middle, mlp_lines = after(middle, mlp_lines)
+    mlp_use = join_columns(mlp_lines, swap(mlp_lines, "head", 2, 1), rank)
     output, grad_middle, grad_mlp, grad_conv, grad_norm_two = mlp_layer(
-        middle, grad_out, mlp_use, jnp.repeat(conv_use, GRID_W, axis=0), norm_w, neighbour_masks(segments), own_rows
+        same_images(segments), middle, grad_out, mlp_use, spread_taps(conv_use), norm_w
     )
-    grad_tokens, grad_attn, grad_norm_one = attn_backward(
-        starts, classes, counts, tokens, grad_middle, qkv, context, ext, attn_use, norm_w, images
+
+    def back(first, count, so_far):
+        return attn_backward(
+            first, count, so_far, starts, classes, counts, tokens, grad_middle, qkv, context, ext, attn_use, norm_w, images
+        )
+
+    norm_two = jnp.sum(grad_norm_two.reshape(2, 8, width), axis=1).reshape(1, 2 * width)
+    columns = conv_w.shape[1]
+    wide_norm = jnp.pad(norm_two, ((0, 0), (0, columns - 2 * width)))
+    small = jnp.concatenate([half_columns(grad_conv[:9], rank), wide_norm])
+    held = by_line(half_columns(grad_mlp, rank), size)
+    got = start_exchange(
+        by_line(half_columns(grad_mlp, 1 - rank), size),
+        jnp.concatenate([half_columns(grad_conv[:9], 1 - rank), wide_norm]),
+        "head", 2, 1,
     )
-    grad_mlp = scatter_lines(own_columns(grad_mlp, rank), size)
-    grad_conv = own_columns(grad_conv[:9], rank)
-    for bit in bits_of(size):
-        grad_conv = grad_conv + swap(grad_conv, "dp", size, bit)
-    grad_attn = scatter_lines(own_columns(grad_attn, rank), size)
+    bits = bits_of(size)
+    first_rows = max(1, own_rows // 3)
+    so_far = back(0, first_rows, None)
+    so_far, got = after(so_far, got)
+    held, small = finish_exchange(held, got, small)
+    keep, send = halves(held, bits[0])
+    got = start_exchange(send, small, "dp", size, bits[0])
+    if first_rows < own_rows:
+        so_far, send = after(so_far, send)
+        so_far = back(first_rows, own_rows - first_rows, so_far)
+        so_far, got = after(so_far, got)
+    grad_tokens, grad_attn, grad_norm_one = so_far
+    held, small = finish_exchange(keep, got, small)
+
+    attn_got = start_exchange(half_columns(grad_attn, 1 - rank), None, "head", 2, 1)
+    attn_held = half_columns(grad_attn, rank)
+    attn_held = by_line(attn_held + attn_got.reshape(attn_held.shape).astype(f32), size)
+    for n, bit in enumerate(bits):
+        attn_keep, attn_send = halves(attn_held, bit)
+        attn_got = start_exchange(attn_send, None, "dp", size, bit)
+        if n + 1 < len(bits):
+            keep, send = halves(held, bits[n + 1])
+            got = start_exchange(send, small, "dp", size, bits[n + 1])
+        attn_held = attn_keep + attn_got.reshape(attn_keep.shape).astype(f32)
+        if n + 1 < len(bits):
+            held, small = finish_exchange(keep, got, small)
+    grad_attn = attn_held.reshape(attn_w.shape)
+    grad_mlp = held.reshape(mlp_w.shape)
+    grad_conv = small[:9]
+    norm_two = small[9, : 2 * width].reshape(2, width)
+
     new_attn_m, new_attn_v, attn_direction = adam_terms(grad_attn, attn_m, attn_v)
     new_mlp_m, new_mlp_v, mlp_direction = adam_terms(grad_mlp, mlp_m, mlp_v)
     new_conv_m, new_conv_v, conv_direction = adam_terms(grad_conv, conv_m, conv_v)
@@ -721,16 +814,10 @@
             (first_line * jnp.sum(conv_update * conv_update))[None],
         ]
     )
-    width = norm_w.shape[1]
-    norm_part = jnp.concatenate(
-        [
-            jnp.sum(grad_norm_one.reshape(2, 8, width), axis=1),
-            jnp.sum(grad_norm_two.reshape(2, 8, width), axis=1),
-        ]
-    )
     squares = jnp.pad(jnp.stack([weight_squares, update_squares]), ((0, 0), (0, width - 7)))
-    summed = sum_everywhere(jnp.concatenate([squares, norm_part, jnp.zeros((2, width), f32)]), size)
-    squares, norm_grads = summed[:2, :7], summed[2:6]
+    norm_one = jnp.sum(grad_norm_one.reshape(2, 8, width), axis=1)
+    summed = sum_everywhere(jnp.concatenate([squares, norm_one, jnp.zeros((4, width), f32)]), size)
+    squares, norm_grads = summed[:2, :7], jnp.concatenate([summed[2:4], norm_two])
     ratio = jnp.sqrt(squares[0]) / jnp.sqrt(squares[1])
     new_attn_w = attn_w - RATE * ratio[:4, None, None] * attn_update
     new_mlp_w = mlp_w - RATE * ratio[4:6, None, None] * mlp_update

time: 425 us -> 354 us (0.83)
  waiting for transfers between devices: 97.5 us -> 53.5 us
  Pallas kernels: 249 us -> 214 us
  starting transfers between devices: 24.9 us -> 29.7 us
    pallas_call x2 -> x3, Pallas kernels: 201 us -> 166 us  [the longest x1 103 us: mlp_layer(): pl.pallas_call(mlp_kernel, grid_spec=pltpu.PrefetchScalarGridSpec(num_sca...]
    all_gather x1, waiting for transfers between devices: 27.7 us -> 0.01 us  [body(): mlp_lines = lax.all_gather(mlp_w.astype(bf16), 'dp', axis=1, tiled=True)]
    ppermute x27 -> x22, waiting for transfers between devices: 69.8 us -> 53.5 us  [swap(): return lax.ppermute(values, axis, [(i, i ^ bit) for i in range(size)])]
    ppermute x27 -> x22, starting transfers between devices: 24.9 us -> 29.6 us  [swap(): return lax.ppermute(values, axis, [(i, i ^ bit) for i in range(size)])]
  transfers between devices with their start and end apart: 28 -> 23, of which waited for: 19 -> 17; matrix products, arithmetic and copies ran while one was open for 6% -> 5% of each run, Pallas kernels for 25% -> 32%
where the time goes in v2:
time: 354 us; the launch traced here: 350 us
  Pallas kernels  214 us (60%)
  waiting for transfers between devices  53.5 us (15%)
  starting transfers between devices  29.7 us (8%)
  other arithmetic  20.3 us (6%)
  between operations  17 us (5%)
  local copies, waits for them, and re-layouts  15.5 us (4%)
    pallas_call x1, Pallas kernels, mlp_layer(): pl.pallas_call(mlp_kernel, grid_spec=pltpu.PrefetchScalarGridSpec(num_sca...  103 us
    pallas_call x2, Pallas kernels, attn_backward(): pl.pallas_call(functools.partial(attn_backward_kernel, first), grid_spec=...  63.3 us
    ppermute x22, waiting for transfers between devices, swap(): return lax.ppermute(values, axis, [(i, i ^ bit) for i in range(size)])  53.5 us
    pallas_call x1, Pallas kernels, attn_forward(): pl.pallas_call(attn_forward_kernel, grid_spec=pltpu.PrefetchScalarGridSpe...  48.2 us
    ppermute x22, starting transfers between devices, swap(): return lax.ppermute(values, axis, [(i, i ^ bit) for i in range(size)])  29.6 us
  transfers between devices with their start and end apart: 23, of which 17 were waited for; matrix products, arithmetic and copies ran while one was open for 5% of the time, Pallas kernels for 32%

profile of v2, /device:TPU:0, one launch (start us, length us, event | category | flops | bytes accessed | tf_op | source)
XLA Modules:
  0.0 350.2 jit_solution(3488179989354675392)
XLA Ops:
  7.3 0.9 convert_bitcast_fusion
  8.2 4.0 %collective-permute-start = (bf16[1,4,24,192]{3,2,1,0:T(8,128)(2,1)S(1)}, bf16[1,4,24,192]{3,2,1,0:T(8,128)(2,1)S(1)}, u32[]{:S(2)}, u32[]{:S(2)}) collective-permute-start(bf16[1,4,24,192]{3,2,1,0:T(8,128)(2,1)S(1)} %convert_bitcast_fusion), channel_id=1, source_target_pairs={{0,16},{2,18},{4,20},{6,22},{8,24},{10,26},{12,28},{14,30},{16,0},... | collective-permute-start | bytes 110600 | tf_op jit(solution)/shard_map/ppermute | solution.py:639
  12.2 1.6 convert_element_type.304
  15.5 0.9 select_bitcast_fusion.7
  16.4 1.6 collective-permute-start.1
  18.3 3.4 collective-permute-done.1
  21.8 1.6 collective-permute-start.2
  24.9 4.0 %collective-permute-done.2 = bf16[4,4,24,192]{3,2,1,0:T(8,128)(2,1)S(1)} collective-permute-done((bf16[4,4,24,192]{3,2,1,0:T(8,128)(2,1)S(1)}, bf16[4,4,24,192]{3,2,1,0:T(8,128)(2,1)S(1)}, u32[]{:S(2)}, u32[]{:S(2)}) %collective-permute-start.2) | collective-permute-done | bytes 147488 | tf_op jit(solution)/shard_map/ppermute | solution.py:639
  29.0 1.6 collective-permute-start.3
  31.2 7.8 %collective-permute-done.3 = bf16[8,4,24,192]{3,2,1,0:T(8,128)(2,1)S(1)} collective-permute-done((bf16[8,4,24,192]{3,2,1,0:T(8,128)(2,1)S(1)}, bf16[8,4,24,192]{3,2,1,0:T(8,128)(2,1)S(1)}, u32[]{:S(2)}, u32[]{:S(2)}) %collective-permute-start.3) | collective-permute-done | bytes 294944 | tf_op jit(solution)/shard_map/ppermute | solution.py:639
  40.0 1.7 collective-permute-done.4
  42.3 1.2 copy.79
  43.5 48.2 %shard_map.263 = (f32[3072,384]{1,0:T(8,128)}, bf16[3072,1152]{1,0:T(8,128)(2,1)}, bf16[3072,384]{1,0:T(8,128)(2,1)}, bf16[3072,128]{1,0:T(8,128)(2,1)}) custom-call(s32[3,8]{1,0:T(4,128)} %get-tuple-element.140.start_ref, s32[3,8]{1,0:T(4,128)} %get-tuple-element.139.class_ref, s32[3]{0:T(128)} %dynamic_slice.73.count_ref, bf16[3072,384]{1,0:T(8,128)(2,1)} %tokens_ref.5, ...), custom_call_target="tpu_custom_call" | custom-call | tf_op jit(solution)/shard_map/pallas_call | solution.py:176
  91.7 1.3 collective-permute-start.5
  93.1 1.0 pad_maximum_fusion.2.taps_ref
  94.1 1.6 collective-permute-done.5
  95.8 1.6 pad_maximum_fusion.w_ref
  97.4 102.8 %shard_map.264 = (bf16[3072,384]{1,0:T(8,128)(2,1)}, f32[3072,384]{1,0:T(8,128)}, f32[2,384,1536]{2,1,0:T(8,128)}, f32[16,1536]{1,0:T(8,128)}, f32[16,384]{1,0:T(8,128)}) custom-call(s32[3,65]{1,0:T(4,128)} %pad_add_fusion.same_ref, f32[3072,384]{1,0:T(8,128)} %get-tuple-element.67.middle_ref, bf16[3072,384]{1,0:T(8,128)(2,1)} %out_grad_ref.1, ...), custom_call_target="tpu_custom_call" | custom-call | tf_op jit(solution)/shard_map/pallas_call | solution.py:550
  201.9 1.8 dynamic-slice_convert_fusion
  203.7 1.2 pad_maximum_fusion.1
  205.3 1.8 constant_dynamic-slice_fusion.5
  207.4 22.5 %shard_map.265 = (f32[3072,384]{1,0:T(8,128)}, f32[4,384,384]{2,1,0:T(8,128)}, f32[16,384]{1,0:T(8,128)}) custom-call(s32[3,8]{1,0:T(4,128)} %get-tuple-element.140.start_ref, s32[3,8]{1,0:T(4,128)} %get-tuple-element.139.class_ref, s32[3]{0:T(128)} %dynamic_slice.73.count_ref, bf16[3072,384]{1,0:T(8,128)(2,1)} %tokens_ref.5, ...), custom_call_target="tpu_custom_call" | custom-call | tf_op jit(solution)/shard_map/pallas_call | solution.py:344
  230.2 1.4 copy-done.2
  232.6 1.8 collective-permute-start.8
  234.4 40.8 %shard_map.266 = (f32[3072,384]{1,0:T(8,128)}, f32[4,384,384]{2,1,0:T(8,128)}, f32[16,384]{1,0:T(8,128)}) custom-call(s32[3,8]{1,0:T(4,128)} %get-tuple-element.140.start_ref, s32[3,8]{1,0:T(4,128)} %get-tuple-element.139.class_ref, s32[3]{0:T(128)} %dynamic_slice.73.count_ref, bf16[3072,384]{1,0:T(8,128)(2,1)} %tokens_ref.5, ...), custom_call_target="tpu_custom_call", output_to_operand_aliasing={{0}: (11, {})} | custom-call | tf_op jit(solution)/shard_map/pallas_call | solution.py:344
  275.6 2.6 collective-permute-start.14
  278.3 8.0 %collective-permute-done.14 = bf16[212,768]{1,0:T(8,128)(2,1)S(1)} collective-permute-done((bf16[212,768]{1,0:T(8,128)(2,1)S(1)}, bf16[212,768]{1,0:T(8,128)(2,1)S(1)}, u32[]{:S(2)}, u32[]{:S(2)}) %collective-permute-start.14) | collective-permute-done | bytes 325664 | tf_op jit(solution)/shard_map/ppermute | solution.py:639
  287.0 1.7 dynamic-slice_convert_fusion.1
  289.3 3.5 collective-permute-done.15
  292.9 1.3 copy.83
  294.3 2.1 dynamic-slice_add_fusion
  297.7 2.2 collective-permute-done.16
  299.9 4.5 %collective-permute-done.10 = bf16[768,192]{0,1:T(8,128)(2,1)} collective-permute-done((bf16[768,192]{0,1:T(8,128)(2,1)S(1)}, bf16[768,192]{0,1:T(8,128)(2,1)}, u32[]{:S(2)}, u32[]{:S(2)}) %collective-permute-start.10) | collective-permute-done | bytes 294944 | tf_op jit(solution)/shard_map/ppermute | solution.py:639
  304.4 1.1 copy.89
  305.9 1.7 collective-permute-start.11
  307.9 3.2 collective-permute-done.11
  311.3 1.8 collective-permute-start.12
  313.1 3.4 collective-permute-done.12
  316.6 2.4 collective-permute-start.13
  322.1 1.2 collective-permute-done.17
  323.3 1.6 collective-permute-start.18
  324.9 2.1 collective-permute-done.18
  327.0 1.6 collective-permute-start.19
  328.6 2.1 collective-permute-done.19
  330.7 1.7 collective-permute-start.20
  332.4 2.0 collective-permute-done.20
  334.4 2.3 collective-permute-start.21
  336.8 2.2 collective-permute-done.21
  (174 shorter events, 19.1 us)
Async XLA Ops:
  7.2 7.4 %copy-start = (s32[6,1024]{1,0:T(8,128)S(1)}, s32[6,1024]{1,0:T(8,128)}, u32[]{:S(2)}) copy-start(s32[6,1024]{1,0:T(8,128)} %param.22) | copy-start | bytes 73732
  7.2 16.8 %copy-start.25 = (s32[6]{0:T(128)S(1)}, s32[6]{0:T(128)}, u32[]{:S(2)}) copy-start(s32[6]{0:T(128)} %param.23) | copy-start | bytes 76
  7.2 84.5 %all-gather.2.cloned.1.call-start = ((), (), s32[]{:S(2)}) async-start(), calls=%async_computation | async-start | bytes 1253376 | tf_op jit(solution)/shard_map/all_gather | solution.py:739
  8.2 7.3 %collective-permute-start = (bf16[1,4,24,192]{3,2,1,0:T(8,128)(2,1)S(1)}, bf16[1,4,24,192]{3,2,1,0:T(8,128)(2,1)S(1)}, u32[]{:S(2)}, u32[]{:S(2)}) collective-permute-start(bf16[1,4,24,192]{3,2,1,0:T(8,128)(2,1)S(1)} %convert_bitcast_fusion), channel_id=1, source_target_pairs={{0,16},{2,18},{4,20},{6,22},{8,24},{10,26},{12,28},{14,30},{16,0},... | collective-permute-start | bytes 110600 | tf_op jit(solution)/shard_map/ppermute | solution.py:639
  14.6 24.8 %collective-permute-start.6 = (bf16[9,768]{1,0:T(8,128)(2,1)S(1)}, bf16[9,768]{1,0:T(8,128)(2,1)S(1)}, u32[]{:S(2)}, u32[]{:S(2)}) collective-permute-start(bf16[9,768]{1,0:T(8,128)(2,1)S(1)} %convert_element_type.305), channel_id=1, source_target_pairs={{0,1},{1,0},{2,3},{3,2},{4,5},{5,4},{6,7},{7,6},{8,9},{9,8},{10,11... | collective-permute-start | bytes 41480 | tf_op jit(solution)/shard_map/ppermute | solution.py:639
  16.4 5.3 %collective-permute-start.1 = (bf16[2,4,24,192]{3,2,1,0:T(8,128)(2,1)S(1)}, bf16[2,4,24,192]{3,2,1,0:T(8,128)(2,1)S(1)}, u32[]{:S(2)}, u32[]{:S(2)}) collective-permute-start(bf16[2,4,24,192]{3,2,1,0:T(8,128)(2,1)S(1)} %maximum_bitcast_fusion.1), channel_id=1, source_target_pairs={{0,8},{2,10},{4,12},{6,14},{8,0},{10,2},{12,4},{14,6},{16,24},{18,... | collective-permute-start | bytes 221192 | tf_op jit(solution)/shard_map/ppermute | solution.py:639
  21.8 7.1 %collective-permute-start.2 = (bf16[4,4,24,192]{3,2,1,0:T(8,128)(2,1)S(1)}, bf16[4,4,24,192]{3,2,1,0:T(8,128)(2,1)S(1)}, u32[]{:S(2)}, u32[]{:S(2)}) collective-permute-start(bf16[4,4,24,192]{3,2,1,0:T(8,128)(2,1)S(1)} %bitcast.151), channel_id=1, source_target_pairs={{0,4},{2,6},{4,0},{6,2},{8,12},{10,14},{12,8},{14,10},{16,20},{18,... | collective-permute-start | bytes 442376 | tf_op jit(solution)/shard_map/ppermute | solution.py:639
  24.6 14.5 %copy-start.14 = (s32[3,8,128]{2,1,0:T(8,128)}, s32[3,8,128]{2,1,0:T(8,128)S(1)}, u32[]{:S(2)}) copy-start(s32[3,8,128]{2,1,0:T(8,128)S(1)} %scatter.9.image_ref) | copy-start | bytes 36868
  29.0 10.0 %collective-permute-start.3 = (bf16[8,4,24,192]{3,2,1,0:T(8,128)(2,1)S(1)}, bf16[8,4,24,192]{3,2,1,0:T(8,128)(2,1)S(1)}, u32[]{:S(2)}, u32[]{:S(2)}) collective-permute-start(bf16[8,4,24,192]{3,2,1,0:T(8,128)(2,1)S(1)} %bitcast.145), channel_id=1, source_target_pairs={{0,2},{2,0},{4,6},{6,4},{8,10},{10,8},{12,14},{14,12},{16,18},{18,... | collective-permute-start | bytes 884744 | tf_op jit(solution)/shard_map/ppermute | solution.py:639
  39.3 2.4 collective-permute-start.4
  91.7 4.0 %copy-start.6 = (bf16[2,384,768]{2,1,0:T(8,128)(2,1)S(1)}, bf16[2,384,768]{2,1,0:T(8,128)(2,1)}, u32[]{:S(2)}) copy-start(bf16[2,384,768]{2,1,0:T(8,128)(2,1)} %all-gather.2.cloned.1.call-done) | copy-start | bytes 3538948
  91.7 4.0 %collective-permute-start.5 = (bf16[2,384,768]{2,1,0:T(8,128)(2,1)}, bf16[2,384,768]{2,1,0:T(8,128)(2,1)S(1)}, u32[]{:S(2)}, u32[]{:S(2)}) collective-permute-start(bf16[2,384,768]{2,1,0:T(8,128)(2,1)} %all-gather.2.cloned.1.call-done), channel_id=1, source_target_pairs={{0,1},{1,0},{2,3},{3,2},{4,5},{5,4},{6,7},{7,6},{8,9},{9,8},{10,11... | collective-permute-start | bytes 3538952 | tf_op jit(solution)/shard_map/ppermute | solution.py:639
  204.9 24.9 %collective-permute-start.7 = (bf16[788,768]{1,0:T(8,128)(2,1)}, bf16[788,768]{1,0:T(8,128)(2,1)S(1)}, u32[]{:S(2)}, u32[]{:S(2)}) collective-permute-start(bf16[788,768]{1,0:T(8,128)(2,1)} %pad_maximum_fusion.1), channel_id=1, source_target_pairs={{0,1},{1,0},{2,3},{3,2},{4,5},{5,4},{6,7},{7,6},{8,9},{9,8},{10,11... | collective-permute-start | bytes 3631112 | tf_op jit(solution)/shard_map/ppermute | solution.py:639
  230.2 1.4 copy-start.2
  232.6 42.7 %collective-permute-start.8 = (bf16[404,768]{1,0:T(8,128)(2,1)}, bf16[404,768]{1,0:T(8,128)(2,1)S(1)}, u32[]{:S(2)}, u32[]{:S(2)}) collective-permute-start(bf16[404,768]{1,0:T(8,128)(2,1)} %pad_maximum_fusion.4), channel_id=1, source_target_pairs={{0,2},{2,0},{4,6},{6,4},{8,10},{10,8},{12,14},{14,12},{16,18},{18,... | collective-permute-start | bytes 1861640 | tf_op jit(solution)/shard_map/ppermute | solution.py:639
  234.4 40.9 %copy-start.3 = (f32[8,2,48,768]{3,2,1,0:T(8,128)S(1)}, f32[8,2,48,768]{3,2,1,0:T(8,128)}, u32[]{:S(2)}) copy-start(f32[8,2,48,768]{3,2,1,0:T(8,128)} %copy-done.2) | copy-start | bytes 7077892
  275.6 10.7 %collective-permute-start.14 = (bf16[212,768]{1,0:T(8,128)(2,1)S(1)}, bf16[212,768]{1,0:T(8,128)(2,1)S(1)}, u32[]{:S(2)}, u32[]{:S(2)}) collective-permute-start(bf16[212,768]{1,0:T(8,128)(2,1)S(1)} %pad_maximum_fusion.6), channel_id=1, source_target_pairs={{0,4},{2,6},{4,0},{6,2},{8,12},{10,14},{12,8},{14,10},{16,20},{18,... | collective-permute-start | bytes 976904 | tf_op jit(solution)/shard_map/ppermute | solution.py:639
  286.4 2.8 copy-start.22
  286.5 6.2 %collective-permute-start.15 = (bf16[116,768]{1,0:T(8,128)(2,1)S(1)}, bf16[116,768]{1,0:T(8,128)(2,1)S(1)}, u32[]{:S(2)}, u32[]{:S(2)}) collective-permute-start(bf16[116,768]{1,0:T(8,128)(2,1)S(1)} %pad_maximum_fusion.8), channel_id=1, source_target_pairs={{0,8},{2,10},{4,12},{6,14},{8,0},{10,2},{12,4},{14,6},{16,24},{18,... | collective-permute-start | bytes 534536 | tf_op jit(solution)/shard_map/ppermute | solution.py:639
  289.0 4.0 %collective-permute-start.9 = (bf16[1536,192]{0,1:T(8,128)(2,1)S(1)}, bf16[1536,192]{0,1:T(8,128)(2,1)}, u32[]{:S(2)}, u32[]{:S(2)}) collective-permute-start(bf16[1536,192]{0,1:T(8,128)(2,1)S(1)} %copy.82), channel_id=1, source_target_pairs={{0,1},{1,0},{2,3},{3,2},{4,5},{5,4},{6,7},{7,6},{8,9},{9,8},{10,11... | collective-permute-start | bytes 1769480 | tf_op jit(solution)/shard_map/ppermute | solution.py:639
  292.9 7.0 %collective-permute-start.16 = (bf16[68,768]{1,0:T(8,128)(2,1)S(1)}, bf16[68,768]{1,0:T(8,128)(2,1)S(1)}, u32[]{:S(2)}, u32[]{:S(2)}) collective-permute-start(bf16[68,768]{1,0:T(8,128)(2,1)S(1)} %pad_maximum_fusion.9), channel_id=1, source_target_pairs={{0,16},{2,18},{4,20},{6,22},{8,24},{10,26},{12,28},{14,30},{16,0},... | collective-permute-start | bytes 313352 | tf_op jit(solution)/shard_map/ppermute | solution.py:639
  296.8 7.6 %collective-permute-start.10 = (bf16[768,192]{0,1:T(8,128)(2,1)S(1)}, bf16[768,192]{0,1:T(8,128)(2,1)}, u32[]{:S(2)}, u32[]{:S(2)}) collective-permute-start(bf16[768,192]{0,1:T(8,128)(2,1)S(1)} %copy.85), channel_id=1, source_target_pairs={{0,2},{2,0},{4,6},{6,4},{8,10},{10,8},{12,14},{14,12},{16,18},{18,... | collective-permute-start | bytes 884744 | tf_op jit(solution)/shard_map/ppermute | solution.py:639
  305.5 2.0 copy-start.5
  305.5 2.0 copy-start.16
  305.6 2.0 copy-start.17
  305.9 5.2 %collective-permute-start.11 = (bf16[384,192]{0,1:T(8,128)(2,1)S(1)}, bf16[384,192]{0,1:T(8,128)(2,1)S(1)}, u32[]{:S(2)}, u32[]{:S(2)}) collective-permute-start(bf16[384,192]{0,1:T(8,128)(2,1)S(1)} %copy.87), channel_id=1, source_target_pairs={{0,4},{2,6},{4,0},{6,2},{8,12},{10,14},{12,8},{14,10},{16,20},{18,... | collective-permute-start | bytes 442376 | tf_op jit(solution)/shard_map/ppermute | solution.py:639
  307.8 33.2 %copy-start.8 = (f32[2,24,768]{2,1,0:T(8,128)}, f32[2,24,768]{2,1,0:T(8,128)S(1)}, u32[]{:S(2)}) copy-start(f32[2,24,768]{2,1,0:T(8,128)S(1)} %get-tuple-element.111) | copy-start | bytes 442372
  307.8 33.2 %copy-start.9 = (f32[2,24,768]{2,1,0:T(8,128)}, f32[2,24,768]{2,1,0:T(8,128)S(1)}, u32[]{:S(2)}) copy-start(f32[2,24,768]{2,1,0:T(8,128)S(1)} %get-tuple-element.112) | copy-start | bytes 442372
  307.8 11.2 %copy-start.20 = (f32[9,768]{1,0:T(8,128)S(1)}, f32[9,768]{1,0:T(8,128)}, u32[]{:S(2)}) copy-start(f32[9,768]{1,0:T(8,128)} %param.31) | copy-start | bytes 82948
  307.8 11.2 %copy-start.21 = (f32[9,768]{1,0:T(8,128)S(1)}, f32[9,768]{1,0:T(8,128)}, u32[]{:S(2)}) copy-start(f32[9,768]{1,0:T(8,128)} %param.32) | copy-start | bytes 82948
  307.9 13.8 %copy-start.4 = (f32[4,24,192]{2,1,0:T(8,128)S(1)}, f32[4,24,192]{2,1,0:T(8,128)}, u32[]{:S(2)}) copy-start(f32[4,24,192]{2,1,0:T(8,128)} %param.24) | copy-start | bytes 221188
  307.9 13.8 %copy-start.18 = (f32[4,24,192]{2,1,0:T(8,128)S(1)}, f32[4,24,192]{2,1,0:T(8,128)}, u32[]{:S(2)}) copy-start(f32[4,24,192]{2,1,0:T(8,128)} %param.25) | copy-start | bytes 221188
  307.9 13.8 %copy-start.19 = (f32[4,24,192]{2,1,0:T(8,128)S(1)}, f32[4,24,192]{2,1,0:T(8,128)}, u32[]{:S(2)}) copy-start(f32[4,24,192]{2,1,0:T(8,128)} %param.26) | copy-start | bytes 221188
  311.3 5.2 %collective-permute-start.12 = (bf16[192,192]{1,0:T(8,128)(2,1)S(1)}, bf16[192,192]{1,0:T(8,128)(2,1)S(1)}, u32[]{:S(2)}, u32[]{:S(2)}) collective-permute-start(bf16[192,192]{1,0:T(8,128)(2,1)S(1)} %bitcast.159), channel_id=1, source_target_pairs={{0,8},{2,10},{4,12},{6,14},{8,0},{10,2},{12,4},{14,6},{16,24},{18,... | collective-permute-start | bytes 221192 | tf_op jit(solution)/shard_map/ppermute | solution.py:639
  316.5 26.6 %copy-start.1 = (s32[6,1024]{1,0:T(8,128)S(1)}, s32[6,1024]{1,0:T(8,128)}, u32[]{:S(2)}) copy-start(s32[6,1024]{1,0:T(8,128)} %param.22) | copy-start | bytes 73732
  316.5 26.0 %copy-start.15 = (f32[4,384]{1,0:T(4,128)S(1)}, f32[4,384]{1,0:T(4,128)}, u32[]{:S(2)}) copy-start(f32[4,384]{1,0:T(4,128)} %norm_ref.7) | copy-start | bytes 18436
  316.5 26.0 %copy-start.23 = (f32[4,384]{1,0:T(4,128)S(1)}, f32[4,384]{1,0:T(4,128)}, u32[]{:S(2)}) copy-start(f32[4,384]{1,0:T(4,128)} %param.34) | copy-start | bytes 18436
  316.5 26.0 %copy-start.24 = (f32[4,384]{1,0:T(4,128)S(1)}, f32[4,384]{1,0:T(4,128)}, u32[]{:S(2)}) copy-start(f32[4,384]{1,0:T(4,128)} %param.35) | copy-start | bytes 18436
  316.6 5.1 %collective-permute-start.13 = (bf16[96,192]{1,0:T(8,128)(2,1)S(1)}, bf16[96,192]{1,0:T(8,128)(2,1)S(1)}, u32[]{:S(2)}, u32[]{:S(2)}) collective-permute-start(bf16[96,192]{1,0:T(8,128)(2,1)S(1)} %fusion.14), channel_id=1, source_target_pairs={{0,16},{2,18},{4,20},{6,22},{8,24},{10,26},{12,28},{14,30},{16,0},... | collective-permute-start | bytes 110600 | tf_op jit(solution)/shard_map/ppermute | solution.py:639
  319.6 23.5 %copy-start.12 = (f32[9,768]{1,0:T(8,128)}, f32[9,768]{1,0:T(8,128)S(1)}, u32[]{:S(2)}) copy-start(f32[9,768]{1,0:T(8,128)S(1)} %get-tuple-element.113) | copy-start | bytes 82948
  319.6 23.5 %copy-start.13 = (f32[9,768]{1,0:T(8,128)}, f32[9,768]{1,0:T(8,128)S(1)}, u32[]{:S(2)}) copy-start(f32[9,768]{1,0:T(8,128)S(1)} %get-tuple-element.114) | copy-start | bytes 82948
  321.9 21.2 %copy-start.10 = (f32[4,24,192]{2,1,0:T(8,128)}, f32[4,24,192]{2,1,0:T(8,128)S(1)}, u32[]{:S(2)}) copy-start(f32[4,24,192]{2,1,0:T(8,128)S(1)} %get-tuple-element.109) | copy-start | bytes 221188
  321.9 21.2 %copy-start.11 = (f32[4,24,192]{2,1,0:T(8,128)}, f32[4,24,192]{2,1,0:T(8,128)S(1)}, u32[]{:S(2)}) copy-start(f32[4,24,192]{2,1,0:T(8,128)S(1)} %get-tuple-element.110) | copy-start | bytes 221188
  322.0 1.2 collective-permute-start.17
  323.3 3.7 %collective-permute-start.18 = (f32[8,384]{1,0:T(8,128)S(1)}, f32[8,384]{1,0:T(8,128)S(1)}, u32[]{:S(2)}, u32[]{:S(2)}) collective-permute-start(f32[8,384]{1,0:T(8,128)S(1)} %fusion.23), channel_id=1, source_target_pairs={{0,2},{2,0},{4,6},{6,4},{8,10},{10,8},{12,14},{14,12},{16,18},{18,... | collective-permute-start | bytes 36872 | tf_op jit(solution)/shard_map/ppermute | solution.py:639
  327.0 3.7 %collective-permute-start.19 = (f32[8,384]{1,0:T(8,128)S(1)}, f32[8,384]{1,0:T(8,128)S(1)}, u32[]{:S(2)}, u32[]{:S(2)}) collective-permute-start(f32[8,384]{1,0:T(8,128)S(1)} %add.304), channel_id=1, source_target_pairs={{0,4},{2,6},{4,0},{6,2},{8,12},{10,14},{12,8},{14,10},{16,20},{18,... | collective-permute-start | bytes 36872 | tf_op jit(solution)/shard_map/ppermute | solution.py:639
  330.7 3.7 %collective-permute-start.20 = (f32[8,384]{1,0:T(8,128)S(1)}, f32[8,384]{1,0:T(8,128)S(1)}, u32[]{:S(2)}, u32[]{:S(2)}) collective-permute-start(f32[8,384]{1,0:T(8,128)S(1)} %add.305), channel_id=1, source_target_pairs={{0,8},{2,10},{4,12},{6,14},{8,0},{10,2},{12,4},{14,6},{16,24},{18,... | collective-permute-start | bytes 36872 | tf_op jit(solution)/shard_map/ppermute | solution.py:639
  334.4 4.6 %collective-permute-start.21 = (f32[8,384]{1,0:T(8,128)S(1)}, f32[8,384]{1,0:T(8,128)S(1)}, u32[]{:S(2)}, u32[]{:S(2)}) collective-permute-start(f32[8,384]{1,0:T(8,128)S(1)} %add.306), channel_id=1, source_target_pairs={{0,16},{2,18},{4,20},{6,22},{8,24},{10,26},{12,28},{14,30},{16,0},... | collective-permute-start | bytes 36872 | tf_op jit(solution)/shard_map/ppermute | solution.py:639
  (1 other events, 0.8 us)
Sparse Core Ops, SparseCore 0:
  13.9 56.3 all-gather.1

commit v3 on v2

v3 whole, which is shorter than its diff:
```python
import functools
import jax
import jax.numpy as jnp
from jax import lax
from jax.experimental import pallas as pl
from jax.experimental.pallas import tpu as pltpu
from jax.sharding import PartitionSpec as P

HEAD_DIM = 64
GRID_W = 16
STEP = 10
IMAGES = 8

NORM_EPS = 1e-06
BETA_ONE = 0.9
BETA_TWO = 0.999
ADAM_EPS = 1e-06
DECAY = 0.01
RATE = 0.5
LOG2E = 1.4426950408889634
LN2 = 0.6931471805599453
BIG = 2.0**100
GELU_ONE = 0.7978845608028654
GELU_TWO = 0.044715
GELU_S = (GELU_ONE * GELU_TWO) ** (1.0 / 3.0)
GELU_A = GELU_ONE / GELU_S
ACT_SCALE = 0.5 / GELU_S
EXTRA = 32
TILE = 128
LANES = 128
STRIDE = GRID_W + 8
VMEM_BYTES = 60 * 1024 * 1024

f32 = jnp.float32
bf16 = jnp.bfloat16
NN = (((1,), (0,)), ((), ()))
NT = (((1,), (1,)), ((), ()))
TN = (((0,), (0,)), ((), ()))


def dot(left, right, dims=NN):
    return lax.dot_general(left, right, dims, preferred_element_type=f32)


def widths_for(length):
    return [w for w in (256, 384, 512, 768) if w < length] + [length]


def norm_parts(values):
    average = jnp.mean(values, axis=-1, keepdims=True)
    centered = values - average
    inverse = lax.rsqrt(jnp.mean(centered * centered, axis=-1, keepdims=True) + NORM_EPS)
    return centered * inverse, inverse


def norm_back(upstream, gain_row, unit_rows, inverse):
    grad_unit = upstream * gain_row
    first_term = jnp.mean(grad_unit, axis=-1, keepdims=True)
    second_term = jnp.mean(grad_unit * unit_rows, axis=-1, keepdims=True)
    return inverse * (grad_unit - first_term - unit_rows * second_term)


def fold_rows(values):
    rows, columns = values.shape
    return jnp.sum(values.reshape(rows // 8, 8, columns), axis=0)


def pair_columns(flat):
    empty = jnp.zeros((HEAD_DIM, LANES), flat.dtype)
    return jnp.concatenate(
        [jnp.concatenate([flat[:HEAD_DIM], empty], axis=0), jnp.concatenate([empty, flat[HEAD_DIM:]], axis=0)], axis=1
    )


def pair_rows(both):
    return jnp.concatenate([both[:HEAD_DIM, :LANES], both[HEAD_DIM:, LANES:]], axis=0)


def fold_max(values):
    pieces = [values[at : at + 64] for at in range(0, values.shape[0], 64)]
    while len(pieces) > 1:
        pieces = [jnp.maximum(a, b) for a, b in zip(pieces[::2], pieces[1::2])] + ([pieces[-1]] if len(pieces) % 2 else [])
    top = pieces[0]
    top = jnp.maximum(top[:32], top[32:])
    top = jnp.maximum(top[:16], top[16:])
    return jnp.max(jnp.maximum(top[:8], top[8:]), axis=0, keepdims=True)


def three_parts(value, part):
    high = value.astype(bf16).astype(f32)
    rest = value - high
    middle = rest.astype(bf16).astype(f32)
    return jnp.where(part == 0, high, jnp.where(part == 1, middle, rest - middle))


def image_tags(image_ref, start, rows):
    place = start + lax.broadcasted_iota(jnp.int32, (rows, LANES), 0)
    inside = (place >= image_ref[0, 0:1, :]) & (place < image_ref[0, 1:2, :])
    return jnp.where(inside, 1.0, 0.0).astype(bf16)


def attn_forward_kernel(
    start_ref, class_ref, count_ref, tokens_ref, w_ref, norm_ref, image_ref,
    middle_ref, qkv_ref, context_ref, ext_ref,
    tag_ref, normed_ref, qt_ref, vt_ref,
):
    row = pl.program_id(0)
    length, width = tokens_ref.shape
    pairs = width // LANES
    big = 256
    gain, bias = norm_ref[0:1, :], norm_ref[1:2, :]

    def prepare(step, carry):
        rows = pl.ds(pl.multiple_of(step * big, big), big)
        unit, _ = norm_parts(tokens_ref[rows, :].astype(f32))
        normed_ref[rows, :] = (unit * gain + bias).astype(bf16)
        tag_ref[rows, :] = image_tags(image_ref, step * big, big)
        return carry

    lax.fori_loop(0, length // big, prepare, 0)
    queries = (dot(normed_ref[...], w_ref[0]) * (HEAD_DIM**-0.5 * LOG2E)).astype(bf16)
    qkv_ref[:, :width] = queries
    qt_ref[...] = jnp.transpose(queries)
    qkv_ref[:, width : 2 * width] = dot(normed_ref[...], w_ref[1]).astype(bf16)
    values = dot(normed_ref[...], w_ref[2]).astype(bf16)
    qkv_ref[:, 2 * width :] = values
    vt_ref[...] = jnp.transpose(values)

    def tile(step, carry):
        q0 = pl.multiple_of(step * TILE, TILE)
        here = pl.ds(q0, TILE)
        place = q0 + lax.broadcasted_iota(jnp.int32, (IMAGES, LANES), 1)
        inside = (place >= image_ref[0, 8 : 8 + IMAGES, :]) & (place < image_ref[0, 16 : 16 + IMAGES, :])
        mask = jnp.where(inside, 0.0, -BIG)
        mask_low = jnp.concatenate([mask, jnp.zeros((LANES - IMAGES, LANES), f32)], axis=0).astype(bf16)
        ext_rows = lax.broadcasted_iota(jnp.int32, (EXTRA - IMAGES, LANES), 0)

        def attend(window):
            there = pl.ds(pl.multiple_of(start_ref[row, step], LANES), window)
            tags = tag_ref[there, :]
            ones = jnp.ones((GRID_W, window), bf16)
            extra = jnp.zeros((EXTRA - IMAGES, LANES), f32)
            slices = [slice(p * LANES, (p + 1) * LANES) for p in range(pairs)]
            masks = jnp.concatenate([mask_low, mask_low], axis=1)
            scores, tops, exponents, mixes = [], [], [], []
            for p, at in enumerate(slices):
                keys = qkv_ref[there, width + p * LANES : width + (p + 1) * LANES]
                right = jnp.concatenate([pair_columns(qt_ref[at, here]), masks], axis=0)
                scores.append(dot(jnp.concatenate([keys, tags], axis=1), right))
            for p in range(pairs):
                tops.append(fold_max(scores[p]))
                exponents.append(jnp.exp2(scores[p] - tops[p]).astype(bf16))
            for p, at in enumerate(slices):
                mixes.append(dot(jnp.concatenate([vt_ref[at, there], ones], axis=0), exponents[p]))
            for p, at in enumerate(slices):
                mixed = mixes[p]
                total = mixed[LANES : LANES + 1, :]
                minus_lse = -(tops[p] + jnp.log(total) * LOG2E)
                scale = 1.0 / total
                lane = lax.broadcasted_iota(jnp.int32, (1, 2 * TILE), 1)
                head = 2 * p + jnp.where(lane < TILE, 0, 1)
                scale = jnp.where(head < count_ref[row], scale, 0.0)
                context_ref[here, at] = jnp.transpose(pair_rows(mixed[:LANES] * scale)).astype(bf16)
                for h in range(2):
                    value = minus_lse[:, h * TILE : (h + 1) * TILE]
                    first = 6 * p + 3 * h
                    extra = jnp.where(
                        (ext_rows >= first) & (ext_rows < first + 3), three_parts(value, ext_rows - first), extra
                    )
            ext_ref[:, here] = jnp.concatenate([mask, extra], axis=0).astype(bf16)

        for index, window in enumerate(widths_for(length)):
            pl.when(class_ref[row, step] == index)(functools.partial(attend, window))
        return carry

    lax.fori_loop(0, length // TILE, tile, 0)
    middle_ref[...] = tokens_ref[...].astype(f32) + dot(context_ref[...], w_ref[3], NT)


def attn_forward(starts, classes, counts, tokens, attn_use, norm_w, images):
    rows_all, width = tokens.shape
    row_count = counts.shape[0]
    length = rows_all // row_count
    by_row = lambda columns: pl.BlockSpec((length, columns), lambda r, *_: (r, 0))
    return pl.pallas_call(
        attn_forward_kernel,
        grid_spec=pltpu.PrefetchScalarGridSpec(
            num_scalar_prefetch=3,
            grid=(row_count,),
            in_specs=[
                by_row(width),
                pl.BlockSpec(attn_use.shape, lambda r, *_: (0, 0, 0)),
                pl.BlockSpec(norm_w.shape, lambda r, *_: (0, 0)),
                pl.BlockSpec((1, 24, LANES), lambda r, *_: (r, 0, 0)),
            ],
            out_specs=[
                by_row(width), by_row(3 * width), by_row(width), pl.BlockSpec((EXTRA, length), lambda r, *_: (r, 0))
            ],
            scratch_shapes=[
                pltpu.VMEM((length, LANES), bf16),
                pltpu.VMEM((length, width), bf16),
                pltpu.VMEM((width, length), bf16),
                pltpu.VMEM((width, length), bf16),
            ],
        ),
        out_shape=[
            jax.ShapeDtypeStruct((rows_all, width), f32),
            jax.ShapeDtypeStruct((rows_all, 3 * width), bf16),
            jax.ShapeDtypeStruct((rows_all, width), bf16),
            jax.ShapeDtypeStruct((row_count * EXTRA, length), bf16),
        ],
        compiler_params=pltpu.CompilerParams(vmem_limit_bytes=VMEM_BYTES),
    )(starts, classes, counts, tokens, attn_use, norm_w, images)


def attn_backward_kernel(
    first, final, start_ref, class_ref, count_ref, rank_ref, tokens_ref, middle_grad_ref, qkv_ref, context_ref, ext_ref, w_ref, norm_ref,
    image_ref, *refs,
):
    sums = None
    if first:
        sums, refs = refs[1:3], refs[3:]
    sent = None
    if final:
        tokens_grad_ref, keep_ref, send_ref, norm_grad_ref, *scratch, w_grad_ref = refs
        sent = (keep_ref, send_ref)
    else:
        tokens_grad_ref, w_grad_ref, norm_grad_ref, *scratch = refs
    attn_backward_row(
        first, sums, sent, start_ref, class_ref, count_ref, rank_ref, tokens_ref, middle_grad_ref, qkv_ref, context_ref, ext_ref, w_ref,
        norm_ref, image_ref, tokens_grad_ref, w_grad_ref, norm_grad_ref, *scratch,
    )


def attn_backward_row(
    first, sums, sent, start_ref, class_ref, count_ref, rank_ref, tokens_ref, middle_grad_ref, qkv_ref, context_ref, ext_ref, w_ref,
    norm_ref, image_ref, tokens_grad_ref, w_grad_ref, norm_grad_ref,
    tag_ref, up_ref, delta_ref, normed_ref, dq_ref, dk_ref, dv_ref, low_ref, proj_ref, qt_ref, kt_ref, upt_ref, upstream_ref,
):
    step_at = pl.program_id(0)
    row = first + step_at
    length, width = tokens_ref.shape
    pairs = width // LANES
    big = 256
    gain, bias = norm_ref[0:1, :], norm_ref[1:2, :]

    @pl.when(step_at == 0)
    def _():
        for n, ref in enumerate((w_grad_ref, norm_grad_ref)):
            ref[...] = sums[n][...] if sums else jnp.zeros_like(ref)

    target = lax.broadcasted_iota(jnp.int32, (EXTRA, width), 0) - IMAGES
    source = lax.broadcasted_iota(jnp.int32, (EXTRA, width), 1) // HEAD_DIM * 3
    collect = jnp.where((target >= source) & (target < source + 3), -1.0, 0.0).astype(bf16)
    active = jnp.where(
        lax.broadcasted_iota(jnp.int32, (1, width), 1) // HEAD_DIM < count_ref[row], 1.0, 0.0
    )

    def prepare(step, carry):
        rows = pl.ds(pl.multiple_of(step * big, big), big)
        unit, _ = norm_parts(tokens_ref[rows, :].astype(f32))
        normed_ref[rows, :] = (unit * gain + bias).astype(bf16)
        tag_ref[rows, :] = image_tags(image_ref, step * big, big)
        low_ref[rows, :] = middle_grad_ref[rows, :].astype(bf16)
        dk_ref[rows, :] = jnp.zeros((big, width), f32)
        dv_ref[rows, :] = jnp.zeros((big, width), f32)
        return carry

    lax.fori_loop(0, length // big, prepare, 0)
    up = (dot(low_ref[...], w_ref[3]) * active).astype(bf16)
    up_ref[...] = up
    upt_ref[...] = jnp.transpose(up)
    qt_ref[...] = jnp.transpose(qkv_ref[:, :width])
    kt_ref[...] = jnp.transpose(qkv_ref[:, width : 2 * width])

    def gather(step, carry):
        rows = pl.ds(pl.multiple_of(step * big, big), big)
        product = up_ref[rows, :].astype(f32) * context_ref[rows, :].astype(f32)
        high = product.astype(bf16)
        rest = (product - high.astype(f32)).astype(bf16)
        delta = dot(collect, high, NT) + dot(collect, rest, NT)
        part = lax.rem(lax.broadcasted_iota(jnp.int32, (EXTRA, big), 0) + 3 * EXTRA - IMAGES, 3)
        delta_ref[:, rows] = three_parts(delta, part).astype(bf16)
        return carry

    lax.fori_loop(0, length // big, gather, 0)
    lane = lax.broadcasted_iota(jnp.int32, (1, LANES), 1)
    first_half = jnp.where(lane < HEAD_DIM, 1.0, 0.0).astype(bf16)
    second_half = jnp.where(lane >= HEAD_DIM, 1.0, 0.0).astype(bf16)

    def tile(step, carry):
        q0 = pl.multiple_of(step * TILE, TILE)
        here = pl.ds(q0, TILE)

        def attend(window):
            there = pl.ds(pl.multiple_of(start_ref[row, step], LANES), window)
            tags = tag_ref[there, :]
            ext = ext_ref[:, here]
            delta = delta_ref[:, here]
            at_row = lax.broadcasted_iota(jnp.int32, (EXTRA, LANES), 0)
            empty = jnp.zeros((LANES - EXTRA, 2 * TILE), bf16)

            def own(edge, masks):
                keep = (at_row >= edge) & (at_row < edge + 3)
                return jnp.where(keep | (at_row < IMAGES) if masks else keep, 1.0, 0.0).astype(bf16)

            slices = [slice(p * LANES, (p + 1) * LANES) for p in range(pairs)]
            scores, grad_probs, probs, grad_scores = [], [], [], []
            for p, at in enumerate(slices):
                keys = qkv_ref[there, width + p * LANES : width + (p + 1) * LANES]
                values = qkv_ref[there, 2 * width + p * LANES : 2 * width + (p + 1) * LANES]
                edge = IMAGES + 6 * p
                q_side = jnp.concatenate(
                    [
                        pair_columns(qt_ref[at, here]),
                        jnp.concatenate([ext * own(edge, True), ext * own(edge + 3, True)], axis=1),
                        empty,
                    ],
                    axis=0,
                )
                up_side = jnp.concatenate(
                    [
                        pair_columns(upt_ref[at, here]),
                        jnp.concatenate([delta * own(edge, False), delta * own(edge + 3, False)], axis=1),
                        empty,
                    ],
                    axis=0,
                )
                scores.append(dot(jnp.concatenate([keys, tags], axis=1), q_side))
                grad_probs.append(dot(jnp.concatenate([values, tags], axis=1), up_side))
            for p in range(pairs):
                weight = jnp.exp2(scores[p])
                probs.append(weight.astype(bf16))
                grad_scores.append((weight * grad_probs[p]).astype(bf16))
            for p, at in enumerate(slices):
                queries, ups = qkv_ref[here, at], up_ref[here, at]
                q_pair = jnp.concatenate([queries * first_half, queries * second_half], axis=0)
                up_pair = jnp.concatenate([ups * first_half, ups * second_half], axis=0)
                dv_ref[there, at] += dot(probs[p], up_pair)
                dk_ref[there, at] += dot(grad_scores[p], q_pair)
                dq = pair_rows(dot(kt_ref[at, there], grad_scores[p]))
                dq_ref[here, at] = jnp.transpose(dq * HEAD_DIM**-0.5).astype(bf16)

        for index, window in enumerate(widths_for(length)):
            pl.when(class_ref[row, step] == index)(functools.partial(attend, window))
        return carry

    lax.fori_loop(0, length // TILE, tile, 0)
    keys_grad = (dk_ref[...] * LN2).astype(bf16)
    values_grad = dv_ref[...].astype(bf16)
    proj_ref[...] = jnp.concatenate([dq_ref[...], keys_grad, values_grad], axis=1)
    w_cat = jnp.concatenate([w_ref[0], w_ref[1], w_ref[2]], axis=1)
    upstream_ref[...] = dot(proj_ref[...], w_cat, NT)

    def finish(step, carry):
        rows = pl.ds(pl.multiple_of(step * big, big), big)
        upstream = upstream_ref[rows, :]
        unit, inverse = norm_parts(tokens_ref[rows, :].astype(f32))
        tokens_grad_ref[rows, :] = middle_grad_ref[rows, :] + norm_back(upstream, gain, unit, inverse)
        norm_grad_ref[0:8, :] += fold_rows(upstream * unit)
        norm_grad_ref[8:16, :] += fold_rows(upstream)
        return carry

    lax.fori_loop(0, length // big, finish, 0)
    normed_t = jnp.transpose(normed_ref[...])
    for k in range(3):
        w_grad_ref[k] += dot(normed_t, proj_ref[:, k * width : (k + 1) * width])
    w_grad_ref[3] += dot(jnp.transpose(low_ref[...]), context_ref[...])
    if sent:

        @pl.when(step_at == pl.num_programs(0) - 1)
        def _():
            for k in range(w_grad_ref.shape[0]):
                halves = w_grad_ref[k, :, : width // 2], w_grad_ref[k, :, width // 2 :]
                sent[0][k] = jnp.where(rank_ref[0] == 0, halves[0], halves[1])
                sent[1][k] = jnp.where(rank_ref[0] == 0, halves[1], halves[0]).astype(bf16)


def attn_backward(first, count, so_far, starts, classes, counts, rank, tokens, middle_grad, qkv, context, ext, attn_use, norm_w, images):
    rows_all, width = tokens.shape
    length = rows_all // counts.shape[0]
    by_row = lambda columns: pl.BlockSpec((length, columns), lambda r, *_: (first + r, 0))
    final = first + count == counts.shape[0]
    half = attn_use.shape[:2] + (width // 2,)
    halves = pl.BlockSpec(half, lambda r, *_: (0, 0, 0))
    whole = pl.BlockSpec(attn_use.shape, lambda r, *_: (0, 0, 0))
    sums = pl.BlockSpec((16, width), lambda r, *_: (0, 0))
    return pl.pallas_call(
        functools.partial(attn_backward_kernel, first, final),
        grid_spec=pltpu.PrefetchScalarGridSpec(
            num_scalar_prefetch=4,
            grid=(count,),
            in_specs=[
                by_row(width),
                by_row(width),
                by_row(3 * width),
                by_row(width),
                pl.BlockSpec((EXTRA, length), lambda r, *_: (first + r, 0)),
                whole,
                pl.BlockSpec(norm_w.shape, lambda r, *_: (0, 0)),
                pl.BlockSpec((1, 24, LANES), lambda r, *_: (first + r, 0, 0)),
            ]
            + ([pl.BlockSpec(memory_space=pl.ANY), whole, sums] if first else []),
            out_specs=[by_row(width), halves, halves, sums] if final else [by_row(width), whole, sums],
            scratch_shapes=[
                pltpu.VMEM((length, LANES), bf16),
                pltpu.VMEM((length, width), bf16),
                pltpu.VMEM((EXTRA, length), bf16),
                pltpu.VMEM((length, width), bf16),
                pltpu.VMEM((length, width), bf16),
                pltpu.VMEM((length, width), f32),
                pltpu.VMEM((length, width), f32),
                pltpu.VMEM((length, width), bf16),
                pltpu.VMEM((length, 3 * width), bf16),
                pltpu.VMEM((width, length), bf16),
                pltpu.VMEM((width, length), bf16),
                pltpu.VMEM((width, length), bf16),
                pltpu.VMEM((length, width), f32),
            ]
            + ([pltpu.VMEM(attn_use.shape, f32)] if final else []),
        ),
        out_shape=[jax.ShapeDtypeStruct((rows_all, width), f32)]
        + (
            [jax.ShapeDtypeStruct(half, f32), jax.ShapeDtypeStruct(half, bf16)]
            if final
            else [jax.ShapeDtypeStruct(attn_use.shape, f32)]
        )
        + [jax.ShapeDtypeStruct((16, width), f32)],
        input_output_aliases={12: 0} if first else {},
        compiler_params=pltpu.CompilerParams(vmem_limit_bytes=VMEM_BYTES),
    )(starts, classes, counts, rank, tokens, middle_grad, qkv, context, ext, attn_use, norm_w, images, *(so_far or ()))


def mlp_kernel(
    place_ref, rank_ref, middle_ref, out_grad_ref, w_ref, taps_ref, norm_ref,
    output_ref, middle_grad_ref, keep_ref, send_ref, taps_grad_ref, norm_grad_ref,
    w_grad_ref, normed_ref, normed_t_ref, out_grad_t_ref, out_sum_ref, up_sum_ref, tap_sum_ref,
    act_grads_ref, acts_ref, hidden_grads_ref, *buffers,
):
    row = pl.program_id(0)
    length, width = middle_ref.shape
    hidden = w_ref.shape[2]
    chunk = 2 * LANES
    big = 256
    grid_rows = length // GRID_W
    chunks = hidden // chunk
    h_refs, g_refs = buffers[:2], buffers[2:]
    gain, bias = norm_ref[2:3, :], norm_ref[3:4, :]

    @pl.when(row == 0)
    def _():
        w_grad_ref[...] = jnp.zeros_like(w_grad_ref)
        norm_grad_ref[...] = jnp.zeros_like(norm_grad_ref)
        tap_sum_ref[...] = jnp.zeros_like(tap_sum_ref)

    for ref in buffers:
        ref[...] = jnp.zeros_like(ref)

    def normalize(step, carry):
        rows = pl.ds(pl.multiple_of(step * big, big), big)
        middle = middle_ref[rows, :]
        unit, _ = norm_parts(middle)
        normed_ref[rows, :] = (unit * gain + bias).astype(bf16)
        out_sum_ref[rows, :] = jnp.zeros((big, width), f32)
        up_sum_ref[rows, :] = jnp.zeros((big, width), f32)
        return carry

    lax.fori_loop(0, length // big, normalize, 0)
    normed_t_ref[...] = jnp.transpose(normed_ref[...])
    out_grad_t_ref[...] = jnp.transpose(out_grad_ref[...])

    def lanes_of(c):
        return pl.ds(pl.multiple_of(c * chunk, chunk), chunk)

    def lanes_of(c):
        return pl.ds(pl.multiple_of(c * chunk, chunk), chunk)

    def place(r):
        return pl.multiple_of(place_ref[row, r], 8)

    def neighbours(ref, at):
        return [ref[pl.ds(at + (a * STRIDE + b), GRID_W), :] for a in (-1, 0, 1) for b in (-1, 0, 1)]

    def tall(values):
        return jnp.concatenate([values, values], axis=0)

    def total_of(terms):
        while len(terms) > 1:
            terms = [a + b for a, b in zip(terms[::2], terms[1::2])] + ([terms[-1]] if len(terms) % 2 else [])
        return terms[0]

    def taps_for(c, part, at):
        lane = pl.ds(pl.multiple_of(c * chunk + part * LANES, LANES), LANES)
        return [tall(taps_ref[at + k * 8 : at + (k + 1) * 8, lane]) for k in range(9)]

    lines = 16

    def do_chunk(c, carry):
        lanes = lanes_of(c)
        for t in range(length // big):
            rows = slice(t * big, (t + 1) * big)
            values = dot(normed_ref[rows, :], w_ref[0, :, lanes])
            for part in range(2):
                for s in range(big // GRID_W):
                    at = place(t * (big // GRID_W) + s)
                    h_refs[part][pl.ds(at, GRID_W), :] = values[
                        s * GRID_W : (s + 1) * GRID_W, part * LANES : (part + 1) * LANES
                    ]
        act_grads_ref[...] = dot(out_grad_ref[...], w_ref[1, :, lanes])

        def forward(t, carry):
            tokens_base = pl.multiple_of(t * (lines * GRID_W), lines * GRID_W)
            for part in range(2):
                taps = taps_for(c, part, 0)
                cols = slice(part * LANES, (part + 1) * LANES)
                for s in range(lines):
                    near = pl.ds(pl.multiple_of(tokens_base + s * GRID_W, GRID_W), GRID_W)
                    at = place(t * lines + s)
                    x = total_of([x * tap for x, tap in zip(neighbours(h_refs[part], at), taps)])
                    square = x * x
                    value = jnp.tanh(x * (GELU_A + square))
                    gate = 1.0 + value
                    twice = x * gate
                    acts_ref[near, cols] = twice.astype(bf16)
                    slope = gate + (twice * (1.0 - value)) * (GELU_A + 3.0 * square)
                    g_refs[part][pl.ds(at, GRID_W), :] = act_grads_ref[near, cols] * slope
            return carry

        lax.fori_loop(0, grid_rows // lines, forward, 0)

        def backward(t, carry):
            tokens_base = pl.multiple_of(t * (lines * GRID_W), lines * GRID_W)
            for part in range(2):
                taps = taps_for(c, part, 72)
                lane = pl.ds(pl.multiple_of(c * chunk + part * LANES, LANES), LANES)
                cols = slice(part * LANES, (part + 1) * LANES)
                totals = [None] * 9
                for s in range(lines):
                    near = pl.ds(pl.multiple_of(tokens_base + s * GRID_W, GRID_W), GRID_W)
                    at = place(t * lines + s)
                    source = h_refs[part][pl.ds(at, GRID_W), :]
                    moved = neighbours(g_refs[part], at)[::-1]
                    for k in range(9):
                        product = source * moved[k]
                        folded = product[:8] + product[8:]
                        totals[k] = folded if totals[k] is None else totals[k] + folded
                    terms = [x * tap for x, tap in zip(moved, taps)]
                    hidden_grads_ref[near, cols] = total_of(terms).astype(bf16)
                for k in range(9):
                    tap_sum_ref[k * 8 : (k + 1) * 8, lane] += totals[k]
            return carry

        lax.fori_loop(0, grid_rows // lines, backward, 0)
        w_grad_ref[0, :, lanes] += dot(normed_t_ref[...], hidden_grads_ref[...])
        w_grad_ref[1, :, lanes] += dot(out_grad_t_ref[...], acts_ref[...])
        out_sum_ref[...] += dot(acts_ref[...], w_ref[1, :, lanes], NT)
        up_sum_ref[...] += dot(hidden_grads_ref[...], w_ref[0, :, lanes], NT)
        return carry

    lax.fori_loop(0, chunks, do_chunk, 0)

    def finish(step, carry):
        rows = pl.ds(pl.multiple_of(step * big, big), big)
        middle = middle_ref[rows, :]
        output_ref[rows, :] = (middle + ACT_SCALE * out_sum_ref[rows, :]).astype(bf16)
        upstream = 0.5 * up_sum_ref[rows, :]
        unit, inverse = norm_parts(middle)
        middle_grad_ref[rows, :] = out_grad_ref[rows, :].astype(f32) + norm_back(upstream, gain, unit, inverse)
        norm_grad_ref[0:8, :] += fold_rows(upstream * unit)
        norm_grad_ref[8:16, :] += fold_rows(upstream)
        return carry

    lax.fori_loop(0, length // big, finish, 0)

    @pl.when(row == pl.num_programs(0) - 1)
    def _():
        for k, scale in enumerate((0.5, ACT_SCALE)):
            halves = w_grad_ref[k, :, : hidden // 2], w_grad_ref[k, :, hidden // 2 :]
            keep_ref[k] = scale * jnp.where(rank_ref[0] == 0, halves[0], halves[1])
            send_ref[k] = (scale * jnp.where(rank_ref[0] == 0, halves[1], halves[0])).astype(bf16)
        taps_grad_ref[...] = jnp.zeros_like(taps_grad_ref)
        for k in range(9):
            total = jnp.sum(tap_sum_ref[k * 8 : (k + 1) * 8, :], axis=0, keepdims=True)
            taps_grad_ref[k : k + 1, :] = 0.5 * total


def mlp_layer(places, rank, middle, out_grad, mlp_use, taps, norm_w):
    rows_all, width = middle.shape
    row_count = places.shape[0]
    length = rows_all // row_count
    hidden = mlp_use.shape[2]
    half = mlp_use.shape[:2] + (hidden // 2,)
    by_row = lambda columns: pl.BlockSpec((length, columns), lambda r, *_: (r, 0))
    slots = (length // GRID_W + IMAGES + 2) * STRIDE
    return pl.pallas_call(
        mlp_kernel,
        grid_spec=pltpu.PrefetchScalarGridSpec(
            num_scalar_prefetch=2,
            grid=(row_count,),
            in_specs=[
                by_row(width),
                by_row(width),
                pl.BlockSpec(mlp_use.shape, lambda r, *_: (0, 0, 0)),
                pl.BlockSpec(taps.shape, lambda r, *_: (0, 0)),
                pl.BlockSpec(norm_w.shape, lambda r, *_: (0, 0)),
            ],
            out_specs=[
                by_row(width),
                by_row(width),
                pl.BlockSpec(half, lambda r, *_: (0, 0, 0)),
                pl.BlockSpec(half, lambda r, *_: (0, 0, 0)),
                pl.BlockSpec((16, hidden), lambda r, *_: (0, 0)),
                pl.BlockSpec((16, width), lambda r, *_: (0, 0)),
            ],
            scratch_shapes=[
                pltpu.VMEM(mlp_use.shape, f32),
                pltpu.VMEM((length, width), bf16),
                pltpu.VMEM((width, length), bf16),
                pltpu.VMEM((width, length), bf16),
                pltpu.VMEM((length, width), f32),
                pltpu.VMEM((length, width), f32),
                pltpu.VMEM((9 * 8, hidden), f32),
                pltpu.VMEM((length, 2 * LANES), f32),
                pltpu.VMEM((length, 2 * LANES), bf16),
                pltpu.VMEM((length, 2 * LANES), bf16),
            ]
            + [pltpu.VMEM((slots, LANES), f32)] * 4,
        ),
        out_shape=[
            jax.ShapeDtypeStruct((rows_all, width), bf16),
            jax.ShapeDtypeStruct((rows_all, width), f32),
            jax.ShapeDtypeStruct(half, f32),
            jax.ShapeDtypeStruct(half, bf16),
            jax.ShapeDtypeStruct((16, hidden), f32),
            jax.ShapeDtypeStruct((16, width), f32),
        ],
        compiler_params=pltpu.CompilerParams(vmem_limit_bytes=VMEM_BYTES),
    )(places, rank, middle, out_grad, mlp_use, taps, norm_w)


def attention_plan(segments):
    row_count, length = segments.shape
    tiles = segments.reshape(row_count, length // TILE, TILE)
    first, last = tiles[:, :, 0], tiles[:, :, -1]
    ids = jnp.arange(IMAGES, dtype=jnp.int32)
    begins = jnp.sum((segments[:, None, :] < ids[None, :, None]).astype(jnp.int32), axis=-1)
    ends = jnp.sum((segments[:, None, :] <= ids[None, :, None]).astype(jnp.int32), axis=-1)
    low_end = jnp.sum(jnp.where(first[:, :, None] == ids, begins[:, None, :], 0), axis=-1) // LANES * LANES
    high_end = jnp.sum(jnp.where(last[:, :, None] == ids, ends[:, None, :], 0), axis=-1)
    widths = widths_for(length)
    classes = sum(((high_end - low_end) > w).astype(jnp.int32) for w in widths[:-1])
    chosen = jnp.full_like(classes, widths[-1])
    for index, w in enumerate(widths):
        chosen = jnp.where(classes == index, w, chosen)
    starts = jnp.minimum(low_end, length - chosen)
    used = jnp.zeros((row_count, EXTRA - IMAGES), jnp.int32)
    unused = jnp.zeros((row_count, LANES - EXTRA), jnp.int32)
    first_lane = jnp.concatenate([begins, used, unused], axis=1)
    end_lane = jnp.concatenate([ends, used + length, unused], axis=1)
    by_lane = jnp.pad(jnp.stack([first_lane, end_lane], axis=1), ((0, 0), (0, 6), (0, 0)))
    by_image = jnp.broadcast_to(jnp.concatenate([begins, ends], axis=1)[:, :, None], (row_count, 2 * IMAGES, LANES))
    return starts, classes, jnp.concatenate([by_lane, by_image], axis=1)


def spread_taps(conv_use):
    taps = conv_use.astype(f32)
    own = (jnp.arange(9) == 4).astype(f32)[:, None]
    taps = jnp.repeat(taps + own, 8, axis=0)
    return jnp.concatenate([taps * GELU_S, taps], axis=0)


def line_places(segments):
    ids = segments[:, ::GRID_W]
    return (jnp.arange(ids.shape[1], dtype=jnp.int32) + ids + 1) * STRIDE + 8


def bits_of(size):
    bits = []
    b = 1
    while b < size:
        bits.append(b)
        b *= 2
    return bits


def swap(values, axis, size, bit):
    return lax.ppermute(values, axis, [(i, i ^ bit) for i in range(size)])


def gather_lines(shard, size):
    place = lax.axis_index("dp")
    bits = bits_of(size)
    groups = [bits[at : at + 2] for at in range(0, len(bits), 2)]
    held = shard[None]
    for group in reversed(groups):
        steps = range(1 << len(group))
        found = [held if step == 0 else swap(held, "dp", size, step * group[0]) for step in steps]
        mine = (place // group[0]) % len(steps)
        ordered = []
        for target in steps:
            value = found[0]
            for step in steps[1:]:
                value = jnp.where((mine ^ step) == target, found[step], value)
            ordered.append(value)
        held = jnp.stack(ordered, axis=1).reshape((-1,) + shard.shape)
    return held


def join_columns(mine, other, rank):
    first = jnp.where(rank == 0, mine, other)
    second = jnp.where(rank == 0, other, mine)
    return jnp.concatenate([first, second], axis=-1)


def gather_weights(shard, size, rank):
    count, part, columns = shard.shape
    held = gather_lines(shard, size)
    full = join_columns(held, swap(held, "head", 2, 1), rank)
    return jnp.moveaxis(full, 0, 1).reshape(count, size * part, 2 * columns)


def half_columns(values, side):
    half = values.shape[-1] // 2
    return lax.dynamic_slice_in_dim(values, side * half, half, axis=values.ndim - 1)


def by_line(values, size):
    count, rows, columns = values.shape
    return values.reshape(count, size, rows // size, columns)


def two_parts(values):
    high = values.astype(bf16)
    return jnp.concatenate([high, (values - high.astype(f32)).astype(bf16)], axis=0)


def from_parts(parts):
    count = parts.shape[0] // 2
    return parts[:count].astype(f32) + parts[count:].astype(f32)


def finish_exchange(keep, got, small_keep):
    rows = keep.size // keep.shape[-1]
    small = from_parts(two_parts(small_keep)) + from_parts(got[rows:])
    return keep + got[:rows].reshape(keep.shape).astype(f32), small


def start_exchange(send, small_send, axis, size, bit):
    sent = send.astype(bf16).reshape(-1, send.shape[-1])
    if small_send is not None:
        sent = jnp.concatenate([sent, two_parts(small_send)], axis=0)
    return swap(sent, axis, size, bit)


def halves(held, bit):
    count, lines = held.shape[:2]
    held = held.reshape((count, lines // 2, 2) + held.shape[2:])
    side = (lax.axis_index("dp") & bit) // bit
    mine = lax.dynamic_index_in_dim(held, side, 2, keepdims=False)
    return mine, lax.dynamic_index_in_dim(held, 1 - side, 2, keepdims=False)


def sum_everywhere(values, size):
    values = values + swap(values, "head", 2, 1)
    for bit in bits_of(size):
        values = values + swap(values, "dp", size, bit)
    return values


def adam_terms(grad_sum, first_old, second):
    first_new = BETA_ONE * first_old + (1.0 - BETA_ONE) * grad_sum
    second_new = BETA_TWO * second + (1.0 - BETA_TWO) * grad_sum * grad_sum
    direction = (
        first_new
        / (1.0 - BETA_ONE**STEP)
        / (jnp.sqrt(second_new / (1.0 - BETA_TWO**STEP)) + ADAM_EPS)
    )
    return (first_new, second_new, direction)


def after(first, second):
    return lax.optimization_barrier((first, second))


def body(
    size,
    tokens, grad_out, segments, counts,
    attn_w, attn_m, attn_v, mlp_w, mlp_m, mlp_v, conv_w, conv_m, conv_v, norm_w, norm_m, norm_v,
):
    rank = lax.axis_index("head")
    own_rows = segments.shape[0] // 2
    segments = lax.dynamic_slice_in_dim(segments, rank * own_rows, own_rows, axis=0)
    counts = lax.dynamic_slice_in_dim(counts, rank * own_rows, own_rows, axis=0)
    width = norm_w.shape[1]
    attn_use = gather_weights(attn_w.astype(bf16), size, rank)
    mlp_lines = lax.all_gather(mlp_w.astype(bf16), "dp", axis=1, tiled=True)
    conv_low = conv_w.astype(bf16)
    conv_use = join_columns(conv_low, swap(conv_low, "head", 2, 1), rank)
    starts, classes, images = attention_plan(segments)
    middle, qkv, context, ext = attn_forward(starts, classes, counts, tokens, attn_use, norm_w, images)
    middle, mlp_lines = after(middle, mlp_lines)
    mlp_use = join_columns(mlp_lines, swap(mlp_lines, "head", 2, 1), rank)
    rank_at = rank.astype(jnp.int32).reshape(1)
    output, grad_middle, held, send, grad_conv, grad_norm_two = mlp_layer(
        line_places(segments), rank_at, middle, grad_out, mlp_use, spread_taps(conv_use), norm_w
    )

    def back(first, count, so_far):
        return attn_backward(
            first, count, so_far, starts, classes, counts, rank_at, tokens, grad_middle, qkv, context, ext, attn_use, norm_w, images
        )

    bits = bits_of(size)
    norm_two = jnp.sum(grad_norm_two.reshape(2, 8, width), axis=1).reshape(1, 2 * width)
    columns = conv_w.shape[1]
    wide_norm = jnp.pad(norm_two, ((0, 0), (0, columns - 2 * width)))
    small = jnp.concatenate([half_columns(grad_conv[:9], rank), wide_norm])
    got = start_exchange(send, jnp.concatenate([half_columns(grad_conv[:9], 1 - rank), wide_norm]), "head", 2, 1)
    first_rows = max(1, own_rows // 3)
    so_far = back(0, first_rows, None)
    so_far, got = after(so_far, got)
    held, small = finish_exchange(held, got, small)
    keep, send = halves(by_line(held, size), bits[0])
    got = start_exchange(send, small, "dp", size, bits[0])
    so_far, send = after(so_far, send)
    grad_tokens, attn_held, attn_send, grad_norm_one = back(first_rows, own_rows - first_rows, so_far)

    attn_got = start_exchange(attn_send, None, "head", 2, 1)
    attn_held, got = after(attn_held, got)
    held, small = finish_exchange(keep, got, small)
    attn_held = by_line(attn_held + attn_got.reshape(attn_held.shape).astype(f32), size)
    for n, bit in enumerate(bits):
        attn_keep, attn_send = halves(attn_held, bit)
        more = n + 1 < len(bits)
        if more:
            keep, send = halves(held, bits[n + 1])
            attn_send, send = after(attn_send, send)
        attn_got = start_exchange(attn_send, None, "dp", size, bit)
        if more:
            got = start_exchange(send, small, "dp", size, bits[n + 1])
        attn_held = attn_keep + attn_got.reshape(attn_keep.shape).astype(f32)
        if more:
            held, small = finish_exchange(keep, got, small)
    grad_attn = attn_held.reshape(attn_w.shape)
    grad_mlp = held.reshape(mlp_w.shape)
    grad_conv = small[:9]
    norm_two = small[9, : 2 * width].reshape(2, width)

    new_attn_m, new_attn_v, attn_direction = adam_terms(grad_attn, attn_m, attn_v)
    new_mlp_m, new_mlp_v, mlp_direction = adam_terms(grad_mlp, mlp_m, mlp_v)
    new_conv_m, new_conv_v, conv_direction = adam_terms(grad_conv, conv_m, conv_v)
    attn_update = attn_direction + DECAY * attn_w
    mlp_update = mlp_direction + DECAY * mlp_w
    conv_update = conv_direction + DECAY * conv_w
    first_line = (lax.axis_index("dp") == 0).astype(f32)
    weight_squares = jnp.concatenate(
        [
            jnp.sum(attn_w * attn_w, axis=(1, 2)),
            jnp.sum(mlp_w * mlp_w, axis=(1, 2)),
            (first_line * jnp.sum(conv_w * conv_w))[None],
        ]
    )
    update_squares = jnp.concatenate(
        [
            jnp.sum(attn_update * attn_update, axis=(1, 2)),
            jnp.sum(mlp_update * mlp_update, axis=(1, 2)),
            (first_line * jnp.sum(conv_update * conv_update))[None],
        ]
    )
    squares = jnp.pad(jnp.stack([weight_squares, update_squares]), ((0, 0), (0, width - 7)))
    norm_one = jnp.sum(grad_norm_one.reshape(2, 8, width), axis=1)
    summed = sum_everywhere(jnp.concatenate([squares, norm_one, jnp.zeros((4, width), f32)]), size)
    squares, norm_grads = summed[:2, :7], jnp.concatenate([summed[2:4], norm_two])
    ratio = jnp.sqrt(squares[0]) / jnp.sqrt(squares[1])
    new_attn_w = attn_w - RATE * ratio[:4, None, None] * attn_update
    new_mlp_w = mlp_w - RATE * ratio[4:6, None, None] * mlp_update
    new_conv_w = conv_w - RATE * ratio[6] * conv_update
    new_norm_m, new_norm_v, norm_direction = adam_terms(norm_grads, norm_m, norm_v)
    new_norm_w = norm_w - RATE * norm_direction
    return (
        output, grad_tokens, new_attn_w, new_attn_m, new_attn_v, new_mlp_w, new_mlp_m, new_mlp_v,
        new_conv_w, new_conv_m, new_conv_v, new_norm_w, new_norm_m, new_norm_v,
    )


def solution(mesh):
    rows, lines = P(("dp", "head"), None), P("dp", None)
    shards, columns = P(None, "dp", "head"), P(None, "head")
    in_specs = (rows, rows, lines, P("dp")) + (shards,) * 6 + (columns,) * 3 + (P(),) * 3
    out_specs = (rows, rows) + (shards,) * 6 + (columns,) * 3 + (P(),) * 3
    return jax.shard_map(
        functools.partial(body, mesh.shape["dp"]), mesh=mesh, in_specs=in_specs, out_specs=out_specs, check_vma=False
    )
```

time: 354 us -> 326 us (0.921)
  Pallas kernels: 214 us -> 196 us
  starting transfers between devices: 29.7 us -> 24.4 us
  local copies, waits for them, and re-layouts: 15.5 us -> 11.4 us
    pallas_call x1, Pallas kernels: 48.2 us -> 32.9 us  [attn_forward(): pl.pallas_call(attn_forward_kernel, grid_spec=pltpu.PrefetchScalarGridSpe...]
    ppermute x22 -> x24, starting transfers between devices: 29.6 us -> 24.4 us  [swap(): return lax.ppermute(values, axis, [(i, i ^ bit) for i in range(size)])]
    ppermute x22 -> x24, waiting for transfers between devices: 53.5 us -> 48.8 us  [swap(): return lax.ppermute(values, axis, [(i, i ^ bit) for i in range(size)])]
    convert_element_type x11 -> x2, local copies, waits for them, and re-layouts: 4.11 us -> 0.09 us  [start_exchange(): sent = send.astype(bf16).reshape(-1, send.shape[-1])]
    all_gather x1, waiting for transfers between devices: 0.01 us -> 3.86 us  [body(): mlp_lines = lax.all_gather(mlp_w.astype(bf16), 'dp', axis=1, tiled=True)]
  transfers between devices with their start and end apart: 23 -> 25, of which waited for: 17 -> 18; matrix products, arithmetic and copies ran while one was open for 5% -> 5% of each run, Pallas kernels for 32% -> 29%
where the time goes in v3:
time: 326 us; the launch traced here: 322 us
  Pallas kernels  196 us (60%)
  waiting for transfers between devices  52.7 us (16%)
  starting transfers between devices  24.4 us (7%)
  other arithmetic  20.9 us (6%)
  between operations  16.9 us (5%)
  local copies, waits for them, and re-layouts  11.4 us (3%)
    pallas_call x1, Pallas kernels, mlp_layer(): pl.pallas_call(mlp_kernel, grid_spec=pltpu.PrefetchScalarGridSpec(num_sca...  101 us
    pallas_call x2, Pallas kernels, attn_backward(): pl.pallas_call(functools.partial(attn_backward_kernel, first, final), gri...  61.9 us
    ppermute x24, waiting for transfers between devices, swap(): return lax.ppermute(values, axis, [(i, i ^ bit) for i in range(size)])  48.8 us
    pallas_call x1, Pallas kernels, attn_forward(): pl.pallas_call(attn_forward_kernel, grid_spec=pltpu.PrefetchScalarGridSpe...  32.9 us
    ppermute x24, starting transfers between devices, swap(): return lax.ppermute(values, axis, [(i, i ^ bit) for i in range(size)])  24.4 us
  transfers between devices with their start and end apart: 25, of which 18 were waited for; matrix products, arithmetic and copies ran while one was open for 5% of the time, Pallas kernels for 29%

profile of v3, /device:TPU:0, one launch (start us, length us, event | category | flops | bytes accessed | tf_op | source)
XLA Modules:
  0.0 322.1 jit_solution(7391575597824626804)
XLA Ops:
  7.3 0.9 convert_bitcast_fusion
  8.2 5.0 %collective-permute-start = (bf16[1,4,24,192]{3,2,1,0:T(8,128)(2,1)S(1)}, bf16[1,4,24,192]{3,2,1,0:T(8,128)(2,1)S(1)}, u32[]{:S(2)}, u32[]{:S(2)}) collective-permute-start(bf16[1,4,24,192]{3,2,1,0:T(8,128)(2,1)S(1)} %convert_bitcast_fusion), channel_id=1, source_target_pairs={{0,24},{2,26},{4,28},{6,30},{8,16},{10,18},{12,20},{14,22},{16,8},... | collective-permute-start | bytes 110600 | tf_op jit(solution)/shard_map/ppermute | solution.py:687
  13.8 1.6 convert_element_type.273
  15.4 0.8 convert_element_type.274
  18.7 0.9 select_bitcast_fusion.7
  19.6 2.7 collective-permute-start.3
  24.5 3.9 %collective-permute-done.3 = bf16[4,4,24,192]{3,2,1,0:T(8,128)(2,1)S(1)} collective-permute-done((bf16[4,4,24,192]{3,2,1,0:T(8,128)(2,1)S(1)}, bf16[4,4,24,192]{3,2,1,0:T(8,128)(2,1)S(1)}, u32[]{:S(2)}, u32[]{:S(2)}) %collective-permute-start.3) | collective-permute-done | bytes 147488 | tf_op jit(solution)/shard_map/ppermute | solution.py:687
  28.3 4.3 %collective-permute-done.4 = bf16[4,4,24,192]{3,2,1,0:T(8,128)(2,1)S(1)} collective-permute-done((bf16[4,4,24,192]{3,2,1,0:T(8,128)(2,1)S(1)}, bf16[4,4,24,192]{3,2,1,0:T(8,128)(2,1)S(1)}, u32[]{:S(2)}, u32[]{:S(2)}) %collective-permute-start.4) | collective-permute-done | bytes 147488 | tf_op jit(solution)/shard_map/ppermute | solution.py:687
  33.9 1.7 collective-permute-done.6
  36.2 1.2 copy.66
  37.4 32.9 %shard_map.263 = (f32[3072,384]{1,0:T(8,128)}, bf16[3072,1152]{1,0:T(8,128)(2,1)}, bf16[3072,384]{1,0:T(8,128)(2,1)}, bf16[96,1024]{1,0:T(8,128)(2,1)}) custom-call(s32[3,8]{1,0:T(4,128)} %get-tuple-element.126.start_ref, s32[3,8]{1,0:T(4,128)} %get-tuple-element.125.class_ref, s32[3]{0:T(128)} %dynamic_slice.61.count_ref, bf16[3072,384]{1,0:T(8,128)(2,1)} %tokens_ref.5, ...), custom_call_target="tpu_custom_call" | custom-call | tf_op jit(solution)/shard_map/pallas_call | solution.py:185
  70.4 3.9 %all-gather.2.cloned.1.call-done = bf16[2,384,768]{2,1,0:T(8,128)(2,1)} async-done(((bf16[2,24,768]{2,1,0:T(8,128)(2,1)}), bf16[2,384,768]{2,1,0:T(8,128)(2,1)}) %all-gather.2.cloned.1.call-update) | async-done | bytes 1179664 | tf_op jit(solution)/shard_map/all_gather | solution.py:796
  74.3 1.0 pad_maximum_fusion.2.taps_ref
  75.3 2.0 collective-permute-done.7
  77.4 1.6 pad_maximum_fusion.w_ref
  79.0 100.9 %shard_map.264 = (bf16[3072,384]{1,0:T(8,128)(2,1)}, f32[3072,384]{1,0:T(8,128)}, f32[2,384,768]{2,1,0:T(8,128)}, bf16[2,384,768]{2,1,0:T(8,128)(2,1)}, f32[16,1536]{1,0:T(8,128)}, /*index=5*/f32[16,384]{1,0:T(8,128)}) custom-call(s32[3,64]{1,0:T(4,128)} %multiply_add_fusion.7.place_ref, s32[1]{0:T(128)} %bitcast.rank_ref, ...), custom_call_target="tpu_custom_call" | custom-call | tf_op jit(solution)/shard_map/pallas_call | solution.py:595
  180.7 0.8 constant_dynamic-slice_fusion.6
  181.5 1.4 pad_maximum_fusion.1
  183.1 21.9 %shard_map.265 = (f32[3072,384]{1,0:T(8,128)}, f32[4,384,384]{2,1,0:T(8,128)}, f32[16,384]{1,0:T(8,128)}) custom-call(s32[3,8]{1,0:T(4,128)} %get-tuple-element.126.start_ref, s32[3,8]{1,0:T(4,128)} %get-tuple-element.125.class_ref, s32[3]{0:T(128)} %dynamic_slice.61.count_ref, s32[1]{0:T(128)} %bitcast.rank_ref, bf16[3072,384]{1,0:T(8,128)(2,1)} %tokens_ref.5, ...), custom_call_target="tpu_custom_call" | custom-call | tf_op jit(solution)/shard_map/pallas_call | solution.py:388
  205.1 1.5 copy-done.2
  207.0 0.9 pad_maximum_fusion.4
  207.9 1.1 collective-permute-start.10
  209.0 40.0 %shard_map.266 = (f32[3072,384]{1,0:T(8,128)}, f32[4,384,192]{2,1,0:T(8,128)}, bf16[4,384,192]{2,1,0:T(8,128)(2,1)}, f32[16,384]{1,0:T(8,128)}) custom-call(s32[3,8]{1,0:T(4,128)} %get-tuple-element.126.start_ref, s32[3,8]{1,0:T(4,128)} %get-tuple-element.125.class_ref, s32[3]{0:T(128)} %dynamic_slice.61.count_ref, ...), custom_call_target="tpu_custom_call", output_to_operand_aliasing={{0}: (12, {})} | custom-call | tf_op jit(solution)/shard_map/pallas_call | solution.py:388
  249.0 2.2 copy.69
  251.2 1.4 collective-permute-start.11
  252.8 1.8 collective-permute-done.11
  254.6 1.3 copy.70
  255.9 1.1 slice.110
  257.1 0.8 fusion.8
  257.9 1.6 add.289
  259.7 0.8 collective-permute-start.12
  260.6 4.7 %collective-permute-start.13 = (bf16[212,768]{1,0:T(8,128)(2,1)S(1)}, bf16[212,768]{1,0:T(8,128)(2,1)S(1)}, u32[]{:S(2)}, u32[]{:S(2)}) collective-permute-start(bf16[212,768]{1,0:T(8,128)(2,1)S(1)} %pad_maximum_fusion.5), channel_id=1, source_target_pairs={{0,4},{2,6},{4,0},{6,2},{8,12},{10,14},{12,8},{14,10},{16,20},{18,... | collective-permute-start | bytes 976904 | tf_op jit(solution)/shard_map/ppermute | solution.py:687
  265.4 5.8 %collective-permute-done.12 = bf16[768,192]{1,0:T(8,128)(2,1)S(1)} collective-permute-done((bf16[768,192]{1,0:T(8,128)(2,1)S(1)}, bf16[768,192]{1,0:T(8,128)(2,1)S(1)}, u32[]{:S(2)}, u32[]{:S(2)}) %collective-permute-start.12) | collective-permute-done | bytes 294944 | tf_op jit(solution)/shard_map/ppermute | solution.py:687
  271.4 2.0 collective-permute-done.13
  273.5 3.2 collective-permute-start.14
  276.9 4.2 %collective-permute-done.14 = bf16[384,192]{1,0:T(8,128)(2,1)S(1)} collective-permute-done((bf16[384,192]{1,0:T(8,128)(2,1)S(1)}, bf16[384,192]{1,0:T(8,128)(2,1)S(1)}, u32[]{:S(2)}, u32[]{:S(2)}) %collective-permute-start.14) | collective-permute-done | bytes 147488 | tf_op jit(solution)/shard_map/ppermute | solution.py:687
  281.2 1.2 collective-permute-done.15
  283.3 4.0 %collective-permute-done.16 = bf16[192,192]{1,0:T(8,128)(2,1)S(1)} collective-permute-done((bf16[192,192]{1,0:T(8,128)(2,1)S(1)}, bf16[192,192]{1,0:T(8,128)(2,1)S(1)}, u32[]{:S(2)}, u32[]{:S(2)}) %collective-permute-start.16) | collective-permute-done | bytes 73760 | tf_op jit(solution)/shard_map/ppermute | solution.py:687
  287.3 1.1 collective-permute-start.17
  288.4 2.7 collective-permute-done.18
  294.0 1.2 collective-permute-done.19
  295.2 0.9 collective-permute-start.20
  296.1 2.8 collective-permute-done.20
  298.9 0.8 collective-permute-start.21
  299.7 2.9 collective-permute-done.21
  302.6 3.7 %collective-permute-done.22 = f32[8,384]{1,0:T(8,128)S(1)} collective-permute-done((f32[8,384]{1,0:T(8,128)S(1)}, f32[8,384]{1,0:T(8,128)S(1)}, u32[]{:S(2)}, u32[]{:S(2)}) %collective-permute-start.22) | collective-permute-done | bytes 12320 | tf_op jit(solution)/shard_map/ppermute | solution.py:687
  306.3 4.6 %collective-permute-done.23 = f32[8,384]{1,0:T(8,128)S(1)} collective-permute-done((f32[8,384]{1,0:T(8,128)S(1)}, f32[8,384]{1,0:T(8,128)S(1)}, u32[]{:S(2)}, u32[]{:S(2)}) %collective-permute-start.23) | collective-permute-done | bytes 12320 | tf_op jit(solution)/shard_map/ppermute | solution.py:687
  312.9 0.8 multiply_subtract_fusion
  (175 shorter events, 14.9 us)
Async XLA Ops:
  7.2 9.1 %copy-start = (s32[6,1024]{1,0:T(8,128)S(1)}, s32[6,1024]{1,0:T(8,128)}, u32[]{:S(2)}) copy-start(s32[6,1024]{1,0:T(8,128)} %param.18) | copy-start | bytes 73732
  7.2 16.0 %copy-start.28 = (s32[6]{0:T(128)S(1)}, s32[6]{0:T(128)}, u32[]{:S(2)}) copy-start(s32[6]{0:T(128)} %param.19) | copy-start | bytes 76
  7.2 67.0 %all-gather.2.cloned.1.call-start = ((), (), s32[]{:S(2)}) async-start(), calls=%async_computation | async-start | bytes 1253376 | tf_op jit(solution)/shard_map/all_gather | solution.py:796
  8.2 10.5 %collective-permute-start = (bf16[1,4,24,192]{3,2,1,0:T(8,128)(2,1)S(1)}, bf16[1,4,24,192]{3,2,1,0:T(8,128)(2,1)S(1)}, u32[]{:S(2)}, u32[]{:S(2)}) collective-permute-start(bf16[1,4,24,192]{3,2,1,0:T(8,128)(2,1)S(1)} %convert_bitcast_fusion), channel_id=1, source_target_pairs={{0,24},{2,26},{4,28},{6,30},{8,16},{10,18},{12,20},{14,22},{16,8},... | collective-permute-start | bytes 110600 | tf_op jit(solution)/shard_map/ppermute | solution.py:687
  13.2 5.4 %collective-permute-start.1 = (bf16[1,4,24,192]{3,2,1,0:T(8,128)(2,1)S(1)}, bf16[1,4,24,192]{3,2,1,0:T(8,128)(2,1)S(1)}, u32[]{:S(2)}, u32[]{:S(2)}) collective-permute-start(bf16[1,4,24,192]{3,2,1,0:T(8,128)(2,1)S(1)} %convert_bitcast_fusion), channel_id=1, source_target_pairs={{0,16},{2,18},{4,20},{6,22},{8,24},{10,26},{12,28},{14,30},{16,0},... | collective-permute-start | bytes 110600 | tf_op jit(solution)/shard_map/ppermute | solution.py:687
  13.2 5.4 %collective-permute-start.2 = (bf16[1,4,24,192]{3,2,1,0:T(8,128)(2,1)S(1)}, bf16[1,4,24,192]{3,2,1,0:T(8,128)(2,1)S(1)}, u32[]{:S(2)}, u32[]{:S(2)}) collective-permute-start(bf16[1,4,24,192]{3,2,1,0:T(8,128)(2,1)S(1)} %convert_bitcast_fusion), channel_id=1, source_target_pairs={{0,8},{2,10},{4,12},{6,14},{8,0},{10,2},{12,4},{14,6},{16,24},{18,... | collective-permute-start | bytes 110600 | tf_op jit(solution)/shard_map/ppermute | solution.py:687
  16.2 17.1 %collective-permute-start.8 = (bf16[9,768]{1,0:T(8,128)(2,1)S(1)}, bf16[9,768]{1,0:T(8,128)(2,1)S(1)}, u32[]{:S(2)}, u32[]{:S(2)}) collective-permute-start(bf16[9,768]{1,0:T(8,128)(2,1)S(1)} %convert_element_type.274), channel_id=1, source_target_pairs={{0,1},{1,0},{2,3},{3,2},{4,5},{5,4},{6,7},{7,6},{8,9},{9,8},{10,11... | collective-permute-start | bytes 41480 | tf_op jit(solution)/shard_map/ppermute | solution.py:687
  19.6 8.7 %collective-permute-start.3 = (bf16[4,4,24,192]{3,2,1,0:T(8,128)(2,1)S(1)}, bf16[4,4,24,192]{3,2,1,0:T(8,128)(2,1)S(1)}, u32[]{:S(2)}, u32[]{:S(2)}) collective-permute-start(bf16[4,4,24,192]{3,2,1,0:T(8,128)(2,1)S(1)} %maximum_bitcast_fusion.1), channel_id=1, source_target_pairs={{0,6},{2,4},{4,2},{6,0},{8,14},{10,12},{12,10},{14,8},{16,22},{18,... | collective-permute-start | bytes 442376 | tf_op jit(solution)/shard_map/ppermute | solution.py:687
  22.3 10.3 %collective-permute-start.4 = (bf16[4,4,24,192]{3,2,1,0:T(8,128)(2,1)S(1)}, bf16[4,4,24,192]{3,2,1,0:T(8,128)(2,1)S(1)}, u32[]{:S(2)}, u32[]{:S(2)}) collective-permute-start(bf16[4,4,24,192]{3,2,1,0:T(8,128)(2,1)S(1)} %maximum_bitcast_fusion.1), channel_id=1, source_target_pairs={{0,4},{2,6},{4,0},{6,2},{8,12},{10,14},{12,8},{14,10},{16,20},{18,... | collective-permute-start | bytes 442376 | tf_op jit(solution)/shard_map/ppermute | solution.py:687
  22.8 10.1 %collective-permute-start.5 = (bf16[4,4,24,192]{3,2,1,0:T(8,128)(2,1)S(1)}, bf16[4,4,24,192]{3,2,1,0:T(8,128)(2,1)S(1)}, u32[]{:S(2)}, u32[]{:S(2)}) collective-permute-start(bf16[4,4,24,192]{3,2,1,0:T(8,128)(2,1)S(1)} %maximum_bitcast_fusion.1), channel_id=1, source_target_pairs={{0,2},{2,0},{4,6},{6,4},{8,10},{10,8},{12,14},{14,12},{16,18},{18,... | collective-permute-start | bytes 442376 | tf_op jit(solution)/shard_map/ppermute | solution.py:687
  33.3 2.4 collective-permute-start.6
  74.2 3.1 collective-permute-start.7
  182.9 22.1 %collective-permute-start.9 = (bf16[788,768]{1,0:T(8,128)(2,1)S(1)}, bf16[788,768]{1,0:T(8,128)(2,1)S(1)}, u32[]{:S(2)}, u32[]{:S(2)}) collective-permute-start(bf16[788,768]{1,0:T(8,128)(2,1)S(1)} %pad_maximum_fusion.1), channel_id=1, source_target_pairs={{0,1},{1,0},{2,3},{3,2},{4,5},{5,4},{6,7},{7,6},{8,9},{9,8},{10,11... | collective-permute-start | bytes 3631112 | tf_op jit(solution)/shard_map/ppermute | solution.py:687
  207.9 48.0 %collective-permute-start.10 = (bf16[404,768]{1,0:T(8,128)(2,1)}, bf16[404,768]{1,0:T(8,128)(2,1)}, u32[]{:S(2)}, u32[]{:S(2)}) collective-permute-start(bf16[404,768]{1,0:T(8,128)(2,1)} %pad_maximum_fusion.4), channel_id=1, source_target_pairs={{0,2},{2,0},{4,6},{6,4},{8,10},{10,8},{12,14},{14,12},{16,18},{18,... | collective-permute-start | bytes 1861640 | tf_op jit(solution)/shard_map/ppermute | solution.py:687
  251.2 3.4 %collective-permute-start.11 = (bf16[1536,192]{0,1:T(8,128)(2,1)}, bf16[1536,192]{0,1:T(8,128)(2,1)}, u32[]{:S(2)}, u32[]{:S(2)}) collective-permute-start(bf16[1536,192]{0,1:T(8,128)(2,1)} %copy.69), channel_id=1, source_target_pairs={{0,1},{1,0},{2,3},{3,2},{4,5},{5,4},{6,7},{7,6},{8,9},{9,8},{10,11... | collective-permute-start | bytes 1769480 | tf_op jit(solution)/shard_map/ppermute | solution.py:687
  252.8 4.2 %copy-start.13 = (bf16[10,768]{1,0:T(8,128)(2,1)S(1)}, bf16[10,768]{1,0:T(8,128)(2,1)}, u32[]{:S(2)}) copy-start(bf16[10,768]{1,0:T(8,128)(2,1)} %copy-done.12) | copy-start | bytes 46084
  252.8 4.2 %copy-start.15 = (bf16[10,768]{1,0:T(8,128)(2,1)S(1)}, bf16[10,768]{1,0:T(8,128)(2,1)}, u32[]{:S(2)}) copy-start(bf16[10,768]{1,0:T(8,128)(2,1)} %copy-done.14) | copy-start | bytes 46084
  259.7 11.5 %collective-permute-start.12 = (bf16[768,192]{1,0:T(8,128)(2,1)S(1)}, bf16[768,192]{1,0:T(8,128)(2,1)S(1)}, u32[]{:S(2)}, u32[]{:S(2)}) collective-permute-start(bf16[768,192]{1,0:T(8,128)(2,1)S(1)} %bitcast.171), channel_id=1, source_target_pairs={{0,2},{2,0},{4,6},{6,4},{8,10},{10,8},{12,14},{14,12},{16,18},{18,... | collective-permute-start | bytes 884744 | tf_op jit(solution)/shard_map/ppermute | solution.py:687
  260.6 12.8 %collective-permute-start.13 = (bf16[212,768]{1,0:T(8,128)(2,1)S(1)}, bf16[212,768]{1,0:T(8,128)(2,1)S(1)}, u32[]{:S(2)}, u32[]{:S(2)}) collective-permute-start(bf16[212,768]{1,0:T(8,128)(2,1)S(1)} %pad_maximum_fusion.5), channel_id=1, source_target_pairs={{0,4},{2,6},{4,0},{6,2},{8,12},{10,14},{12,8},{14,10},{16,20},{18,... | collective-permute-start | bytes 976904 | tf_op jit(solution)/shard_map/ppermute | solution.py:687
  273.5 7.6 %collective-permute-start.14 = (bf16[384,192]{1,0:T(8,128)(2,1)S(1)}, bf16[384,192]{1,0:T(8,128)(2,1)S(1)}, u32[]{:S(2)}, u32[]{:S(2)}) collective-permute-start(bf16[384,192]{1,0:T(8,128)(2,1)S(1)} %bitcast.175), channel_id=1, source_target_pairs={{0,4},{2,6},{4,0},{6,2},{8,12},{10,14},{12,8},{14,10},{16,20},{18,... | collective-permute-start | bytes 442376 | tf_op jit(solution)/shard_map/ppermute | solution.py:687
  276.8 5.6 %collective-permute-start.15 = (bf16[116,768]{1,0:T(8,128)(2,1)S(1)}, bf16[116,768]{1,0:T(8,128)(2,1)S(1)}, u32[]{:S(2)}, u32[]{:S(2)}) collective-permute-start(bf16[116,768]{1,0:T(8,128)(2,1)S(1)} %pad_maximum_fusion.6), channel_id=1, source_target_pairs={{0,8},{2,10},{4,12},{6,14},{8,0},{10,2},{12,4},{14,6},{16,24},{18,... | collective-permute-start | bytes 534536 | tf_op jit(solution)/shard_map/ppermute | solution.py:687
  281.2 9.9 %copy-start.4 = (f32[2,24,768]{2,1,0:T(8,128)S(1)}, f32[2,24,768]{2,1,0:T(8,128)}, u32[]{:S(2)}) copy-start(f32[2,24,768]{2,1,0:T(8,128)} %param.23) | copy-start | bytes 442372
  281.2 9.9 %copy-start.19 = (f32[2,24,768]{2,1,0:T(8,128)S(1)}, f32[2,24,768]{2,1,0:T(8,128)}, u32[]{:S(2)}) copy-start(f32[2,24,768]{2,1,0:T(8,128)} %param.24) | copy-start | bytes 442372
  281.2 9.9 %copy-start.20 = (f32[2,24,768]{2,1,0:T(8,128)S(1)}, f32[2,24,768]{2,1,0:T(8,128)}, u32[]{:S(2)}) copy-start(f32[2,24,768]{2,1,0:T(8,128)} %param.25) | copy-start | bytes 442372
  282.5 9.0 %copy-start.7 = (f32[9,768]{1,0:T(8,128)S(1)}, f32[9,768]{1,0:T(8,128)}, u32[]{:S(2)}) copy-start(f32[9,768]{1,0:T(8,128)} %param.26) | copy-start | bytes 82948
  282.5 9.0 %copy-start.23 = (f32[9,768]{1,0:T(8,128)S(1)}, f32[9,768]{1,0:T(8,128)}, u32[]{:S(2)}) copy-start(f32[9,768]{1,0:T(8,128)} %param.27) | copy-start | bytes 82948
  282.5 9.0 %copy-start.24 = (f32[9,768]{1,0:T(8,128)S(1)}, f32[9,768]{1,0:T(8,128)}, u32[]{:S(2)}) copy-start(f32[9,768]{1,0:T(8,128)} %param.28) | copy-start | bytes 82948
  282.5 10.9 %copy-start.3 = (f32[4,24,192]{2,1,0:T(8,128)S(1)}, f32[4,24,192]{2,1,0:T(8,128)}, u32[]{:S(2)}) copy-start(f32[4,24,192]{2,1,0:T(8,128)} %param.20) | copy-start | bytes 221188
  282.6 10.9 %copy-start.21 = (f32[4,24,192]{2,1,0:T(8,128)S(1)}, f32[4,24,192]{2,1,0:T(8,128)}, u32[]{:S(2)}) copy-start(f32[4,24,192]{2,1,0:T(8,128)} %param.21) | copy-start | bytes 221188
  282.6 10.9 %copy-start.22 = (f32[4,24,192]{2,1,0:T(8,128)S(1)}, f32[4,24,192]{2,1,0:T(8,128)}, u32[]{:S(2)}) copy-start(f32[4,24,192]{2,1,0:T(8,128)} %param.22) | copy-start | bytes 221188
  282.6 4.7 %collective-permute-start.16 = (bf16[192,192]{1,0:T(8,128)(2,1)S(1)}, bf16[192,192]{1,0:T(8,128)(2,1)S(1)}, u32[]{:S(2)}, u32[]{:S(2)}) collective-permute-start(bf16[192,192]{1,0:T(8,128)(2,1)S(1)} %bitcast.178), channel_id=1, source_target_pairs={{0,8},{2,10},{4,12},{6,14},{8,0},{10,2},{12,4},{14,6},{16,24},{18,... | collective-permute-start | bytes 221192 | tf_op jit(solution)/shard_map/ppermute | solution.py:687
  283.0 8.1 %collective-permute-start.18 = (bf16[68,768]{1,0:T(8,128)(2,1)S(1)}, bf16[68,768]{1,0:T(8,128)(2,1)S(1)}, u32[]{:S(2)}, u32[]{:S(2)}) collective-permute-start(bf16[68,768]{1,0:T(8,128)(2,1)S(1)} %pad_maximum_fusion.7), channel_id=1, source_target_pairs={{0,16},{2,18},{4,20},{6,22},{8,24},{10,26},{12,28},{14,30},{16,0},... | collective-permute-start | bytes 313352 | tf_op jit(solution)/shard_map/ppermute | solution.py:687
  287.3 6.1 %collective-permute-start.17 = (bf16[96,192]{1,0:T(8,128)(2,1)S(1)}, bf16[96,192]{1,0:T(8,128)(2,1)S(1)}, u32[]{:S(2)}, u32[]{:S(2)}) collective-permute-start(bf16[96,192]{1,0:T(8,128)(2,1)S(1)} %bitcast.185), channel_id=1, source_target_pairs={{0,16},{2,18},{4,20},{6,22},{8,24},{10,26},{12,28},{14,30},{16,0},... | collective-permute-start | bytes 110600 | tf_op jit(solution)/shard_map/ppermute | solution.py:687
  291.4 23.0 %copy-start.8 = (f32[2,24,768]{2,1,0:T(8,128)}, f32[2,24,768]{2,1,0:T(8,128)S(1)}, u32[]{:S(2)}) copy-start(f32[2,24,768]{2,1,0:T(8,128)S(1)} %get-tuple-element.97) | copy-start | bytes 442372
  291.4 23.0 %copy-start.9 = (f32[2,24,768]{2,1,0:T(8,128)}, f32[2,24,768]{2,1,0:T(8,128)S(1)}, u32[]{:S(2)}) copy-start(f32[2,24,768]{2,1,0:T(8,128)S(1)} %get-tuple-element.98) | copy-start | bytes 442372
  291.4 23.0 %copy-start.18 = (f32[4,384]{1,0:T(4,128)S(1)}, f32[4,384]{1,0:T(4,128)}, u32[]{:S(2)}) copy-start(f32[4,384]{1,0:T(4,128)} %norm_ref.7) | copy-start | bytes 18436
  291.4 23.0 %copy-start.26 = (f32[4,384]{1,0:T(4,128)S(1)}, f32[4,384]{1,0:T(4,128)}, u32[]{:S(2)}) copy-start(f32[4,384]{1,0:T(4,128)} %param.30) | copy-start | bytes 18436
  291.4 23.0 %copy-start.27 = (f32[4,384]{1,0:T(4,128)S(1)}, f32[4,384]{1,0:T(4,128)}, u32[]{:S(2)}) copy-start(f32[4,384]{1,0:T(4,128)} %param.31) | copy-start | bytes 18436
  291.4 23.6 %copy-start.1 = (s32[6,1024]{1,0:T(8,128)S(1)}, s32[6,1024]{1,0:T(8,128)}, u32[]{:S(2)}) copy-start(s32[6,1024]{1,0:T(8,128)} %param.18) | copy-start | bytes 73732
  292.2 22.9 %copy-start.16 = (f32[9,768]{1,0:T(8,128)}, f32[9,768]{1,0:T(8,128)S(1)}, u32[]{:S(2)}) copy-start(f32[9,768]{1,0:T(8,128)S(1)} %get-tuple-element.99) | copy-start | bytes 82948
  292.2 22.9 %copy-start.17 = (f32[9,768]{1,0:T(8,128)}, f32[9,768]{1,0:T(8,128)S(1)}, u32[]{:S(2)}) copy-start(f32[9,768]{1,0:T(8,128)S(1)} %get-tuple-element.100) | copy-start | bytes 82948
  293.7 21.3 %copy-start.10 = (f32[4,24,192]{2,1,0:T(8,128)}, f32[4,24,192]{2,1,0:T(8,128)S(1)}, u32[]{:S(2)}) copy-start(f32[4,24,192]{2,1,0:T(8,128)S(1)} %get-tuple-element.95) | copy-start | bytes 221188
  293.7 21.3 %copy-start.11 = (f32[4,24,192]{2,1,0:T(8,128)}, f32[4,24,192]{2,1,0:T(8,128)S(1)}, u32[]{:S(2)}) copy-start(f32[4,24,192]{2,1,0:T(8,128)S(1)} %get-tuple-element.96) | copy-start | bytes 221188
  293.9 1.2 collective-permute-start.19
  295.2 3.7 %collective-permute-start.20 = (f32[8,384]{1,0:T(8,128)S(1)}, f32[8,384]{1,0:T(8,128)S(1)}, u32[]{:S(2)}, u32[]{:S(2)}) collective-permute-start(f32[8,384]{1,0:T(8,128)S(1)} %fusion.25), channel_id=1, source_target_pairs={{0,2},{2,0},{4,6},{6,4},{8,10},{10,8},{12,14},{14,12},{16,18},{18,... | collective-permute-start | bytes 36872 | tf_op jit(solution)/shard_map/ppermute | solution.py:687
  298.9 3.7 %collective-permute-start.21 = (f32[8,384]{1,0:T(8,128)S(1)}, f32[8,384]{1,0:T(8,128)S(1)}, u32[]{:S(2)}, u32[]{:S(2)}) collective-permute-start(f32[8,384]{1,0:T(8,128)S(1)} %add.333), channel_id=1, source_target_pairs={{0,4},{2,6},{4,0},{6,2},{8,12},{10,14},{12,8},{14,10},{16,20},{18,... | collective-permute-start | bytes 36872 | tf_op jit(solution)/shard_map/ppermute | solution.py:687
  302.6 3.7 %collective-permute-start.22 = (f32[8,384]{1,0:T(8,128)S(1)}, f32[8,384]{1,0:T(8,128)S(1)}, u32[]{:S(2)}, u32[]{:S(2)}) collective-permute-start(f32[8,384]{1,0:T(8,128)S(1)} %add.334), channel_id=1, source_target_pairs={{0,8},{2,10},{4,12},{6,14},{8,0},{10,2},{12,4},{14,6},{16,24},{18,... | collective-permute-start | bytes 36872 | tf_op jit(solution)/shard_map/ppermute | solution.py:687
  306.3 4.6 %collective-permute-start.23 = (f32[8,384]{1,0:T(8,128)S(1)}, f32[8,384]{1,0:T(8,128)S(1)}, u32[]{:S(2)}, u32[]{:S(2)}) collective-permute-start(f32[8,384]{1,0:T(8,128)S(1)} %add.335), channel_id=1, source_target_pairs={{0,16},{2,18},{4,20},{6,22},{8,24},{10,26},{12,28},{14,30},{16,0},... | collective-permute-start | bytes 36872 | tf_op jit(solution)/shard_map/ppermute | solution.py:687
  (6 other events, 12.9 us)
Sparse Core Ops, SparseCore 0:
  15.5 58.6 all-gather.1

commit v4 on v3

--- a/solution.py
+++ b/solution.py
@@ -370,8 +370,9 @@
 
         @pl.when(step_at == pl.num_programs(0) - 1)
         def _():
-            for k in range(w_grad_ref.shape[0]):
-                halves = w_grad_ref[k, :, : width // 2], w_grad_ref[k, :, width // 2 :]
+            for k in range(2):
+                one, two = w_grad_ref[k], w_grad_ref[k + 2]
+                halves = [jnp.concatenate([one[:, at : at + width // 2], two[:, at : at + width // 2]], axis=1) for at in (0, width // 2)]
                 sent[0][k] = jnp.where(rank_ref[0] == 0, halves[0], halves[1])
                 sent[1][k] = jnp.where(rank_ref[0] == 0, halves[1], halves[0]).astype(bf16)
 
@@ -381,7 +382,7 @@
     length = rows_all // counts.shape[0]
     by_row = lambda columns: pl.BlockSpec((length, columns), lambda r, *_: (first + r, 0))
     final = first + count == counts.shape[0]
-    half = attn_use.shape[:2] + (width // 2,)
+    half = (2, width, width)
     halves = pl.BlockSpec(half, lambda r, *_: (0, 0, 0))
     whole = pl.BlockSpec(attn_use.shape, lambda r, *_: (0, 0, 0))
     sums = pl.BlockSpec((16, width), lambda r, *_: (0, 0))
@@ -683,27 +684,42 @@
     return bits
 
 
+def groups_of(size):
+    bits = bits_of(size)
+    return [(bits[at], 1 << len(bits[at : at + 2])) for at in range(0, len(bits), 2)]
+
+
 def swap(values, axis, size, bit):
     return lax.ppermute(values, axis, [(i, i ^ bit) for i in range(size)])
 
 
+def in_order(found, mine):
+    ordered = []
+    for target in range(len(found)):
+        value = found[0]
+        for step in range(1, len(found)):
+            value = jnp.where((mine ^ step) == target, found[step], value)
+        ordered.append(value)
+    return ordered
+
+
 def gather_lines(shard, size):
     place = lax.axis_index("dp")
-    bits = bits_of(size)
-    groups = [bits[at : at + 2] for at in range(0, len(bits), 2)]
     held = shard[None]
-    for group in reversed(groups):
-        steps = range(1 << len(group))
-        found = [held if step == 0 else swap(held, "dp", size, step * group[0]) for step in steps]
-        mine = (place // group[0]) % len(steps)
-        ordered = []
-        for target in steps:
-            value = found[0]
-            for step in steps[1:]:
-                value = jnp.where((mine ^ step) == target, found[step], value)
-            ordered.append(value)
-        held = jnp.stack(ordered, axis=1).reshape((-1,) + shard.shape)
+    for low, count in reversed(groups_of(size)):
+        found = [held] + [swap(held, "dp", size, step * low) for step in range(1, count)]
+        held = jnp.stack(in_order(found, (place // low) % count), axis=1).reshape((-1,) + shard.shape)
     return held
+
+
+def fold_pairs(values):
+    count = values.shape[0] // 2
+    return jnp.concatenate([values[:count], values[count:]], axis=-1)
+
+
+def unfold_pairs(values):
+    half = values.shape[-1] // 2
+    return jnp.concatenate([values[..., :half], values[..., half:]], axis=0)
 
 
 def join_columns(mine, other, rank):
@@ -714,9 +730,10 @@
 
 def gather_weights(shard, size, rank):
     count, part, columns = shard.shape
-    held = gather_lines(shard, size)
-    full = join_columns(held, swap(held, "head", 2, 1), rank)
-    return jnp.moveaxis(full, 0, 1).reshape(count, size * part, 2 * columns)
+    mine = gather_lines(fold_pairs(shard), size)
+    other = swap(mine, "head", 2, 1)
+    full = [join_columns(mine[..., at : at + columns], other[..., at : at + columns], rank) for at in (0, columns)]
+    return jnp.moveaxis(jnp.concatenate(full, axis=1), 0, 1).reshape(count, size * part, 2 * columns)
 
 
 def half_columns(values, side):
@@ -739,25 +756,15 @@
     return parts[:count].astype(f32) + parts[count:].astype(f32)
 
 
-def finish_exchange(keep, got, small_keep):
-    rows = keep.size // keep.shape[-1]
-    small = from_parts(two_parts(small_keep)) + from_parts(got[rows:])
-    return keep + got[:rows].reshape(keep.shape).astype(f32), small
-
-
-def start_exchange(send, small_send, axis, size, bit):
-    sent = send.astype(bf16).reshape(-1, send.shape[-1])
-    if small_send is not None:
-        sent = jnp.concatenate([sent, two_parts(small_send)], axis=0)
-    return swap(sent, axis, size, bit)
-
-
-def halves(held, bit):
-    count, lines = held.shape[:2]
-    held = held.reshape((count, lines // 2, 2) + held.shape[2:])
-    side = (lax.axis_index("dp") & bit) // bit
-    mine = lax.dynamic_index_in_dim(held, side, 2, keepdims=False)
-    return mine, lax.dynamic_index_in_dim(held, 1 - side, 2, keepdims=False)
+def pieces_of(held, low, count):
+    n, lines = held.shape[:2]
+    split = held.reshape((n, lines // count, count) + held.shape[2:])
+    mine = (lax.axis_index("dp") // low) % count
+    return [lax.dynamic_index_in_dim(split, mine ^ step, 2, keepdims=False) for step in range(count)]
+
+
+def flat(values):
+    return values.astype(bf16).reshape(-1, values.shape[-1])
 
 
 def sum_everywhere(values, size):
@@ -765,6 +772,10 @@
     for bit in bits_of(size):
         values = values + swap(values, "dp", size, bit)
     return values
+
+
+def after(first, second):
+    return lax.optimization_barrier((first, second))
 
 
 def adam_terms(grad_sum, first_old, second):
@@ -778,8 +789,57 @@
     return (first_new, second_new, direction)
 
 
-def after(first, second):
-    return lax.optimization_barrier((first, second))
+def moments_kernel(line_ref, norm_ref, *refs):
+    count = 3
+    grads, weights, firsts, seconds = (refs[n * count : (n + 1) * count] for n in range(4))
+    new_firsts, new_seconds, updates = (refs[(4 + n) * count : (5 + n) * count] for n in range(3))
+    sums_ref = refs[7 * count]
+    width = sums_ref.shape[1]
+    lane = lax.broadcasted_iota(jnp.int32, (1, width), 1)
+    rows = [jnp.zeros((1, width), f32), jnp.zeros((1, width), f32)]
+    at = 0
+    for n in range(count):
+        grad, weight = grads[n][...], weights[n][...]
+        new_first, new_second, direction = adam_terms(grad, firsts[n][...], seconds[n][...])
+        update = direction + DECAY * weight
+        new_firsts[n][...], new_seconds[n][...], updates[n][...] = new_first, new_second, update
+        matrices = weight.shape[0] if weight.ndim == 3 else 1
+        for k in range(matrices):
+            for row, values in enumerate((weight, update)):
+                values = values[k] if weight.ndim == 3 else values
+                total = jnp.sum(jnp.sum(values * values, axis=0, keepdims=True), axis=1, keepdims=True)
+                if weight.ndim == 2:
+                    total = jnp.where(line_ref[0] == 0, total, 0.0)
+                rows[row] = jnp.where(lane == at, total, rows[row])
+            at += 1
+    gain = jnp.sum(norm_ref[0:8, :], axis=0, keepdims=True)
+    bias = jnp.sum(norm_ref[8:16, :], axis=0, keepdims=True)
+    sums_ref[...] = jnp.concatenate(rows + [gain, bias, jnp.zeros((4, width), f32)], axis=0)
+
+
+def apply_kernel(sums_ref, norm_two_ref, norm_w_ref, norm_m_ref, norm_v_ref, *refs):
+    count = 3
+    weights, updates, news = (refs[n * count : (n + 1) * count] for n in range(3))
+    new_norm_w_ref, new_norm_m_ref, new_norm_v_ref = refs[3 * count :]
+    ratio = jnp.sqrt(sums_ref[0:1, :]) / jnp.sqrt(sums_ref[1:2, :])
+    at = 0
+    for n in range(count):
+        shape = weights[n].shape
+        if len(shape) == 3:
+            for k in range(shape[0]):
+                news[n][k] = weights[n][k] - RATE * ratio[:, at : at + 1] * updates[n][k]
+                at += 1
+        else:
+            news[n][...] = weights[n][...] - RATE * ratio[:, at : at + 1] * updates[n][...]
+            at += 1
+    grads = jnp.concatenate([sums_ref[2:4, :], norm_two_ref[...]], axis=0)
+    new_first, new_second, direction = adam_terms(grads, norm_m_ref[...], norm_v_ref[...])
+    new_norm_m_ref[...], new_norm_v_ref[...] = new_first, new_second
+    new_norm_w_ref[...] = norm_w_ref[...] - RATE * direction
+
+
+def like(values):
+    return [jax.ShapeDtypeStruct(v.shape, f32) for v in values]
 
 
 def body(
@@ -788,17 +848,19 @@
     attn_w, attn_m, attn_v, mlp_w, mlp_m, mlp_v, conv_w, conv_m, conv_v, norm_w, norm_m, norm_v,
 ):
     rank = lax.axis_index("head")
+    place = lax.axis_index("dp")
     own_rows = segments.shape[0] // 2
     segments = lax.dynamic_slice_in_dim(segments, rank * own_rows, own_rows, axis=0)
     counts = lax.dynamic_slice_in_dim(counts, rank * own_rows, own_rows, axis=0)
     width = norm_w.shape[1]
     attn_use = gather_weights(attn_w.astype(bf16), size, rank)
-    mlp_lines = lax.all_gather(mlp_w.astype(bf16), "dp", axis=1, tiled=True)
+    mlp_lines = [lax.all_gather(mlp_w[k].astype(bf16), "dp", axis=0, tiled=True) for k in range(2)]
     conv_low = conv_w.astype(bf16)
     conv_use = join_columns(conv_low, swap(conv_low, "head", 2, 1), rank)
     starts, classes, images = attention_plan(segments)
     middle, qkv, context, ext = attn_forward(starts, classes, counts, tokens, attn_use, norm_w, images)
     middle, mlp_lines = after(middle, mlp_lines)
+    mlp_lines = jnp.stack(mlp_lines)
     mlp_use = join_columns(mlp_lines, swap(mlp_lines, "head", 2, 1), rank)
     rank_at = rank.astype(jnp.int32).reshape(1)
     output, grad_middle, held, send, grad_conv, grad_norm_two = mlp_layer(
@@ -810,76 +872,89 @@
             first, count, so_far, starts, classes, counts, rank_at, tokens, grad_middle, qkv, context, ext, attn_use, norm_w, images
         )
 
-    bits = bits_of(size)
+    groups = groups_of(size)
+    columns = conv_w.shape[1]
     norm_two = jnp.sum(grad_norm_two.reshape(2, 8, width), axis=1).reshape(1, 2 * width)
-    columns = conv_w.shape[1]
-    wide_norm = jnp.pad(norm_two, ((0, 0), (0, columns - 2 * width)))
-    small = jnp.concatenate([half_columns(grad_conv[:9], rank), wide_norm])
-    got = start_exchange(send, jnp.concatenate([half_columns(grad_conv[:9], 1 - rank), wide_norm]), "head", 2, 1)
+    norm_two = jnp.pad(norm_two, ((0, 0), (0, columns - 2 * width)))
+    taps = grad_conv[:9]
+    small = jnp.concatenate([half_columns(taps, rank), norm_two])
+    small_send = jnp.concatenate([half_columns(taps, 1 - rank), norm_two])
+    got = swap(jnp.concatenate([flat(send), two_parts(small_send)], axis=0), "head", 2, 1)
     first_rows = max(1, own_rows // 3)
-    so_far = back(0, first_rows, None)
-    so_far, got = after(so_far, got)
-    held, small = finish_exchange(held, got, small)
-    keep, send = halves(by_line(held, size), bits[0])
-    got = start_exchange(send, small, "dp", size, bits[0])
-    so_far, send = after(so_far, send)
+    so_far, got = after(back(0, first_rows, None), got)
+    rows = held.size // columns
+    held = by_line(held + got[:rows].reshape(held.shape).astype(f32), size)
+    small = from_parts(two_parts(small)) + from_parts(got[rows:])
+    low, count = groups[0]
+    pieces = pieces_of(held, low, count)
+    small_parts = two_parts(small)
+    gots = [
+        swap(jnp.concatenate([flat(pieces[step]), small_parts], axis=0), "dp", size, step * low) for step in range(1, count)
+    ]
+    so_far, pieces = after(so_far, pieces)
     grad_tokens, attn_held, attn_send, grad_norm_one = back(first_rows, own_rows - first_rows, so_far)
 
-    attn_got = start_exchange(attn_send, None, "head", 2, 1)
-    attn_held, got = after(attn_held, got)
-    held, small = finish_exchange(keep, got, small)
+    def take(pieces, gots, small_parts, low, count):
+        keep = pieces[0]
+        rows = keep.size // keep.shape[-1]
+        for got in gots:
+            keep = keep + got[:rows].reshape(keep.shape).astype(f32)
+        ordered = in_order([small_parts] + [got[rows:] for got in gots], (place // low) % count)
+        return keep, sum(from_parts(part) for part in ordered)
+
+    attn_got = swap(flat(attn_send), "head", 2, 1)
+    attn_held, gots = after(attn_held, gots)
+    held, small = take(pieces, gots, small_parts, low, count)
+    rest = bits_of(size)[2:]
     attn_held = by_line(attn_held + attn_got.reshape(attn_held.shape).astype(f32), size)
-    for n, bit in enumerate(bits):
-        attn_keep, attn_send = halves(attn_held, bit)
-        more = n + 1 < len(bits)
-        if more:
-            keep, send = halves(held, bits[n + 1])
-            attn_send, send = after(attn_send, send)
-        attn_got = start_exchange(attn_send, None, "dp", size, bit)
-        if more:
-            got = start_exchange(send, small, "dp", size, bits[n + 1])
-        attn_held = attn_keep + attn_got.reshape(attn_keep.shape).astype(f32)
-        if more:
-            held, small = finish_exchange(keep, got, small)
-    grad_attn = attn_held.reshape(attn_w.shape)
+    waiting = list(groups)
+    while waiting or rest:
+        attn_pieces, pieces, extra = [None], None, None
+        if waiting:
+            low, count = waiting.pop(0)
+            attn_pieces = pieces_of(attn_held, low, count)
+        sent = {step * low: [flat(attn_pieces[step])] for step in range(1, len(attn_pieces))}
+        bit = None
+        if rest:
+            bit = rest.pop(0)
+            pieces = pieces_of(held, bit, 2)
+            small_parts = two_parts(small)
+            extra = jnp.concatenate([flat(pieces[1]), small_parts], axis=0).reshape(-1, attn_held.shape[-1])
+            sent.setdefault(bit, []).append(extra)
+        gots = {step: swap(jnp.concatenate(parts, axis=0), "dp", size, step) for step, parts in sent.items()}
+        if bit:
+            got = gots[bit][gots[bit].shape[0] - extra.shape[0] :].reshape(-1, columns)
+            held, small = take(pieces, [got], small_parts, bit, 2)
+        if attn_pieces[0] is not None:
+            attn_held = attn_pieces[0]
+            rows = attn_held.size // attn_held.shape[-1]
+            for step in range(1, len(attn_pieces)):
+                attn_held = attn_held + gots[step * low][:rows].reshape(attn_held.shape).astype(f32)
+    grad_attn = unfold_pairs(attn_held.reshape(attn_held.shape[:1] + attn_held.shape[2:]))
     grad_mlp = held.reshape(mlp_w.shape)
-    grad_conv = small[:9]
     norm_two = small[9, : 2 * width].reshape(2, width)
 
-    new_attn_m, new_attn_v, attn_direction = adam_terms(grad_attn, attn_m, attn_v)
-    new_mlp_m, new_mlp_v, mlp_direction = adam_terms(grad_mlp, mlp_m, mlp_v)
-    new_conv_m, new_conv_v, conv_direction = adam_terms(grad_conv, conv_m, conv_v)
-    attn_update = attn_direction + DECAY * attn_w
-    mlp_update = mlp_direction + DECAY * mlp_w
-    conv_update = conv_direction + DECAY * conv_w
-    first_line = (lax.axis_index("dp") == 0).astype(f32)
-    weight_squares = jnp.concatenate(
-        [
-            jnp.sum(attn_w * attn_w, axis=(1, 2)),
-            jnp.sum(mlp_w * mlp_w, axis=(1, 2)),
-            (first_line * jnp.sum(conv_w * conv_w))[None],
-        ]
-    )
-    update_squares = jnp.concatenate(
-        [
-            jnp.sum(attn_update * attn_update, axis=(1, 2)),
-            jnp.sum(mlp_update * mlp_update, axis=(1, 2)),
-            (first_line * jnp.sum(conv_update * conv_update))[None],
-        ]
-    )
-    squares = jnp.pad(jnp.stack([weight_squares, update_squares]), ((0, 0), (0, width - 7)))
-    norm_one = jnp.sum(grad_norm_one.reshape(2, 8, width), axis=1)
-    summed = sum_everywhere(jnp.concatenate([squares, norm_one, jnp.zeros((4, width), f32)]), size)
-    squares, norm_grads = summed[:2, :7], jnp.concatenate([summed[2:4], norm_two])
-    ratio = jnp.sqrt(squares[0]) / jnp.sqrt(squares[1])
-    new_attn_w = attn_w - RATE * ratio[:4, None, None] * attn_update
-    new_mlp_w = mlp_w - RATE * ratio[4:6, None, None] * mlp_update
-    new_conv_w = conv_w - RATE * ratio[6] * conv_update
-    new_norm_m, new_norm_v, norm_direction = adam_terms(norm_grads, norm_m, norm_v)
-    new_norm_w = norm_w - RATE * norm_direction
+    weights, firsts, seconds = [attn_w, mlp_w, conv_w], [attn_m, mlp_m, conv_m], [attn_v, mlp_v, conv_v]
+    scalars = pl.BlockSpec(memory_space=pltpu.SMEM)
+    vectors = pl.BlockSpec(memory_space=pltpu.VMEM)
+    results = pl.pallas_call(
+        moments_kernel,
+        in_specs=[scalars] + [vectors] * 13,
+        out_specs=[vectors] * 10,
+        out_shape=like(weights) * 3 + [jax.ShapeDtypeStruct((8, width), f32)],
+        compiler_params=pltpu.CompilerParams(vmem_limit_bytes=VMEM_BYTES),
+    )(place.astype(jnp.int32).reshape(1), grad_norm_one, grad_attn, grad_mlp, small[:9], *weights, *firsts, *seconds)
+    new_firsts, new_seconds, updates, sums = results[:3], results[3:6], results[6:9], results[9]
+    new_w = pl.pallas_call(
+        apply_kernel,
+        in_specs=[vectors] * 11,
+        out_specs=[vectors] * 6,
+        out_shape=like(weights) + like([norm_w] * 3),
+        compiler_params=pltpu.CompilerParams(vmem_limit_bytes=VMEM_BYTES),
+    )(sum_everywhere(sums, size), norm_two, norm_w, norm_m, norm_v, *weights, *updates)
     return (
-        output, grad_tokens, new_attn_w, new_attn_m, new_attn_v, new_mlp_w, new_mlp_m, new_mlp_v,
-        new_conv_w, new_conv_m, new_conv_v, new_norm_w, new_norm_m, new_norm_v,
+        output, grad_tokens, new_w[0], new_firsts[0], new_seconds[0], new_w[1], new_firsts[1], new_seconds[1],
+        new_w[2], new_firsts[2], new_seconds[2], *new_w[3:],
     )
 
 

time: 326 us -> 383 us (1.17)
  blocking collectives: 0 us -> 84.2 us
  waiting for transfers between devices: 52.7 us -> 33.4 us
  between operations: 16.9 us -> 1.51 us
  starting transfers between devices: 24.4 us -> 31.5 us
  Pallas kernels: 196 us -> 200 us
    all_gather x0 -> x2, blocking collectives: none -> 84.2 us  [body(): lax.all_gather(mlp_w[k].astype(bf16), 'dp', axis=0, tiled=True)]
    ppermute x24 -> x26, waiting for transfers between devices: 48.8 us -> 33.4 us  [swap(): return lax.ppermute(values, axis, [(i, i ^ bit) for i in range(size)])]
    ppermute x24 -> x26, starting transfers between devices: 24.4 us -> 31.5 us  [swap(): return lax.ppermute(values, axis, [(i, i ^ bit) for i in range(size)])]
    pallas_call x0 -> x2, Pallas kernels: none -> 4.38 us  [the longest x1 2.38 us: body(): pl.pallas_call(moments_kernel, in_specs=[scalars] + [vectors] * 13, out_s...]
    all_gather x1 -> x0, waiting for transfers between devices: 3.86 us -> none  [body(): mlp_lines = lax.all_gather(mlp_w.astype(bf16), 'dp', axis=1, tiled=True)]
  transfers between devices with their start and end apart: 25 -> 26, of which waited for: 18 -> 14; matrix products, arithmetic and copies ran while one was open for 5% -> 2% of each run, Pallas kernels for 29% -> 16%
where the time goes in v4:
time: 383 us; the launch traced here: 378 us
  Pallas kernels  200 us (52%)
  blocking collectives  84.2 us (22%)
  waiting for transfers between devices  33.4 us (9%)
  starting transfers between devices  31.5 us (8%)
  other arithmetic  18.1 us (5%)
  local copies, waits for them, and re-layouts  9.5 us (2%)
    pallas_call x1, Pallas kernels, mlp_layer(): pl.pallas_call(mlp_kernel, grid_spec=pltpu.PrefetchScalarGridSpec(num_sca...  101 us
    all_gather x2, blocking collectives, body(): lax.all_gather(mlp_w[k].astype(bf16), 'dp', axis=0, tiled=True)  84.2 us
    pallas_call x2, Pallas kernels, attn_backward(): pl.pallas_call(functools.partial(attn_backward_kernel, first, final), gri...  61.3 us
    ppermute x26, waiting for transfers between devices, swap(): return lax.ppermute(values, axis, [(i, i ^ bit) for i in range(size)])  33.4 us
    pallas_call x1, Pallas kernels, attn_forward(): pl.pallas_call(attn_forward_kernel, grid_spec=pltpu.PrefetchScalarGridSpe...  33.1 us
    ppermute x26, starting transfers between devices, swap(): return lax.ppermute(values, axis, [(i, i ^ bit) for i in range(size)])  31.5 us
  transfers between devices with their start and end apart: 26, of which 14 were waited for; matrix products, arithmetic and copies ran while one was open for 2% of the time, Pallas kernels for 16%

profile of v4, /device:TPU:0, one launch (start us, length us, event | category | flops | bytes accessed | tf_op | source)
XLA Modules:
  0.0 377.9 jit_solution(4205737301444704710)
XLA Ops:
  0.7 0.9 convert_element_type.330
  1.7 3.0 collective-permute-start.2
  4.7 2.6 collective-permute-start.1
  7.3 0.8 convert_element_type.333
  9.6 0.9 convert.17
  10.5 45.0 %all-gather.1 = bf16[1,384,768]{2,1,0:T(8,128)(2,1)S(1)} all-gather(bf16[1,24,768]{2,1,0:T(8,128)(2,1)S(1)} %get-tuple-element.155), channel_id=3, replica_groups=mesh['dp'=16,'head'=2] {'dp'}, dimensions={1}, use_global_device_ids=true | all-gather | bytes 626688 | tf_op jit(solution)/shard_map/all_gather | solution.py:857
  55.6 39.1 %all-gather = bf16[1,384,768]{2,1,0:T(8,128)(2,1)S(1)} all-gather(bf16[1,24,768]{2,1,0:T(8,128)(2,1)S(1)} %get-tuple-element.156), channel_id=2, replica_groups=mesh['dp'=16,'head'=2] {'dp'}, dimensions={1}, use_global_device_ids=true | all-gather | bytes 626688 | tf_op jit(solution)/shard_map/all_gather | solution.py:857
  95.8 2.4 collective-permute-start.5
  98.2 1.5 collective-permute-start.3
  101.3 3.6 collective-permute-done.4
  105.9 1.4 collective-permute-done.6
  108.0 1.2 copy.68
  109.2 33.1 %shard_map.263 = (f32[3072,384]{1,0:T(8,128)}, bf16[3072,1152]{1,0:T(8,128)(2,1)}, bf16[3072,384]{1,0:T(8,128)(2,1)}, bf16[96,1024]{1,0:T(8,128)(2,1)}) custom-call(s32[3,8]{1,0:T(4,128)} %get-tuple-element.165.start_ref, s32[3,8]{1,0:T(4,128)} %get-tuple-element.164.class_ref, s32[3]{0:T(128)} %dynamic_slice.54.count_ref, bf16[3072,384]{1,0:T(8,128)(2,1)} %tokens_ref.5, ...), custom_call_target="tpu_custom_call" | custom-call | tf_op jit(solution)/shard_map/pallas_call | solution.py:185
  142.5 1.0 pad_maximum_fusion.3.taps_ref
  143.5 1.7 collective-permute-done.7
  145.4 1.6 pad_maximum_fusion.w_ref
  147.0 100.9 %shard_map.264 = (bf16[3072,384]{1,0:T(8,128)(2,1)}, f32[3072,384]{1,0:T(8,128)}, f32[2,384,768]{2,1,0:T(8,128)}, bf16[2,384,768]{2,1,0:T(8,128)(2,1)}, f32[16,1536]{1,0:T(8,128)}, /*index=5*/f32[16,384]{1,0:T(8,128)}) custom-call(s32[3,64]{1,0:T(4,128)} %multiply_add_fusion.place_ref, s32[1]{0:T(128)} %bitcast.rank_ref, ...), custom_call_target="tpu_custom_call" | custom-call | tf_op jit(solution)/shard_map/pallas_call | solution.py:596
  248.7 0.8 constant_dynamic-slice_fusion.2
  249.6 1.4 pad_maximum_fusion.1
  251.1 21.7 %shard_map.265 = (f32[3072,384]{1,0:T(8,128)}, f32[4,384,384]{2,1,0:T(8,128)}, f32[16,384]{1,0:T(8,128)}) custom-call(s32[3,8]{1,0:T(4,128)} %get-tuple-element.165.start_ref, s32[3,8]{1,0:T(4,128)} %get-tuple-element.164.class_ref, s32[3]{0:T(128)} %dynamic_slice.54.count_ref, s32[1]{0:T(128)} %bitcast.rank_ref, bf16[3072,384]{1,0:T(8,128)(2,1)} %tokens_ref.5, ...), custom_call_target="tpu_custom_call" | custom-call | tf_op jit(solution)/shard_map/pallas_call | solution.py:389
  272.9 1.5 copy-done.2
  274.9 1.0 pad_maximum_fusion.5
  275.8 2.9 collective-permute-start.12
  279.4 39.6 %shard_map.266 = (f32[3072,384]{1,0:T(8,128)}, f32[2,384,384]{2,1,0:T(8,128)}, bf16[2,384,384]{2,1,0:T(8,128)(2,1)}, f32[16,384]{1,0:T(8,128)}) custom-call(s32[3,8]{1,0:T(4,128)} %get-tuple-element.165.start_ref, s32[3,8]{1,0:T(4,128)} %get-tuple-element.164.class_ref, s32[3]{0:T(128)} %dynamic_slice.54.count_ref, ...), custom_call_target="tpu_custom_call", output_to_operand_aliasing={{0}: (12, {})} | custom-call | tf_op jit(solution)/shard_map/pallas_call | solution.py:389
  319.1 0.8 select_select_fusion.1
  319.9 0.8 select_select_fusion.3
  320.7 1.0 slice.170
  321.7 1.0 slice.169
  323.2 2.8 collective-permute-start.13
  326.0 2.6 collective-permute-done.18
  329.1 4.5 %collective-permute-start.16 = (bf16[192,384]{1,0:T(8,128)(2,1)S(1)}, bf16[192,384]{1,0:T(8,128)(2,1)S(1)}, u32[]{:S(2)}, u32[]{:S(2)}) collective-permute-start(bf16[192,384]{1,0:T(8,128)(2,1)S(1)} %bitcast.155), channel_id=1, source_target_pairs={{0,6},{2,4},{4,2},{6,0},{8,14},{10,12},{12,10},{14,8},{16,22},{18,... | collective-permute-start | bytes 442376 | tf_op jit(solution)/shard_map/ppermute | solution.py:693
  333.6 1.3 collective-permute-start.15
  334.9 1.8 collective-permute-done.16
  336.7 3.7 collective-permute-done.14
  340.4 1.1 collective-permute-done.15
  341.6 3.0 collective-permute-start.19
  344.6 1.0 collective-permute-start.20
  346.0 6.5 %collective-permute-done.19 = bf16[184,384]{1,0:T(8,128)(2,1)S(1)} collective-permute-done((bf16[184,384]{1,0:T(8,128)(2,1)S(1)}, bf16[184,384]{1,0:T(8,128)(2,1)S(1)}, u32[]{:S(2)}, u32[]{:S(2)}) %collective-permute-start.19) | collective-permute-done | bytes 141344 | tf_op jit(solution)/shard_map/ppermute | solution.py:693
  354.8 2.4 shard_map.267
  357.2 1.4 collective-permute-done.21
  359.3 2.2 collective-permute-start.22
  361.5 1.7 collective-permute-done.22
  363.1 1.4 collective-permute-start.23
  364.6 2.3 collective-permute-done.23
  366.8 0.8 collective-permute-start.24
  367.7 2.9 collective-permute-done.24
  372.5 2.6 collective-permute-done.25
  375.7 2.0 shard_map.268
  (126 shorter events, 15.3 us)
Async XLA Ops:
  0.6 7.4 %copy-start = (s32[6,1024]{1,0:T(8,128)S(1)}, s32[6,1024]{1,0:T(8,128)}, u32[]{:S(2)}) copy-start(s32[6,1024]{1,0:T(8,128)} %param.18) | copy-start | bytes 73732
  1.7 94.0 %collective-permute-start.2 = (bf16[1,2,24,384]{3,2,1,0:T(8,128)(2,1)S(1)}, bf16[1,2,24,384]{3,2,1,0:T(8,128)(2,1)S(1)}, u32[]{:S(2)}, u32[]{:S(2)}) collective-permute-start(bf16[1,2,24,384]{3,2,1,0:T(8,128)(2,1)S(1)} %maximum_bitcast_fusion.2), channel_id=1, source_target_pairs={{0,8},{2,10},{4,12},{6,14},{8,0},{10,2},{12,4},{14,6},{16,24},{18,... | collective-permute-start | bytes 110600 | tf_op jit(solution)/shard_map/ppermute | solution.py:693
  4.7 90.9 %collective-permute-start.1 = (bf16[1,2,24,384]{3,2,1,0:T(8,128)(2,1)S(1)}, bf16[1,2,24,384]{3,2,1,0:T(8,128)(2,1)S(1)}, u32[]{:S(2)}, u32[]{:S(2)}) collective-permute-start(bf16[1,2,24,384]{3,2,1,0:T(8,128)(2,1)S(1)} %maximum_bitcast_fusion.2), channel_id=1, source_target_pairs={{0,16},{2,18},{4,20},{6,22},{8,24},{10,26},{12,28},{14,30},{16,0},... | collective-permute-start | bytes 110600 | tf_op jit(solution)/shard_map/ppermute | solution.py:693
  7.3 88.4 %collective-permute-start = (bf16[1,2,24,384]{3,2,1,0:T(8,128)(2,1)S(1)}, bf16[1,2,24,384]{3,2,1,0:T(8,128)(2,1)S(1)}, u32[]{:S(2)}, u32[]{:S(2)}) collective-permute-start(bf16[1,2,24,384]{3,2,1,0:T(8,128)(2,1)S(1)} %maximum_bitcast_fusion.2), channel_id=1, source_target_pairs={{0,24},{2,26},{4,28},{6,30},{8,16},{10,18},{12,20},{14,22},{16,8},... | collective-permute-start | bytes 110600 | tf_op jit(solution)/shard_map/ppermute | solution.py:693
  8.1 97.2 %collective-permute-start.8 = (bf16[9,768]{1,0:T(8,128)(2,1)S(1)}, bf16[9,768]{1,0:T(8,128)(2,1)S(1)}, u32[]{:S(2)}, u32[]{:S(2)}) collective-permute-start(bf16[9,768]{1,0:T(8,128)(2,1)S(1)} %convert_element_type.333), channel_id=1, source_target_pairs={{0,1},{1,0},{2,3},{3,2},{4,5},{5,4},{6,7},{7,6},{8,9},{9,8},{10,11... | collective-permute-start | bytes 41480 | tf_op jit(solution)/shard_map/ppermute | solution.py:693
  9.6 90.2 %copy-start.5 = (s32[6]{0:T(128)S(1)}, s32[6]{0:T(128)}, u32[]{:S(2)}) copy-start(s32[6]{0:T(128)} %param.19) | copy-start | bytes 76
  95.8 5.5 %collective-permute-start.5 = (bf16[4,2,24,384]{3,2,1,0:T(8,128)(2,1)S(1)}, bf16[4,2,24,384]{3,2,1,0:T(8,128)(2,1)S(1)}, u32[]{:S(2)}, u32[]{:S(2)}) collective-permute-start(bf16[4,2,24,384]{3,2,1,0:T(8,128)(2,1)S(1)} %maximum_bitcast_fusion.1), channel_id=1, source_target_pairs={{0,2},{2,0},{4,6},{6,4},{8,10},{10,8},{12,14},{14,12},{16,18},{18,... | collective-permute-start | bytes 442376 | tf_op jit(solution)/shard_map/ppermute | solution.py:693
  98.2 6.7 %collective-permute-start.4 = (bf16[4,2,24,384]{3,2,1,0:T(8,128)(2,1)S(1)}, bf16[4,2,24,384]{3,2,1,0:T(8,128)(2,1)S(1)}, u32[]{:S(2)}, u32[]{:S(2)}) collective-permute-start(bf16[4,2,24,384]{3,2,1,0:T(8,128)(2,1)S(1)} %maximum_bitcast_fusion.1), channel_id=1, source_target_pairs={{0,4},{2,6},{4,0},{6,2},{8,12},{10,14},{12,8},{14,10},{16,20},{18,... | collective-permute-start | bytes 442376 | tf_op jit(solution)/shard_map/ppermute | solution.py:693
  98.2 6.7 %collective-permute-start.3 = (bf16[4,2,24,384]{3,2,1,0:T(8,128)(2,1)S(1)}, bf16[4,2,24,384]{3,2,1,0:T(8,128)(2,1)S(1)}, u32[]{:S(2)}, u32[]{:S(2)}) collective-permute-start(bf16[4,2,24,384]{3,2,1,0:T(8,128)(2,1)S(1)} %maximum_bitcast_fusion.1), channel_id=1, source_target_pairs={{0,6},{2,4},{4,2},{6,0},{8,14},{10,12},{12,10},{14,8},{16,22},{18,... | collective-permute-start | bytes 442376 | tf_op jit(solution)/shard_map/ppermute | solution.py:693
  105.0 0.8 copy-start.4
  105.2 2.1 collective-permute-start.6
  142.4 2.9 collective-permute-start.7
  251.0 21.9 %collective-permute-start.9 = (bf16[788,768]{1,0:T(8,128)(2,1)S(1)}, bf16[788,768]{1,0:T(8,128)(2,1)S(1)}, u32[]{:S(2)}, u32[]{:S(2)}) collective-permute-start(bf16[788,768]{1,0:T(8,128)(2,1)S(1)} %pad_maximum_fusion.1), channel_id=1, source_target_pairs={{0,1},{1,0},{2,3},{3,2},{4,5},{5,4},{6,7},{7,6},{8,9},{9,8},{10,11... | collective-permute-start | bytes 3631112 | tf_op jit(solution)/shard_map/ppermute | solution.py:693
  272.8 1.7 copy-start.2
  275.8 43.2 %collective-permute-start.12 = (bf16[212,768]{1,0:T(8,128)(2,1)}, bf16[212,768]{1,0:T(8,128)(2,1)S(1)}, u32[]{:S(2)}, u32[]{:S(2)}) collective-permute-start(bf16[212,768]{1,0:T(8,128)(2,1)} %get-tuple-element.157), channel_id=1, source_target_pairs={{0,6},{2,4},{4,2},{6,0},{8,14},{10,12},{12,10},{14,8},{16,22},{18,... | collective-permute-start | bytes 976904 | tf_op jit(solution)/shard_map/ppermute | solution.py:693
  278.7 40.3 %collective-permute-start.11 = (bf16[212,768]{1,0:T(8,128)(2,1)}, bf16[212,768]{1,0:T(8,128)(2,1)}, u32[]{:S(2)}, u32[]{:S(2)}) collective-permute-start(bf16[212,768]{1,0:T(8,128)(2,1)} %get-tuple-element.158), channel_id=1, source_target_pairs={{0,4},{2,6},{4,0},{6,2},{8,12},{10,14},{12,8},{14,10},{16,20},{18,... | collective-permute-start | bytes 976904 | tf_op jit(solution)/shard_map/ppermute | solution.py:693
  278.7 40.4 %collective-permute-start.10 = (bf16[212,768]{1,0:T(8,128)(2,1)}, bf16[212,768]{1,0:T(8,128)(2,1)}, u32[]{:S(2)}, u32[]{:S(2)}) collective-permute-start(bf16[212,768]{1,0:T(8,128)(2,1)} %get-tuple-element.159), channel_id=1, source_target_pairs={{0,2},{2,0},{4,6},{6,4},{8,10},{10,8},{12,14},{14,12},{16,18},{18,... | collective-permute-start | bytes 976904 | tf_op jit(solution)/shard_map/ppermute | solution.py:693
  323.0 5.6 %collective-permute-start.18 = (bf16[232,384]{1,0:T(8,128)(2,1)S(1)}, bf16[232,384]{1,0:T(8,128)(2,1)S(1)}, u32[]{:S(2)}, u32[]{:S(2)}) collective-permute-start(bf16[232,384]{1,0:T(8,128)(2,1)S(1)} %reshape.257), channel_id=1, source_target_pairs={{0,8},{2,10},{4,12},{6,14},{8,0},{10,2},{12,4},{14,6},{16,24},{18,... | collective-permute-start | bytes 534536 | tf_op jit(solution)/shard_map/ppermute | solution.py:693
  323.1 5.8 %copy-start.3 = (f32[2,384,384]{2,1,0:T(8,128)S(1)}, f32[2,384,384]{2,1,0:T(8,128)}, u32[]{:S(2)}) copy-start(f32[2,384,384]{2,1,0:T(8,128)} %get-tuple-element.88) | copy-start | bytes 3538948
  323.2 5.7 %collective-permute-start.13 = (bf16[768,384]{1,0:T(8,128)(2,1)}, bf16[768,384]{1,0:T(8,128)(2,1)S(1)}, u32[]{:S(2)}, u32[]{:S(2)}) collective-permute-start(bf16[768,384]{1,0:T(8,128)(2,1)} %bitcast.166), channel_id=1, source_target_pairs={{0,1},{1,0},{2,3},{3,2},{4,5},{5,4},{6,7},{7,6},{8,9},{9,8},{10,11... | collective-permute-start | bytes 1769480 | tf_op jit(solution)/shard_map/ppermute | solution.py:693
  329.1 7.6 %collective-permute-start.16 = (bf16[192,384]{1,0:T(8,128)(2,1)S(1)}, bf16[192,384]{1,0:T(8,128)(2,1)S(1)}, u32[]{:S(2)}, u32[]{:S(2)}) collective-permute-start(bf16[192,384]{1,0:T(8,128)(2,1)S(1)} %bitcast.155), channel_id=1, source_target_pairs={{0,6},{2,4},{4,2},{6,0},{8,14},{10,12},{12,10},{14,8},{16,22},{18,... | collective-permute-start | bytes 442376 | tf_op jit(solution)/shard_map/ppermute | solution.py:693
  333.6 6.8 %collective-permute-start.14 = (bf16[192,384]{1,0:T(8,128)(2,1)S(1)}, bf16[192,384]{1,0:T(8,128)(2,1)S(1)}, u32[]{:S(2)}, u32[]{:S(2)}) collective-permute-start(bf16[192,384]{1,0:T(8,128)(2,1)S(1)} %bitcast.154), channel_id=1, source_target_pairs={{0,2},{2,0},{4,6},{6,4},{8,10},{10,8},{12,14},{14,12},{16,18},{18,... | collective-permute-start | bytes 442376 | tf_op jit(solution)/shard_map/ppermute | solution.py:693
  333.6 7.9 %collective-permute-start.15 = (bf16[192,384]{1,0:T(8,128)(2,1)S(1)}, bf16[192,384]{1,0:T(8,128)(2,1)S(1)}, u32[]{:S(2)}, u32[]{:S(2)}) collective-permute-start(bf16[192,384]{1,0:T(8,128)(2,1)S(1)} %bitcast.153), channel_id=1, source_target_pairs={{0,4},{2,6},{4,0},{6,2},{8,12},{10,14},{12,8},{14,10},{16,20},{18,... | collective-permute-start | bytes 442376 | tf_op jit(solution)/shard_map/ppermute | solution.py:693
  341.6 10.9 %collective-permute-start.19 = (bf16[184,384]{1,0:T(8,128)(2,1)S(1)}, bf16[184,384]{1,0:T(8,128)(2,1)S(1)}, u32[]{:S(2)}, u32[]{:S(2)}) collective-permute-start(bf16[184,384]{1,0:T(8,128)(2,1)S(1)} %pad_maximum_fusion.12), channel_id=1, source_target_pairs={{0,16},{2,18},{4,20},{6,22},{8,24},{10,26},{12,28},{14,30},{16,0},... | collective-permute-start | bytes 423944 | tf_op jit(solution)/shard_map/ppermute | solution.py:693
  344.6 8.0 %collective-permute-start.20 = (bf16[48,384]{1,0:T(8,128)(2,1)S(1)}, bf16[48,384]{1,0:T(8,128)(2,1)S(1)}, u32[]{:S(2)}, u32[]{:S(2)}) collective-permute-start(bf16[48,384]{1,0:T(8,128)(2,1)S(1)} %bitcast.162), channel_id=1, source_target_pairs={{0,24},{2,26},{4,28},{6,30},{8,16},{10,18},{12,20},{14,22},{16,8},... | collective-permute-start | bytes 110600 | tf_op jit(solution)/shard_map/ppermute | solution.py:693
  345.6 7.1 %collective-permute-start.17 = (bf16[48,384]{1,0:T(8,128)(2,1)S(1)}, bf16[48,384]{1,0:T(8,128)(2,1)S(1)}, u32[]{:S(2)}, u32[]{:S(2)}) collective-permute-start(bf16[48,384]{1,0:T(8,128)(2,1)S(1)} %bitcast.161), channel_id=1, source_target_pairs={{0,8},{2,10},{4,12},{6,14},{8,0},{10,2},{12,4},{14,6},{16,24},{18,... | collective-permute-start | bytes 110600 | tf_op jit(solution)/shard_map/ppermute | solution.py:693
  353.4 24.3 %copy-start.1 = (s32[6,1024]{1,0:T(8,128)S(1)}, s32[6,1024]{1,0:T(8,128)}, u32[]{:S(2)}) copy-start(s32[6,1024]{1,0:T(8,128)} %param.18) | copy-start | bytes 73732
  357.1 1.4 collective-permute-start.21
  359.3 3.8 %collective-permute-start.22 = (f32[8,384]{1,0:T(8,128)S(1)}, f32[8,384]{1,0:T(8,128)S(1)}, u32[]{:S(2)}, u32[]{:S(2)}) collective-permute-start(f32[8,384]{1,0:T(8,128)S(1)} %add.290), channel_id=1, source_target_pairs={{0,2},{2,0},{4,6},{6,4},{8,10},{10,8},{12,14},{14,12},{16,18},{18,... | collective-permute-start | bytes 36872 | tf_op jit(solution)/shard_map/ppermute | solution.py:693
  363.1 3.7 collective-permute-start.23
  366.8 3.7 collective-permute-start.24
  370.5 4.6 %collective-permute-start.25 = (f32[8,384]{1,0:T(8,128)S(1)}, f32[8,384]{1,0:T(8,128)S(1)}, u32[]{:S(2)}, u32[]{:S(2)}) collective-permute-start(f32[8,384]{1,0:T(8,128)S(1)} %add.293), channel_id=1, source_target_pairs={{0,16},{2,18},{4,20},{6,22},{8,24},{10,26},{12,28},{14,30},{16,0},... | collective-permute-start | bytes 36872 | tf_op jit(solution)/shard_map/ppermute | solution.py:693
